TPU v7x, 256 devices: a whole 4x4x8 slice. The times are simulated.
256 devices in a mesh: dp: 64 (over z_hi, y, x, core), mp: 4 (over z_lo).
Axes of the slice: x: 4, y: 4, z: 8 (z_hi: 2, z_lo: 4; z = z_hi * 4 + z_lo), core: 2. Of those that a mesh axis runs over, the one named last changes fastest.
Arguments:
- acts: bfloat16 [32768, 4096], P('dp'), may hold values from -12 to 12
- out_grads: bfloat16 [32768, 5120], P('dp', 'mp'), may hold values from -12 to 12
- owners: int32 [4, 9], P('mp'), may hold values from 0 to 63, as said below
Outputs:
- update: bfloat16 [4096, 5120], P('dp', 'mp')
- kept_roots: bfloat16 [128, 1024, 256], P('dp', 'mp')
Inputs may be any that keep to these rules, and one draw needn't show every extreme that they name: `owners`: in each row, every index of dp owns at most 2 entries, and some index owns exactly 2.
All inputs are finite; a program needn't handle non-finite values.
Results may differ from a plain program's by a relative error of at most 0.0074.
The roundings to bfloat16 on the way count: a program that leaves them out, or rounds other values in their place, can miss the bound.
Values may be sent and summed in bfloat16 or wider, within the bound.
No kernel may reach another device: no remote copies, remote signals or barrier semaphores. Data moves between devices by JAX's collectives and lax.ppermute only.
A program may use at most 128 MiB of HBM per device.

v0:
```python
import math

import jax
import jax.numpy as jnp
from jax import lax
from jax.sharding import PartitionSpec as P

BS = 256
ITERS = 12
MOST = 2


damping = 0.1


def broadcast(value, axis, source):
    kept = jnp.where(lax.axis_index(axis) == source, value, 0).astype(value.dtype)
    return lax.psum(kept, axis)


def inverse_root(blocks):
    identity = jnp.eye(blocks.shape[-1], dtype=jnp.float32)
    norms = jnp.sqrt(jnp.sum(blocks * blocks, axis=(1, 2)))[:, None, None]
    approx = blocks / norms
    estimate = jnp.broadcast_to(identity, blocks.shape)

    def advance(index, carry):
        current, guess = carry
        factor = 1.5 * identity - 0.5 * jnp.matmul(guess, current, precision=lax.Precision.HIGHEST)
        return (
            jnp.matmul(current, factor, precision=lax.Precision.HIGHEST),
            jnp.matmul(factor, guess, precision=lax.Precision.HIGHEST),
        )

    approx, estimate = lax.fori_loop(0, ITERS, advance, (approx, estimate))
    return (estimate / jnp.sqrt(norms)).astype(jnp.bfloat16)


def per_device(acts, out_grads, owners):
    tok_rows = acts.shape[0]
    model_width = acts.shape[1]
    data_count = lax.axis_size("dp")
    model_count = lax.axis_size("mp")
    column = lax.axis_index("mp")
    data_rank = lax.axis_index("dp")
    input_count = model_width // (BS * model_count)
    output_count = out_grads.shape[1] // BS
    block_count = input_count + output_count
    identity = jnp.eye(BS, dtype=jnp.float32)
    input_cols = lax.dynamic_slice_in_dim(acts, column * input_count * BS, input_count * BS, 1)
    input_cols = input_cols.reshape(tok_rows, input_count, BS)
    input_part = jnp.einsum(
        "tki,tkj->kij", input_cols, input_cols, preferred_element_type=jnp.float32
    )
    grad_blocks = out_grads.reshape(tok_rows, output_count, BS)
    grad_part = jnp.einsum(
        "tki,tkj->kij", grad_blocks, grad_blocks, preferred_element_type=jnp.float32
    )
    partial_sums = jnp.concatenate([input_part, grad_part], axis=0)
    summed = lax.psum(partial_sums, "dp")
    total_tokens = tok_rows * data_count
    factors = summed / total_tokens + damping * identity
    owner_row = owners[0]
    mine = (owner_row == data_rank).astype(jnp.int32)
    order = jnp.cumsum(mine) - 1
    slot_ids = jnp.arange(MOST, dtype=jnp.int32)
    select = (mine[None, :] * (order[None, :] == slot_ids[:, None]).astype(jnp.int32)).astype(
        jnp.float32
    )
    filled = jnp.sum(select, axis=1)[:, None, None]
    chosen = jnp.einsum("sk,kij->sij", select, factors, precision=lax.Precision.HIGHEST)
    chosen = chosen + (1.0 - filled) * identity
    slot_roots = inverse_root(chosen)
    kept_roots = (slot_roots.astype(jnp.float32) * filled).astype(jnp.bfloat16)
    gathered = []
    for block in range(block_count):
        offered = jnp.einsum(
            "s,sij->ij",
            select[:, block],
            kept_roots.astype(jnp.float32),
            precision=lax.Precision.HIGHEST,
        )
        gathered.append(broadcast(offered.astype(jnp.bfloat16), "dp", owner_row[block]))
    roots = jnp.stack(gathered, axis=0)
    input_roots = lax.all_gather(roots[:input_count], "mp", axis=0, tiled=True)
    output_roots = roots[input_count:]
    whitened = (
        jnp.einsum(
            "tbi,bij->tbj",
            acts.reshape(tok_rows, model_width // BS, BS),
            input_roots,
            preferred_element_type=jnp.float32,
        )
        .astype(jnp.bfloat16)
        .reshape(tok_rows, model_width)
    )
    scaled = (
        jnp.einsum("tbi,bij->tbj", grad_blocks, output_roots, preferred_element_type=jnp.float32)
        .astype(jnp.bfloat16)
        .reshape(tok_rows, output_count * BS)
    )
    factor_scale = 1.0 / math.sqrt(total_tokens)
    product = lax.dot_general(
        whitened, scaled, (((0,), (0,)), ((), ())), preferred_element_type=jnp.float32
    )
    update = lax.psum_scatter(product * factor_scale, "dp", scatter_dimension=0, tiled=True)
    return (update.astype(jnp.bfloat16), kept_roots)


def solution(mesh):
    return jax.shard_map(
        per_device,
        mesh=mesh,
        in_specs=(P("dp", None), P("dp", "mp"), P("mp", None)),
        out_specs=(P("dp", "mp"), P("dp", "mp", None)),
        check_vma=False,
    )
```

profile of v0, /device:TPU:32, one launch (start us, length us, event | category | flops | bytes accessed | tf_op | source)
XLA Modules:
  0.0 2142.2 jit_solution(11472341042709036395)
XLA Ops:
  7.2 1.3 constant_dynamic-slice_fusion
  9.5 1.6 copy.41
  11.7 1.6 pad_maximum_fusion
  20.8 778.8 %all-reduce.4.cloned.1.call-done = f32[9,256,256]{2,1,0:T(8,128)} async-done(((f32[9,256,256]{2,1,0:T(8,128)}), f32[9,256,256]{2,1,0:T(8,128)}) %all-reduce.4.cloned.1.call-update) | async-done | bytes 2359312 | tf_op jit(solution)/shard_map/psum | solution.py:60
  799.6 1.9 multiply_add_fusion
  801.5 3.9 multiply_reduce_fusion
  806.0 30.4 %while.13 = (s32[]{:T(128)}, f32[2,256,256]{1,2,0:T(8,128)S(1)}, f32[2,256,256]{2,1,0:T(8,128)S(1)}, s32[]{:T(128)}) while((s32[]{:T(128)}, f32[2,256,256]{1,2,0:T(8,128)S(1)}, f32[2,256,256]{2,1,0:T(8,128)S(1)}, s32[]{:T(128)}) %tuple.44), condition=%wide.region_5.6_spmd.clone, body=%wide.region_4.5_spmd.clone.sunk | while | flops 1208352768 | bytes 7340085 | solution.py:35
  807.5 1.0 convolution_bitcast_fusion.2
  810.0 1.0 convolution_bitcast_fusion.2
  812.5 1.0 convolution_bitcast_fusion.2
  815.0 1.0 convolution_bitcast_fusion.2
  817.5 1.0 convolution_bitcast_fusion.2
  827.6 1.0 convolution_bitcast_fusion.2
  836.8 1.7 fusion.48
  839.5 1.7 fusion.46
  847.1 1.1 copy.67
  848.4 1.1 copy.65
  854.0 766.0 %all-reduce.6.cloned.1.call-done = (bf16[1,256,256]{1,2,0:T(8,128)(2,1)}, bf16[1,256,256]{1,2,0:T(8,128)(2,1)}, bf16[1,256,256]{1,2,0:T(8,128)(2,1)}, bf16[1,256...) async-done(((bf16[1,256,256]{1,2,0:T(8,128)(2,1)}, ...) | async-done | bytes 1179664 | tf_op jit(solution)/shard_map/psum | solution.py:18
  1620.0 1.2 pad_maximum_fusion.1
  1623.2 46.6 %all-gather.2.cloned.1.call-done = bf16[16,256,256]{2,1,0:T(8,128)(2,1)} async-done(((bf16[4,256,256]{2,1,0:T(8,128)(2,1)}), bf16[16,256,256]{2,1,0:T(8,128)(2,1)}) %all-gather.2.cloned.1.call-update) | async-done | bytes 2097168 | tf_op jit(solution)/shard_map/all_gather | solution.py:85
  1669.7 4.2 fusion.9
  1673.9 10.0 convolution_multiply_fusion.1
  1683.9 450.1 %reduce-scatter.2.cloned.1.call-done = f32[64,1280]{1,0:T(8,128)} async-done(((f32[4096,1280]{1,0:T(8,128)}), f32[64,1280]{1,0:T(8,128)}) %reduce-scatter.2.cloned.1.call-update) | async-done | bytes 327696 | tf_op jit(solution)/shard_map/reduce_scatter | solution.py:106
  2134.1 1.7 convert_element_type.113
  (132 shorter events, 40.8 us)
Async XLA Ops:
  7.2 792.4 %all-reduce.4.cloned.1.call-start = ((), (), s32[]{:S(2)}) async-start(), calls=%async_computation.1 | async-start | bytes 4718592 | tf_op jit(solution)/shard_map/psum | solution.py:60
  13.3 0.7 copy-start.6
  13.4 1606.6 %all-reduce.6.cloned.1.call-start = ((), (), s32[]{:S(2)}) async-start(), calls=%async_computation.4 | async-start | bytes 2359296 | tf_op jit(solution)/shard_map/psum | solution.py:18
  836.5 6.6 copy-start
  853.9 815.8 %all-gather.2.cloned.1.call-start = ((), (), s32[]{:S(2)}) async-start(), calls=%async_computation.2 | async-start | bytes 2621440 | tf_op jit(solution)/shard_map/all_gather | solution.py:85
  1620.0 2.6 copy-start.5
  1620.0 2.6 copy-start.4
  1620.0 2.6 copy-start.3
  1620.0 2.6 copy-start.2
  1620.0 2.7 copy-start.1
  1622.2 511.8 %reduce-scatter.2.cloned.1.call-start = ((), (), s32[]{:S(2)}) async-start(), calls=%async_computation.3 | async-start | bytes 21299200 | tf_op jit(solution)/shard_map/reduce_scatter | solution.py:106
Sparse Core Ops, SparseCore 0:
  13.5 786.0 all-reduce.3
  854.0 765.8 all-reduce.5
  1622.4 47.3 all-gather.1
  1684.0 449.9 reduce-scatter.1
where the time goes:
time: 2140 us
  waiting for transfers between devices  2040 us (95%)
  matrix products  58.2 us (3%)
    psum x1, waiting for transfers between devices, per_device(): summed = lax.psum(partial_sums, 'dp')  779 us
    psum x1, waiting for transfers between devices, broadcast(): return lax.psum(kept, axis)  766 us
    reduce_scatter x1, waiting for transfers between devices, per_device(): lax.psum_scatter(product * factor_scale, 'dp', scatter_dimension=0, tiled...  450 us
    all_gather x1, waiting for transfers between devices, per_device(): input_roots = lax.all_gather(roots[:input_count], 'mp', axis=0, tiled=True)  46.6 us
  transfers between devices with their start and end apart: 4, of which 4 were waited for; matrix products, arithmetic and copies ran while one was open for 0% of the time, Pallas kernels for 0%

commit v1 on v0

v1 whole, which is shorter than its diff:
```python
import functools
import math

import jax
import jax.numpy as jnp
from jax import lax
from jax.experimental import pallas as pl
from jax.experimental.pallas import tpu as pltpu
from jax.sharding import Mesh, PartitionSpec as P

BS = 256
HALF = 128
ITERS = 12
MOST = 2
DAMPING = 0.1
TOKENS = 32768
DP = ("zh", "y", "x", "c")
HIGHEST = lax.Precision.HIGHEST
F32 = jnp.float32
BF16 = jnp.bfloat16


def tdot(lhs, rhs):
    return lax.dot_general(lhs, rhs, (((0,), (0,)), ((), ())), preferred_element_type=F32)


def factor_kernel(where_ref, acts_ref, grads_ref, out_ref):
    step = pl.program_id(0)
    core = where_ref[1]

    def put(slot, block, value):
        for row in range(4):
            out_ref[slot, row, block, 0:64, :] = value[row * 64 : (row + 1) * 64]

    @pl.when(step < 4)
    def _():
        put(core, step, tdot(acts_ref[...], acts_ref[...]))

    @pl.when(jnp.logical_and(step >= 4, step < 8))
    def _():
        put(1 - core, step - 4, tdot(grads_ref[...], grads_ref[...]))

    @pl.when(step == 8)
    def _():
        for half in range(2):
            value = tdot(grads_ref[:, half * HALF : (half + 1) * HALF], grads_ref[...])
            slot = jnp.where(core == half, 0, 1)
            for row in range(4):
                for block in range(4):
                    out_ref[slot, row, block, 64:96, :] = value[row * 32 : (row + 1) * 32]


def factor_parts(where, acts, grads):
    rows = acts.shape[0]
    return pl.pallas_call(
        factor_kernel,
        grid_spec=pltpu.PrefetchScalarGridSpec(
            num_scalar_prefetch=1,
            grid=(9,),
            in_specs=[
                pl.BlockSpec((rows, BS), lambda i, w: (0, w[0] * 4 + jnp.minimum(i, 3))),
                pl.BlockSpec((rows, BS), lambda i, w: (0, jnp.maximum(i - 4, 0))),
            ],
            out_specs=pl.BlockSpec((2, 4, 4, 96, BS), lambda i, w: (0, 0, 0, 0, 0)),
        ),
        out_shape=jax.ShapeDtypeStruct((2, 4, 4, 96, BS), F32),
        compiler_params=pltpu.CompilerParams(vmem_limit_bytes=40 * 2**20),
        cost_estimate=pl.CostEstimate(flops=2 * 9 * rows * BS * BS, bytes_accessed=6 * 2**20, transcendentals=0),
    )(where, acts, grads)


def product_kernel(where_ref, low_ref, high_ref, low_other, high_other, grads_ref, grads_other, out_ref):
    width = grads_ref.shape[1] // 2
    for zh, (mine, other) in enumerate(((low_ref, low_other), (high_ref, high_other))):
        for xl in range(2):
            cols = slice(xl * width, (xl + 1) * width)
            out_ref[0, 0, xl, zh] = tdot(mine[...], grads_ref[:, cols]) + tdot(other[...], grads_other[:, cols])


def product(where, acts, acts_other, grads, grads_other):
    rows, width = grads.shape
    whole = pl.BlockSpec((rows, width), lambda y, h, w: (0, 0))
    return pl.pallas_call(
        product_kernel,
        grid_spec=pltpu.PrefetchScalarGridSpec(
            num_scalar_prefetch=1,
            grid=(4, 2),
            in_specs=[
                pl.BlockSpec((rows, HALF), lambda y, h, w: (0, 2 * (y * 2 + h) + w[1])),
                pl.BlockSpec((rows, HALF), lambda y, h, w: (0, 2 * (8 + y * 2 + h) + w[1])),
                pl.BlockSpec((rows, HALF), lambda y, h, w: (0, y * 2 + h)),
                pl.BlockSpec((rows, HALF), lambda y, h, w: (0, 8 + y * 2 + h)),
                whole,
                whole,
            ],
            out_specs=pl.BlockSpec((1, 1, 2, 2, HALF, width // 2), lambda y, h, w: (y, h, 0, 0, 0, 0)),
        ),
        out_shape=jax.ShapeDtypeStruct((4, 2, 2, 2, HALF, width // 2), F32),
        compiler_params=pltpu.CompilerParams(vmem_limit_bytes=40 * 2**20),
        cost_estimate=pl.CostEstimate(flops=4 * rows * 2048 * width, bytes_accessed=17 * 2**20, transcendentals=0),
    )(where, acts, acts, acts_other, acts_other, grads, grads_other)


def root_kernel(where_ref, block_ref, mine_ref, other_ref, out_ref, last):
    core = where_ref[1]
    last[pl.ds(pl.multiple_of(core * HALF, HALF), HALF), :] = mine_ref[...]
    last[pl.ds(pl.multiple_of((1 - core) * HALF, HALF), HALF), :] = other_ref[...]
    row = lax.broadcasted_iota(jnp.int32, (BS, BS), 0)
    col = lax.broadcasted_iota(jnp.int32, (BS, BS), 1)
    identity = jnp.where(row == col, 1.0, 0.0).astype(F32)
    mul = functools.partial(jnp.dot, precision=HIGHEST, preferred_element_type=F32)

    def start(summed):
        factor = summed * (1.0 / TOKENS) + DAMPING * identity
        norm = jnp.sqrt(jnp.sum(factor * factor, keepdims=True))
        current = factor / norm
        step = 1.5 * identity - 0.5 * current
        return norm, mul(current, step), step

    norm_a, cur_a, est_a = start(block_ref[...])
    norm_b, cur_b, est_b = start(last[...])

    def advance(_, carry):
        cur_a, est_a, cur_b, est_b = carry
        step_a = 1.5 * identity - 0.5 * mul(est_a, cur_a)
        step_b = 1.5 * identity - 0.5 * mul(est_b, cur_b)
        return mul(cur_a, step_a), mul(step_a, est_a), mul(cur_b, step_b), mul(step_b, est_b)

    cur_a, est_a, cur_b, est_b = lax.fori_loop(0, ITERS - 2, advance, (cur_a, est_a, cur_b, est_b))
    step_a = 1.5 * identity - 0.5 * mul(est_a, cur_a)
    step_b = 1.5 * identity - 0.5 * mul(est_b, cur_b)
    out_ref[0] = (mul(step_a, est_a) / jnp.sqrt(norm_a)).astype(BF16)
    out_ref[1] = (mul(step_b, est_b) / jnp.sqrt(norm_b)).astype(BF16)


def two_roots(where, block, mine, other):
    return pl.pallas_call(
        root_kernel,
        grid_spec=pltpu.PrefetchScalarGridSpec(
            num_scalar_prefetch=1,
            grid=(1,),
            in_specs=[
                pl.BlockSpec((BS, BS), lambda i, w: (0, 0)),
                pl.BlockSpec((HALF, BS), lambda i, w: (0, 0)),
                pl.BlockSpec((HALF, BS), lambda i, w: (0, 0)),
            ],
            out_specs=pl.BlockSpec((2, BS, BS), lambda i, w: (0, 0, 0)),
            scratch_shapes=[pltpu.VMEM((BS, BS), F32)],
        ),
        out_shape=jax.ShapeDtypeStruct((2, BS, BS), BF16),
        compiler_params=pltpu.CompilerParams(vmem_limit_bytes=32 * 2**20),
        cost_estimate=pl.CostEstimate(flops=2 * 36 * 6 * 2 * BS**3, bytes_accessed=2**20, transcendentals=0),
    )(where, block, mine, other)


def apply_kernel(where_ref, mine_ref, other_ref, left_ref, right_ref, last_ref, out_ref, rows_ref):
    core = where_ref[1]
    cols = pl.ds(pl.multiple_of(where_ref[2] * HALF, HALF), HALF)

    def side(at, part):
        rows = pl.ds(pl.multiple_of(at * HALF, HALF), HALF)
        return lax.dot_general(
            left_ref[rows, cols].astype(F32), part, (((0,), (0,)), ((), ())), precision=HIGHEST, preferred_element_type=F32
        )

    rows_ref[...] = side(core, mine_ref[...]) + side(1 - core, other_ref[...])
    kept = rows_ref[pl.ds(pl.multiple_of(core * 64, 64), 64), :]
    for block in range(5):
        root = right_ref[block] if block < 4 else last_ref[...]
        span = slice(block * BS, (block + 1) * BS)
        value = jnp.dot(kept[:, span], root.astype(F32), precision=HIGHEST, preferred_element_type=F32)
        out_ref[:, span] = (value * (1.0 / math.sqrt(TOKENS))).astype(BF16)


def apply_roots(where, mine, other, left, right, last):
    width = mine.shape[1]
    return pl.pallas_call(
        apply_kernel,
        grid_spec=pltpu.PrefetchScalarGridSpec(
            num_scalar_prefetch=1,
            grid=(1,),
            in_specs=[
                pl.BlockSpec((HALF, width), lambda i, w: (0, 0)),
                pl.BlockSpec((HALF, width), lambda i, w: (0, 0)),
                pl.BlockSpec((BS, BS), lambda i, w: (0, 0)),
                pl.BlockSpec((4, BS, BS), lambda i, w: (0, 0, 0)),
                pl.BlockSpec((BS, BS), lambda i, w: (0, 0)),
            ],
            out_specs=pl.BlockSpec((64, width), lambda i, w: (0, 0)),
            scratch_shapes=[pltpu.VMEM((HALF, width), F32)],
        ),
        out_shape=jax.ShapeDtypeStruct((64, width), BF16),
        compiler_params=pltpu.CompilerParams(vmem_limit_bytes=32 * 2**20),
        cost_estimate=pl.CostEstimate(flops=12 * 2 * HALF * BS * width, bytes_accessed=3 * 2**20, transcendentals=0),
    )(where, mine, other, left, right, last)


def swap(value, axis):
    return lax.ppermute(value, axis, [(0, 1), (1, 0)])


def per_device(acts, grads, owners):
    zh, y, x, core, column = (lax.axis_index(a) for a in ("zh", "y", "x", "c", "mp"))
    x_high, x_low = x // 2, x % 2
    rows, width = grads.shape
    where = jnp.stack([column, core, x_low]).astype(jnp.int32)

    with jax.named_scope("exchange"):
        halves = acts.reshape(rows, 16, 2, HALF)
        sent = jnp.where(core == 0, halves[:, :, 1], halves[:, :, 0]).reshape(rows, 16 * HALF)
        acts_other = swap(sent, "c")
        grads_other = swap(grads, "c")

    with jax.named_scope("factors"):
        parts = factor_parts(where, acts, grads)
        mine = parts[0] + swap(parts[1], "c")

    with jax.named_scope("product"):
        raw = product(where, acts, acts_other, grads, grads_other)
        raw = raw.reshape(16 * 2 * HALF, width // 2)
        raw = lax.psum_scatter(raw, ("y", "x"), scatter_dimension=0, tiled=True)
        raw = raw.reshape(2, HALF, width // 2)

    with jax.named_scope("sum_factors"):
        mine = lax.all_to_all(mine.reshape(16 * 96, BS), ("y", "x"), 0, 0, tiled=True)
        mine = jnp.sum(mine.reshape(16, 96, BS), axis=0)
        mine = jnp.broadcast_to(mine, (8, 96, BS)).reshape(8 * 96, BS)
        mine = lax.all_to_all(mine, ("zh", "y"), 0, 0, tiled=True).reshape(2, 4, 96, BS)
        mine = mine[0] + mine[1]
        block = mine[:, :64].reshape(BS, BS)
        last_half = mine[:, 64:].reshape(HALF, BS)

    with jax.named_scope("roots"):
        roots = two_roots(where, block, last_half, swap(last_half, "c"))
        last_root = roots[1]
        four = jnp.broadcast_to(roots[0], (4, BS, BS)).reshape(4 * BS, BS)
        four = lax.all_to_all(four, "x", 0, 0, tiled=True).reshape(4, BS, BS)
        other_four = swap(four, "c")
        input_roots = jnp.where(core == 0, four, other_four)
        output_roots = jnp.where(core == 0, other_four, four)

    with jax.named_scope("left_root"):
        holder = zh * 2 + y // 2
        left = lax.dynamic_index_in_dim(input_roots, (y % 2) * 2 + x_high, 0, keepdims=False)
        got = jnp.zeros_like(left)
        for shift in range(1, 4):
            pairs = []
            for a in range(2):
                for b in range(4):
                    source = a * 2 + b // 2
                    pairs.append(((a * 4 + b) * 4 + source, (a * 4 + b) * 4 + (source + shift) % 4))
            got = got + lax.ppermute(left, ("zh", "y", "mp"), pairs)
        left = jnp.where(column == holder, left, got)

    with jax.named_scope("kept"):
        data_rank = ((zh * 4 + y) * 4 + x) * 2 + core
        owned = (owners[0] == data_rank).astype(jnp.int32)
        order = jnp.cumsum(owned) - 1
        slots = jnp.arange(MOST, dtype=jnp.int32)
        select = owned[None, :] * (order[None, :] == slots[:, None]).astype(jnp.int32)
        filled = jnp.sum(select, axis=1)
        place = jnp.argmax(select, axis=1)
        every = jnp.concatenate([input_roots, output_roots, last_root[None]], axis=0)
        kept = jnp.stack(
            [
                jnp.where(filled[s] > 0, lax.dynamic_index_in_dim(every, place[s], 0, keepdims=False), 0).astype(BF16)
                for s in range(MOST)
            ]
        )

    with jax.named_scope("finish"):
        away = lax.dynamic_index_in_dim(raw, 1 - zh, 0, keepdims=False)
        stay = lax.dynamic_index_in_dim(raw, zh, 0, keepdims=False)
        total = stay + swap(away, "zh")
        beside = lax.ppermute(total, "x", [(0, 1), (1, 0), (2, 3), (3, 2)])
        pair = jnp.where(
            x_low == 0, jnp.concatenate([total, beside], axis=1), jnp.concatenate([beside, total], axis=1)
        )
        update = apply_roots(where, pair, swap(pair, "c"), left, output_roots, last_root)
    return update, kept


def solution(mesh):
    fine = Mesh(mesh.devices.reshape(2, 4, 4, 2, 4), ("zh", "y", "x", "c", "mp"))
    return jax.shard_map(
        per_device,
        mesh=fine,
        in_specs=(P(DP, None), P(DP, "mp"), P("mp", None)),
        out_specs=(P(DP, "mp"), P(DP, "mp", None)),
        check_vma=False,
    )
```

time: 2140 us -> 233 us (0.11)
  waiting for transfers between devices: 2040 us -> 72.5 us
  matrix products: 58.2 us -> 0 us
  blocking collectives: 0 us -> 41.5 us
  Pallas kernels: 0 us -> 40.9 us
    psum x2 -> x0, waiting for transfers between devices: 1540 us -> none  [the longest x1 779 us: per_device(): summed = lax.psum(partial_sums, 'dp')]
    reduce_scatter x1, waiting for transfers between devices: 450 us -> 13.5 us  [per_device(): raw = lax.psum_scatter(raw, ('y', 'x'), scatter_dimension=0, tiled=True)]
    dot_general x51 -> x0, matrix products: 58.2 us -> none  [the longest x12 12.6 us: advance(): jnp.matmul(current, factor, precision=lax.Precision.HIGHEST)]
    all_gather x1 -> x0, waiting for transfers between devices: 46.6 us -> none  [per_device(): input_roots = lax.all_gather(roots[:input_count], 'mp', axis=0, tiled=True)]
    all_to_all x0 -> x1, blocking collectives: none -> 41.5 us  [per_device(): lax.all_to_all(mine.reshape(16 * 96, BS), ('y', 'x'), 0, 0, tiled=True)]
    pallas_call x0 -> x4, Pallas kernels: none -> 40.9 us  [the longest x1 21.2 us: two_roots(): pl.pallas_call(root_kernel, grid_spec=pltpu.PrefetchScalarGridSpec(num_sc...]
    ppermute x0 -> x11, waiting for transfers between devices: none -> 36.3 us  [the longest x7 17.8 us: swap(): return lax.ppermute(value, axis, [(0, 1), (1, 0)])]
    all_to_all x0 -> x2, waiting for transfers between devices: none -> 22.8 us  [the longest x1 22.8 us: per_device(): lax.all_to_all(mine, ('zh', 'y'), 0, 0, tiled=True).reshape(2, 4, 96, BS)]
  transfers between devices with their start and end apart: 4 -> 14, of which waited for: 4 -> 9; matrix products, arithmetic and copies ran while one was open for 0% -> 3% of each run, Pallas kernels for 0% -> 11%
where the time goes in v1:
time: 233 us; the launch traced here: 230 us
  waiting for transfers between devices  72.5 us (31%)
  blocking collectives  41.5 us (18%)
  Pallas kernels  40.9 us (18%)
  local copies, waits for them, and re-layouts  28.1 us (12%)
  starting transfers between devices  20 us (9%)
  between operations  19.5 us (8%)
  other arithmetic  7.39 us (3%)
    all_to_all x1, blocking collectives, per_device(): lax.all_to_all(mine.reshape(16 * 96, BS), ('y', 'x'), 0, 0, tiled=True)  41.5 us
    all_to_all x1, waiting for transfers between devices, per_device(): lax.all_to_all(mine, ('zh', 'y'), 0, 0, tiled=True).reshape(2, 4, 96, BS)  22.8 us
    pallas_call x1, Pallas kernels, two_roots(): pl.pallas_call(root_kernel, grid_spec=pltpu.PrefetchScalarGridSpec(num_sc...  21.2 us
    ppermute x7, waiting for transfers between devices, swap(): return lax.ppermute(value, axis, [(0, 1), (1, 0)])  17.8 us
    ppermute x3, waiting for transfers between devices, per_device(): got = got + lax.ppermute(left, ('zh', 'y', 'mp'), pairs)  17 us
    reduce_scatter x1, waiting for transfers between devices, per_device(): raw = lax.psum_scatter(raw, ('y', 'x'), scatter_dimension=0, tiled=True)  13.5 us
    pallas_call x1, Pallas kernels, product(): pl.pallas_call(product_kernel, grid_spec=pltpu.PrefetchScalarGridSpec(num...  12.7 us
    slice x1, local copies, waits for them, and re-layouts, per_device(): halves[:, :, 1]  9.87 us
  transfers between devices with their start and end apart: 14, of which 9 were waited for; matrix products, arithmetic and copies ran while one was open for 3% of the time, Pallas kernels for 11%

profile of v1, /device:TPU:32, one launch (start us, length us, event | category | flops | bytes accessed | tf_op | source)
XLA Modules:
  0.0 230.0 jit_solution(17093007956314349053)
XLA Ops:
  7.2 7.7 %reshape.83 = bf16[512,16,2,128]{3,2,1,0:T(2,128)(2,1)} reshape(bf16[512,4096]{1,0:T(8,128)(2,1)} %acts_ref.1) | data formatting | bytes 8388608 | tf_op jit(solution)/shard_map/exchange/reshape | solution.py:209
  14.9 9.9 %fusion.4 = (bf16[512,16,1,128]{3,2,1,0:T(2,128)(2,1)}, bf16[512,16,1,128]{3,2,1,0:T(2,128)(2,1)}) fusion(bf16[512,16,2,128]{3,2,1,0:T(2,128)(2,1)} %reshape.83), kind=kLoop, calls=%fused_computation.27 | loop fusion | bytes 8388608 | tf_op jit(solution)/shard_map/exchange/slice | solution.py:210
  24.8 3.9 %copy_select_fusion = bf16[512,16,1,128]{3,1,0,2:T(8,128)(2,1)S(1)} fusion(bf16[512,16,1,128]{3,2,1,0:T(2,128)(2,1)} %get-tuple-element.5, bf16[512,16,1,128]{3,2,1,0:T(2,128)(2,1)} %get-tuple-element.4, pred[]{:T(512)S(6)} %eq.41), kind=kLoop, calls=%fused_computation.1 | loop fusion | flops 1048576 | bytes 6291457 | tf_op jit(solution)/shard_map/exchange/jit(_where)/select_n | solution.py:210
  28.7 1.9 copy.15
  31.2 5.2 %collective-permute-done.1.grads_other = bf16[512,1280]{1,0:T(8,128)(2,1)} collective-permute-done((bf16[512,1280]{1,0:T(8,128)(2,1)S(1)}, bf16[512,1280]{1,0:T(8,128)(2,1)}, u32[]{:S(2)}, u32[]{:S(2)}) %collective-permute-start.1) | collective-permute-done | bytes 1310752 | tf_op jit(solution)/shard_map/exchange/ppermute | solution.py:199
  36.9 2.2 copy-done
  39.1 12.7 %product.1 = f32[4,2,2,2,128,640]{5,4,3,2,1,0:T(8,128)} custom-call(s32[3]{0:T(128)S(1)} %pad_add_fusion.where_ref, bf16[512,4096]{1,0:T(8,128)(2,1)S(1)} %copy-done, bf16[512,4096]{1,0:T(8,128)(2,1)S(1)} %copy-done, bf16[512,2048]{1,0:T(8,128)(2,1)S(1)} %collective-permute-done.low_other.high_other, ...), custom_call_target="tpu_custom_call" | custom-call | flops 5368709120 | bytes 17825792 | tf_op jit(solution)/shard_map/product/pallas_call | solution.py:83
  51.8 2.2 copy-done.1
  54.0 3.6 %factors.1 = f32[2,4,4,96,256]{4,3,2,1,0:T(8,128)S(1)} custom-call(s32[3]{0:T(128)S(1)} %pad_add_fusion.where_ref, bf16[512,4096]{1,0:T(8,128)(2,1)S(1)} %copy-done.1, bf16[512,1280]{1,0:T(8,128)(2,1)S(1)} %copy-done.2), custom_call_target="tpu_custom_call" | custom-call | flops 603979776 | bytes 6291456 | tf_op jit(solution)/shard_map/factors/pallas_call | solution.py:55
  57.9 3.3 %collective-permute-done.5 = f32[4,4,96,256]{3,2,1,0:T(8,128)S(1)} collective-permute-done((f32[4,4,96,256]{3,2,1,0:T(8,128)S(1)}, f32[4,4,96,256]{3,2,1,0:T(8,128)S(1)}, u32[]{:S(2)}, u32[]{:S(2)}) %collective-permute-start.5) | collective-permute-done | bytes 1572896 | tf_op jit(solution)/shard_map/factors/ppermute | solution.py:199
  61.4 41.5 %all_to_all.21 = f32[16,96,256]{2,1,0:T(8,128)S(1)} all-to-all(f32[16,96,256]{2,1,0:T(8,128)S(1)} %bitcast.47), channel_id=1, replica_groups=mesh['zh'=2,'y'=4,'x'=4,'c'=2,'mp'=4] {'y','x'}, dimensions={0} | all-to-all | bytes 3145728 | tf_op jit(solution)/shard_map/sum_factors/all_to_all | solution.py:225
  104.0 7.2 %all-to-all-start.1 = ((f32[8,96,256]{2,1,0:T(8,128)}), f32[8,96,256]{2,1,0:T(8,128)S(1)}, u32[]{:S(2)}, u32[]{:S(2)}) async-start(f32[8,96,256]{2,1,0:T(8,128)} %broadcast_in_dim.14), calls=%async_computation.2 | async-start | bytes 1572864 | tf_op jit(solution)/shard_map/sum_factors/all_to_all | solution.py:228
  111.1 22.8 %all-to-all-done.1 = f32[8,96,256]{2,1,0:T(8,128)S(1)} async-done(((f32[8,96,256]{2,1,0:T(8,128)}), f32[8,96,256]{2,1,0:T(8,128)S(1)}, u32[]{:S(2)}, u32[]{:S(2)}) %all-to-all-start.1) | async-done | bytes 786464 | tf_op jit(solution)/shard_map/sum_factors/all_to_all | solution.py:228
  134.3 1.1 collective-permute-done.6.other_ref
  135.4 21.2 %roots.1 = bf16[2,256,256]{2,1,0:T(8,128)(2,1)S(1)} custom-call(s32[3]{0:T(128)S(1)} %pad_add_fusion.where_ref, f32[256,256]{1,0:T(8,128)S(1)} %bitcast.42, f32[128,256]{1,0:T(8,128)S(1)} %bitcast.44, f32[128,256]{1,0:T(8,128)S(1)} %collective-permute-done.6.other_ref), custom_call_target="tpu_custom_call" | custom-call | flops 14495514624 | bytes 1048576 | tf_op jit(solution)/shard_map/roots/pallas_call | solution.py:137
  157.5 3.5 %all-to-all-start.2 = ((bf16[4,256,256]{2,1,0:T(8,128)(2,1)}), bf16[4,256,256]{2,1,0:T(8,128)(2,1)S(1)}, u32[]{:S(2)}, u32[]{:S(2)}) async-start(bf16[4,256,256]{2,1,0:T(8,128)(2,1)} %broadcast_in_dim.15), calls=%async_computation.3 | async-start | bytes 1048576 | tf_op jit(solution)/shard_map/roots/all_to_all | solution.py:237
  161.0 13.5 %reduce-scatter.2.cloned.1.call-done = f32[256,640]{1,0:T(8,128)} async-done(((f32[4096,640]{1,0:T(8,128)}), f32[256,640]{1,0:T(8,128)}) %reduce-scatter.2.cloned.1.call-update) | async-done | bytes 655376 | tf_op jit(solution)/shard_map/product/reduce_scatter | solution.py:221
  175.4 5.4 %collective-permute-start.2 = (f32[128,640]{1,0:T(8,128)S(1)}, f32[128,640]{1,0:T(8,128)S(1)}, u32[]{:S(2)}, u32[]{:S(2)}) collective-permute-start(f32[128,640]{1,0:T(8,128)S(1)} %dynamic-slice_bitcast_fusion), channel_id=1, source_target_pairs={{0,128},{128,0},{1,129},{129,1},{2,130},{130,2},{3,131},{131,3},{4... | collective-permute-start | bytes 983048 | tf_op jit(solution)/shard_map/finish/ppermute | solution.py:199
  182.2 7.8 %collective-permute-done.2 = f32[128,640]{1,0:T(8,128)S(1)} collective-permute-done((f32[128,640]{1,0:T(8,128)S(1)}, f32[128,640]{1,0:T(8,128)S(1)}, u32[]{:S(2)}, u32[]{:S(2)}) %collective-permute-start.2) | collective-permute-done | bytes 327712 | tf_op jit(solution)/shard_map/finish/ppermute | solution.py:199
  190.0 1.0 bitcast_add_fusion
  197.4 1.4 collective-permute-done.3
  199.7 1.3 collective-permute-start.8
  202.6 17.0 %collective-permute-done.8 = bf16[256,256]{1,0:T(8,128)(2,1)S(1)} collective-permute-done((bf16[256,256]{1,0:T(8,128)(2,1)S(1)}, bf16[256,256]{1,0:T(8,128)(2,1)S(1)}, u32[]{:S(2)}, u32[]{:S(2)}) %collective-permute-start.8) | collective-permute-done | bytes 131104 | tf_op jit(solution)/shard_map/left_root/ppermute | solution.py:252
  219.7 3.5 %finish.1 = bf16[64,1280]{1,0:T(8,128)(2,1)} custom-call(s32[3]{0:T(128)S(1)} %pad_add_fusion.where_ref, f32[128,1280]{1,0:T(8,128)S(1)} %maximum_select_fusion.mine_ref, f32[128,1280]{1,0:T(8,128)S(1)} %collective-permute-done.4.other_ref, bf16[256,256]{1,0:T(8,128)(2,1)S(1)} %add_select_fusion.left_ref, ...), custom_call_target="tpu_custom_call" | custom-call | flops 1006632960 | bytes 3145728 | tf_op jit(solution)/shard_map/finish/pallas_call | solution.py:177
  (48 shorter events, 9.9 us)
Async XLA Ops:
  7.2 167.3 %reduce-scatter.2.cloned.1.call-start = ((), (), s32[]{:S(2)}) async-start(), calls=%async_computation.4 | async-start | bytes 11141120 | tf_op jit(solution)/shard_map/product/reduce_scatter | solution.py:221
  28.7 1.9 copy-start.2
  30.6 6.2 %collective-permute-start = (bf16[512,2048]{1,0:T(8,128)(2,1)}, bf16[512,2048]{1,0:T(8,128)(2,1)S(1)}, u32[]{:S(2)}, u32[]{:S(2)}) collective-permute-start(bf16[512,2048]{1,0:T(8,128)(2,1)} %bitcast.41), channel_id=1, source_target_pairs={{0,4},{4,0},{1,5},{5,1},{2,6},{6,2},{3,7},{7,3},{8,12},{12,8},{9,1... | collective-permute-start | bytes 6291464 | tf_op jit(solution)/shard_map/exchange/ppermute | solution.py:199
  30.7 5.8 %collective-permute-start.1 = (bf16[512,1280]{1,0:T(8,128)(2,1)S(1)}, bf16[512,1280]{1,0:T(8,128)(2,1)}, u32[]{:S(2)}, u32[]{:S(2)}) collective-permute-start(bf16[512,1280]{1,0:T(8,128)(2,1)S(1)} %copy-done.2), channel_id=1, source_target_pairs={{0,4},{4,0},{1,5},{5,1},{2,6},{6,2},{3,7},{7,3},{8,12},{12,8},{9,1... | collective-permute-start | bytes 3932168 | tf_op jit(solution)/shard_map/exchange/ppermute | solution.py:199
  36.9 2.2 copy-start
  51.8 2.2 copy-start.1
  57.7 3.5 %collective-permute-start.5 = (f32[4,4,96,256]{3,2,1,0:T(8,128)S(1)}, f32[4,4,96,256]{3,2,1,0:T(8,128)S(1)}, u32[]{:S(2)}, u32[]{:S(2)}) collective-permute-start(f32[4,4,96,256]{3,2,1,0:T(8,128)S(1)} %slice_bitcast_fusion), channel_id=1, source_target_pairs={{0,4},{4,0},{1,5},{5,1},{2,6},{6,2},{3,7},{7,3},{8,12},{12,8},{9,1... | collective-permute-start | bytes 4718600 | tf_op jit(solution)/shard_map/factors/ppermute | solution.py:199
  103.0 31.1 %copy-start.3 = (s32[1,9]{1,0:T(1,128)S(1)}, s32[1,9]{1,0:T(1,128)}, u32[]{:S(2)}) copy-start(s32[1,9]{1,0:T(1,128)} %param.5) | copy-start | bytes 112
  104.0 29.9 %all-to-all-start.1 = ((f32[8,96,256]{2,1,0:T(8,128)}), f32[8,96,256]{2,1,0:T(8,128)S(1)}, u32[]{:S(2)}, u32[]{:S(2)}) async-start(f32[8,96,256]{2,1,0:T(8,128)} %broadcast_in_dim.14), calls=%async_computation.2 | async-start | bytes 1572864 | tf_op jit(solution)/shard_map/sum_factors/all_to_all | solution.py:228
  134.0 1.4 collective-permute-start.6
  157.5 23.9 %all-to-all-start.2 = ((bf16[4,256,256]{2,1,0:T(8,128)(2,1)}), bf16[4,256,256]{2,1,0:T(8,128)(2,1)S(1)}, u32[]{:S(2)}, u32[]{:S(2)}) async-start(bf16[4,256,256]{2,1,0:T(8,128)(2,1)} %broadcast_in_dim.15), calls=%async_computation.3 | async-start | bytes 1048576 | tf_op jit(solution)/shard_map/roots/all_to_all | solution.py:237
  175.4 14.5 %collective-permute-start.2 = (f32[128,640]{1,0:T(8,128)S(1)}, f32[128,640]{1,0:T(8,128)S(1)}, u32[]{:S(2)}, u32[]{:S(2)}) collective-permute-start(f32[128,640]{1,0:T(8,128)S(1)} %dynamic-slice_bitcast_fusion), channel_id=1, source_target_pairs={{0,128},{128,0},{1,129},{129,1},{2,130},{130,2},{3,131},{131,3},{4... | collective-permute-start | bytes 983048 | tf_op jit(solution)/shard_map/finish/ppermute | solution.py:199
  181.4 15.9 %collective-permute-start.7 = (bf16[4,256,256]{2,1,0:T(8,128)(2,1)S(1)}, bf16[4,256,256]{2,1,0:T(8,128)(2,1)S(1)}, u32[]{:S(2)}, u32[]{:S(2)}) collective-permute-start(bf16[4,256,256]{2,1,0:T(8,128)(2,1)S(1)} %all-to-all-done.2), channel_id=1, source_target_pairs={{0,4},{4,0},{1,5},{5,1},{2,6},{6,2},{3,7},{7,3},{8,12},{12,8},{9,1... | collective-permute-start | bytes 1572872 | tf_op jit(solution)/shard_map/roots/ppermute | solution.py:199
  191.0 7.8 %collective-permute-start.3 = (f32[128,640]{1,0:T(8,128)S(1)}, f32[128,640]{1,0:T(8,128)S(1)}, u32[]{:S(2)}, u32[]{:S(2)}) collective-permute-start(f32[128,640]{1,0:T(8,128)S(1)} %bitcast_add_fusion), channel_id=1, source_target_pairs={{0,8},{8,0},{16,24},{24,16},{1,9},{9,1},{17,25},{25,17},{2,10},{10... | collective-permute-start | bytes 983048 | tf_op jit(solution)/shard_map/finish/ppermute | solution.py:275
  198.9 20.8 %collective-permute-start.4 = (f32[128,1280]{1,0:T(8,128)S(1)}, f32[128,1280]{1,0:T(8,128)S(1)}, u32[]{:S(2)}, u32[]{:S(2)}) collective-permute-start(f32[128,1280]{1,0:T(8,128)S(1)} %maximum_select_fusion.mine_ref), channel_id=1, source_target_pairs={{0,4},{4,0},{1,5},{5,1},{2,6},{6,2},{3,7},{7,3},{8,12},{12,8},{9,1... | collective-permute-start | bytes 1966088 | tf_op jit(solution)/shard_map/finish/ppermute | solution.py:199
  199.0 3.6 %collective-permute-start.10 = (bf16[256,256]{1,0:T(8,128)(2,1)S(1)}, bf16[256,256]{1,0:T(8,128)(2,1)S(1)}, u32[]{:S(2)}, u32[]{:S(2)}) collective-permute-start(bf16[256,256]{1,0:T(8,128)(2,1)S(1)} %dynamic-slice_bitcast_fusion.1), channel_id=1, source_target_pairs={{0,3},{32,35},{65,64},{97,96},{130,129},{162,161},{195,194},{227,2... | collective-permute-start | bytes 393224 | tf_op jit(solution)/shard_map/left_root/ppermute | solution.py:252
  199.7 19.9 %collective-permute-start.8 = (bf16[256,256]{1,0:T(8,128)(2,1)S(1)}, bf16[256,256]{1,0:T(8,128)(2,1)S(1)}, u32[]{:S(2)}, u32[]{:S(2)}) collective-permute-start(bf16[256,256]{1,0:T(8,128)(2,1)S(1)} %dynamic-slice_bitcast_fusion.1), channel_id=1, source_target_pairs={{0,1},{32,33},{65,66},{97,98},{130,131},{162,163},{195,192},{227,2... | collective-permute-start | bytes 393224 | tf_op jit(solution)/shard_map/left_root/ppermute | solution.py:252
  201.0 18.6 %collective-permute-start.9 = (bf16[256,256]{1,0:T(8,128)(2,1)S(1)}, bf16[256,256]{1,0:T(8,128)(2,1)S(1)}, u32[]{:S(2)}, u32[]{:S(2)}) collective-permute-start(bf16[256,256]{1,0:T(8,128)(2,1)S(1)} %dynamic-slice_bitcast_fusion.1), channel_id=1, source_target_pairs={{0,2},{32,34},{65,67},{97,99},{130,128},{162,160},{195,193},{227,2... | collective-permute-start | bytes 393224 | tf_op jit(solution)/shard_map/left_root/ppermute | solution.py:252
Sparse Core Ops, SparseCore 0:
  51.9 122.4 reduce-scatter.1

commit v2 on v1

--- a/solution.py
+++ b/solution.py
@@ -70,34 +70,34 @@
 
 
 def product_kernel(where_ref, low_ref, high_ref, low_other, high_other, grads_ref, grads_other, out_ref):
-    width = grads_ref.shape[1] // 2
     for zh, (mine, other) in enumerate(((low_ref, low_other), (high_ref, high_other))):
         for xl in range(2):
-            cols = slice(xl * width, (xl + 1) * width)
-            out_ref[0, 0, xl, zh] = tdot(mine[...], grads_ref[:, cols]) + tdot(other[...], grads_other[:, cols])
+            cols = slice(xl * HALF, (xl + 1) * HALF)
+            out_ref[0, 0, xl, zh] = tdot(mine[:, cols], grads_ref[...]) + tdot(other[:, cols], grads_other[...])
 
 
 def product(where, acts, acts_other, grads, grads_other):
-    rows, width = grads.shape
-    whole = pl.BlockSpec((rows, width), lambda y, h, w: (0, 0))
+    rows, width = grads_other.shape
+    low = pl.BlockSpec((rows, BS), lambda y, h, w: (0, y * 2 + h))
+    high = pl.BlockSpec((rows, BS), lambda y, h, w: (0, 8 + y * 2 + h))
     return pl.pallas_call(
         product_kernel,
         grid_spec=pltpu.PrefetchScalarGridSpec(
             num_scalar_prefetch=1,
             grid=(4, 2),
             in_specs=[
-                pl.BlockSpec((rows, HALF), lambda y, h, w: (0, 2 * (y * 2 + h) + w[1])),
-                pl.BlockSpec((rows, HALF), lambda y, h, w: (0, 2 * (8 + y * 2 + h) + w[1])),
-                pl.BlockSpec((rows, HALF), lambda y, h, w: (0, y * 2 + h)),
-                pl.BlockSpec((rows, HALF), lambda y, h, w: (0, 8 + y * 2 + h)),
-                whole,
-                whole,
-            ],
-            out_specs=pl.BlockSpec((1, 1, 2, 2, HALF, width // 2), lambda y, h, w: (y, h, 0, 0, 0, 0)),
-        ),
-        out_shape=jax.ShapeDtypeStruct((4, 2, 2, 2, HALF, width // 2), F32),
+                low,
+                high,
+                low,
+                high,
+                pl.BlockSpec((rows, width), lambda y, h, w: (0, w[1])),
+                pl.BlockSpec((rows, width), lambda y, h, w: (0, 0)),
+            ],
+            out_specs=pl.BlockSpec((1, 1, 2, 2, HALF, width), lambda y, h, w: (y, h, 0, 0, 0, 0)),
+        ),
+        out_shape=jax.ShapeDtypeStruct((4, 2, 2, 2, HALF, width), F32),
         compiler_params=pltpu.CompilerParams(vmem_limit_bytes=40 * 2**20),
-        cost_estimate=pl.CostEstimate(flops=4 * rows * 2048 * width, bytes_accessed=17 * 2**20, transcendentals=0),
+        cost_estimate=pl.CostEstimate(flops=4 * rows * 4096 * width, bytes_accessed=20 * 2**20, transcendentals=0),
     )(where, acts, acts, acts_other, acts_other, grads, grads_other)
 
 
@@ -153,9 +153,10 @@
     )(where, block, mine, other)
 
 
-def apply_kernel(where_ref, mine_ref, other_ref, left_ref, right_ref, last_ref, out_ref, rows_ref):
-    core = where_ref[1]
-    cols = pl.ds(pl.multiple_of(where_ref[2] * HALF, HALF), HALF)
+def apply_kernel(where_ref, mine_ref, beside_ref, mine_other, beside_other, left_ref, right_ref, last_ref, out_ref, rows_ref):
+    core, x_low = where_ref[1], where_ref[2]
+    width = mine_ref.shape[1]
+    cols = pl.ds(pl.multiple_of(x_low * HALF, HALF), HALF)
 
     def side(at, part):
         rows = pl.ds(pl.multiple_of(at * HALF, HALF), HALF)
@@ -163,7 +164,9 @@
             left_ref[rows, cols].astype(F32), part, (((0,), (0,)), ((), ())), precision=HIGHEST, preferred_element_type=F32
         )
 
-    rows_ref[...] = side(core, mine_ref[...]) + side(1 - core, other_ref[...])
+    for at, mine, beside in ((core, mine_ref, beside_ref), (1 - core, mine_other, beside_other)):
+        span = pl.ds(pl.multiple_of(at * width, HALF), width)
+        rows_ref[:, span] = side(x_low, mine[...]) + side(1 - x_low, beside[...])
     kept = rows_ref[pl.ds(pl.multiple_of(core * 64, 64), 64), :]
     for block in range(5):
         root = right_ref[block] if block < 4 else last_ref[...]
@@ -172,27 +175,30 @@
         out_ref[:, span] = (value * (1.0 / math.sqrt(TOKENS))).astype(BF16)
 
 
-def apply_roots(where, mine, other, left, right, last):
-    width = mine.shape[1]
+def apply_roots(where, pieces, left, right, last):
+    width = pieces[0].shape[1]
+    piece = pl.BlockSpec((HALF, width), lambda i, w: (0, 0))
     return pl.pallas_call(
         apply_kernel,
         grid_spec=pltpu.PrefetchScalarGridSpec(
             num_scalar_prefetch=1,
             grid=(1,),
             in_specs=[
-                pl.BlockSpec((HALF, width), lambda i, w: (0, 0)),
-                pl.BlockSpec((HALF, width), lambda i, w: (0, 0)),
+                piece,
+                piece,
+                piece,
+                piece,
                 pl.BlockSpec((BS, BS), lambda i, w: (0, 0)),
                 pl.BlockSpec((4, BS, BS), lambda i, w: (0, 0, 0)),
                 pl.BlockSpec((BS, BS), lambda i, w: (0, 0)),
             ],
-            out_specs=pl.BlockSpec((64, width), lambda i, w: (0, 0)),
-            scratch_shapes=[pltpu.VMEM((HALF, width), F32)],
-        ),
-        out_shape=jax.ShapeDtypeStruct((64, width), BF16),
+            out_specs=pl.BlockSpec((64, 2 * width), lambda i, w: (0, 0)),
+            scratch_shapes=[pltpu.VMEM((HALF, 2 * width), F32)],
+        ),
+        out_shape=jax.ShapeDtypeStruct((64, 2 * width), BF16),
         compiler_params=pltpu.CompilerParams(vmem_limit_bytes=32 * 2**20),
-        cost_estimate=pl.CostEstimate(flops=12 * 2 * HALF * BS * width, bytes_accessed=3 * 2**20, transcendentals=0),
-    )(where, mine, other, left, right, last)
+        cost_estimate=pl.CostEstimate(flops=12 * 4 * HALF * BS * width, bytes_accessed=3 * 2**20, transcendentals=0),
+    )(where, *pieces, left, right, last)
 
 
 def swap(value, axis):
@@ -206,10 +212,9 @@
     where = jnp.stack([column, core, x_low]).astype(jnp.int32)
 
     with jax.named_scope("exchange"):
-        halves = acts.reshape(rows, 16, 2, HALF)
-        sent = jnp.where(core == 0, halves[:, :, 1], halves[:, :, 0]).reshape(rows, 16 * HALF)
-        acts_other = swap(sent, "c")
-        grads_other = swap(grads, "c")
+        acts_other = swap(acts, "c")
+        sent = lax.dynamic_slice_in_dim(grads, (1 - core) * (width // 2), width // 2, 1)
+        grads_other = swap(sent, "c")
 
     with jax.named_scope("factors"):
         parts = factor_parts(where, acts, grads)
@@ -269,14 +274,13 @@
         )
 
     with jax.named_scope("finish"):
+        raw, left = lax.optimization_barrier((raw, left))
         away = lax.dynamic_index_in_dim(raw, 1 - zh, 0, keepdims=False)
         stay = lax.dynamic_index_in_dim(raw, zh, 0, keepdims=False)
         total = stay + swap(away, "zh")
         beside = lax.ppermute(total, "x", [(0, 1), (1, 0), (2, 3), (3, 2)])
-        pair = jnp.where(
-            x_low == 0, jnp.concatenate([total, beside], axis=1), jnp.concatenate([beside, total], axis=1)
-        )
-        update = apply_roots(where, pair, swap(pair, "c"), left, output_roots, last_root)
+        pieces = (total, beside, swap(total, "c"), swap(beside, "c"))
+        update = apply_roots(where, pieces, left, output_roots, last_root)
     return update, kept
 
 

time: 233 us -> 210 us (0.901)
  the two profiles are of different devices: /device:TPU:32 before, /device:TPU:65 now
where the time goes in v2:
time: 210 us; the launch traced here: 209 us
  blocking collectives  87.8 us (42%)
  Pallas kernels  40.8 us (19%)
  waiting for transfers between devices  38.7 us (18%)
  between operations  19.4 us (9%)
  starting transfers between devices  11 us (5%)
  local copies, waits for them, and re-layouts  8.06 us (4%)
  other arithmetic  3.4 us (2%)
    all_to_all x1, blocking collectives, per_device(): lax.all_to_all(mine.reshape(16 * 96, BS), ('y', 'x'), 0, 0, tiled=True)  39.7 us
    ppermute x8, waiting for transfers between devices, swap(): return lax.ppermute(value, axis, [(0, 1), (1, 0)])  30.9 us
    all_to_all x1, blocking collectives, per_device(): lax.all_to_all(mine, ('zh', 'y'), 0, 0, tiled=True).reshape(2, 4, 96, BS)  30.3 us
    pallas_call x1, Pallas kernels, two_roots(): pl.pallas_call(root_kernel, grid_spec=pltpu.PrefetchScalarGridSpec(num_sc...  21.2 us
    all_to_all x1, blocking collectives, per_device(): four = lax.all_to_all(four, 'x', 0, 0, tiled=True).reshape(4, BS, BS)  17.9 us
    pallas_call x1, Pallas kernels, product(): pl.pallas_call(product_kernel, grid_spec=pltpu.PrefetchScalarGridSpec(num...  12.6 us
    ppermute x8, starting transfers between devices, swap(): return lax.ppermute(value, axis, [(0, 1), (1, 0)])  7.94 us
    ppermute x3, waiting for transfers between devices, per_device(): got = got + lax.ppermute(left, ('zh', 'y', 'mp'), pairs)  7.61 us
  transfers between devices with their start and end apart: 13, of which 8 were waited for; matrix products, arithmetic and copies ran while one was open for 2% of the time, Pallas kernels for 12%

profile of v2, /device:TPU:65, one launch (start us, length us, event | category | flops | bytes accessed | tf_op | source)
XLA Modules:
  0.0 209.2 jit_solution(3617174399461767120)
XLA Ops:
  7.2 0.8 collective-permute-start
  8.0 1.1 constant_dynamic-slice_fusion
  9.4 6.3 %collective-permute-done.1.grads_other = bf16[512,640]{1,0:T(8,128)(2,1)S(1)} collective-permute-done((bf16[512,640]{1,0:T(8,128)(2,1)S(1)}, bf16[512,640]{1,0:T(8,128)(2,1)S(1)}, u32[]{:S(2)}, u32[]{:S(2)}) %collective-permute-start.1) | collective-permute-done | bytes 655392 | tf_op jit(solution)/shard_map/exchange/ppermute | solution.py:205
  15.7 2.2 %copy-done = bf16[512,4096]{1,0:T(8,128)(2,1)S(1)} copy-done((bf16[512,4096]{1,0:T(8,128)(2,1)S(1)}, bf16[512,4096]{1,0:T(8,128)(2,1)}, u32[]{:S(2)}) %copy-start) | copy-done | bytes 4194328
  17.9 12.6 %product.1 = f32[4,2,2,2,128,640]{5,4,3,2,1,0:T(8,128)} custom-call(s32[3]{0:T(128)S(1)} %pad_add_fusion.where_ref, bf16[512,4096]{1,0:T(8,128)(2,1)S(1)} %copy-done, bf16[512,4096]{1,0:T(8,128)(2,1)S(1)} %copy-done, bf16[512,4096]{1,0:T(8,128)(2,1)} %collective-permute-done.low_other.high_other, ...), custom_call_target="tpu_custom_call" | custom-call | flops 5368709120 | bytes 20971520 | tf_op jit(solution)/shard_map/product/pallas_call | solution.py:83
  30.5 2.2 %copy-done.1 = bf16[512,4096]{1,0:T(8,128)(2,1)S(1)} copy-done((bf16[512,4096]{1,0:T(8,128)(2,1)S(1)}, bf16[512,4096]{1,0:T(8,128)(2,1)}, u32[]{:S(2)}) %copy-start.1) | copy-done | bytes 4194328
  32.7 3.6 %factors.1 = f32[2,4,4,96,256]{4,3,2,1,0:T(8,128)S(1)} custom-call(s32[3]{0:T(128)S(1)} %pad_add_fusion.where_ref, bf16[512,4096]{1,0:T(8,128)(2,1)S(1)} %copy-done.1, bf16[512,1280]{1,0:T(8,128)(2,1)S(1)} %copy-done.2), custom_call_target="tpu_custom_call" | custom-call | flops 603979776 | bytes 6291456 | tf_op jit(solution)/shard_map/factors/pallas_call | solution.py:55
  36.9 3.0 %collective-permute-done.2 = f32[4,4,96,256]{3,2,1,0:T(8,128)S(1)} collective-permute-done((f32[4,4,96,256]{3,2,1,0:T(8,128)S(1)}, f32[4,4,96,256]{3,2,1,0:T(8,128)S(1)}, u32[]{:S(2)}, u32[]{:S(2)}) %collective-permute-start.2) | collective-permute-done | bytes 1572896 | tf_op jit(solution)/shard_map/factors/ppermute | solution.py:205
  40.2 39.7 %all_to_all.21 = f32[16,96,256]{2,1,0:T(8,128)S(1)} all-to-all(f32[16,96,256]{2,1,0:T(8,128)S(1)} %bitcast.40), channel_id=1, replica_groups=mesh['zh'=2,'y'=4,'x'=4,'c'=2,'mp'=4] {'y','x'}, dimensions={0} | all-to-all | bytes 3145728 | tf_op jit(solution)/shard_map/sum_factors/all_to_all | solution.py:230
  80.0 30.3 %all_to_all.22 = f32[8,96,256]{2,1,0:T(8,128)S(1)} all-to-all(f32[8,96,256]{2,1,0:T(8,128)S(1)} %broadcast_in_dim.14), channel_id=1, replica_groups=mesh['zh'=2,'y'=4,'x'=4,'c'=2,'mp'=4] {'zh','y'}, dimensions={0} | all-to-all | bytes 1572864 | tf_op jit(solution)/shard_map/sum_factors/all_to_all | solution.py:233
  110.4 1.8 collective-permute-start.3
  112.2 1.0 collective-permute-done.3.other_ref
  113.2 21.2 %roots.1 = bf16[2,256,256]{2,1,0:T(8,128)(2,1)S(1)} custom-call(s32[3]{0:T(128)S(1)} %pad_add_fusion.where_ref, f32[256,256]{1,0:T(8,128)S(1)} %bitcast.36, f32[128,256]{1,0:T(8,128)S(1)} %bitcast.38, f32[128,256]{1,0:T(8,128)S(1)} %collective-permute-done.3.other_ref), custom_call_target="tpu_custom_call" | custom-call | flops 14495514624 | bytes 1048576 | tf_op jit(solution)/shard_map/roots/pallas_call | solution.py:137
  134.4 17.9 %all_to_all.23 = bf16[4,256,256]{2,1,0:T(8,128)(2,1)S(1)} all-to-all(bf16[4,256,256]{2,1,0:T(8,128)(2,1)S(1)} %broadcast_in_dim.15), channel_id=1, replica_groups=mesh['zh'=2,'y'=4,'x'=4,'c'=2,'mp'=4] {'x'}, dimensions={0} | all-to-all | bytes 1048576 | tf_op jit(solution)/shard_map/roots/all_to_all | solution.py:242
  152.3 1.5 collective-permute-start.4
  153.8 1.5 collective-permute-done.4
  156.8 1.3 collective-permute-start.6
  158.3 7.6 %collective-permute-done.6 = bf16[256,256]{1,0:T(8,128)(2,1)S(1)} collective-permute-done((bf16[256,256]{1,0:T(8,128)(2,1)S(1)}, bf16[256,256]{1,0:T(8,128)(2,1)S(1)}, u32[]{:S(2)}, u32[]{:S(2)}) %collective-permute-start.6) | collective-permute-done | bytes 131104 | tf_op jit(solution)/shard_map/left_root/ppermute | solution.py:257
  165.9 1.0 dynamic-slice_bitcast_fusion
  167.7 18.7 %collective-permute-done.8 = f32[128,640]{1,0:T(8,128)S(1)} collective-permute-done((f32[128,640]{1,0:T(8,128)S(1)}, f32[128,640]{1,0:T(8,128)S(1)}, u32[]{:S(2)}, u32[]{:S(2)}) %collective-permute-start.8) | collective-permute-done | bytes 327712 | tf_op jit(solution)/shard_map/finish/ppermute | solution.py:205
  186.4 1.0 bitcast_add_fusion.mine_ref
  194.3 1.4 collective-permute-start.10
  195.9 1.7 collective-permute-start.11
  198.9 3.5 %finish.1 = bf16[64,1280]{1,0:T(8,128)(2,1)} custom-call(s32[3]{0:T(128)S(1)} %pad_add_fusion.where_ref, f32[128,640]{1,0:T(8,128)S(1)} %bitcast_add_fusion.mine_ref, f32[128,640]{1,0:T(8,128)S(1)} %collective-permute-done.9.beside_ref, f32[128,640]{1,0:T(8,128)S(1)} %collective-permute-done.10.mine_other, ...), custom_call_target="tpu_custom_call" | custom-call | flops 1006632960 | bytes 3145728 | tf_op jit(solution)/shard_map/finish/pallas_call | solution.py:181
  (44 shorter events, 7.0 us)
Async XLA Ops:
  7.2 8.5 %copy-start.2 = (bf16[512,1280]{1,0:T(8,128)(2,1)S(1)}, bf16[512,1280]{1,0:T(8,128)(2,1)}, u32[]{:S(2)}) copy-start(bf16[512,1280]{1,0:T(8,128)(2,1)} %grads_ref.3) | copy-start | bytes 3932164
  7.2 158.8 %reduce-scatter.2.cloned.1.call-start = ((), (), s32[]{:S(2)}) async-start(), calls=%async_computation.4 | async-start | bytes 11141120 | tf_op jit(solution)/shard_map/product/reduce_scatter | solution.py:226
  7.2 8.5 %collective-permute-start = (bf16[512,4096]{1,0:T(8,128)(2,1)}, bf16[512,4096]{1,0:T(8,128)(2,1)}, u32[]{:S(2)}, u32[]{:S(2)}) collective-permute-start(bf16[512,4096]{1,0:T(8,128)(2,1)} %acts_ref.1), channel_id=1, source_target_pairs={{0,4},{4,0},{1,5},{5,1},{2,6},{6,2},{3,7},{7,3},{8,12},{12,8},{9,1... | collective-permute-start | bytes 12582920 | tf_op jit(solution)/shard_map/exchange/ppermute | solution.py:205
  9.1 6.6 %collective-permute-start.1 = (bf16[512,640]{1,0:T(8,128)(2,1)S(1)}, bf16[512,640]{1,0:T(8,128)(2,1)S(1)}, u32[]{:S(2)}, u32[]{:S(2)}) collective-permute-start(bf16[512,640]{1,0:T(8,128)(2,1)S(1)} %constant_dynamic-slice_fusion), channel_id=1, source_target_pairs={{0,4},{4,0},{1,5},{5,1},{2,6},{6,2},{3,7},{7,3},{8,12},{12,8},{9,1... | collective-permute-start | bytes 1966088 | tf_op jit(solution)/shard_map/exchange/ppermute | solution.py:205
  15.7 2.2 %copy-start = (bf16[512,4096]{1,0:T(8,128)(2,1)S(1)}, bf16[512,4096]{1,0:T(8,128)(2,1)}, u32[]{:S(2)}) copy-start(bf16[512,4096]{1,0:T(8,128)(2,1)} %acts_ref.1) | copy-start | bytes 12582916
  30.5 2.2 %copy-start.1 = (bf16[512,4096]{1,0:T(8,128)(2,1)S(1)}, bf16[512,4096]{1,0:T(8,128)(2,1)}, u32[]{:S(2)}) copy-start(bf16[512,4096]{1,0:T(8,128)(2,1)} %acts_ref.1) | copy-start | bytes 12582916
  36.4 3.5 %collective-permute-start.2 = (f32[4,4,96,256]{3,2,1,0:T(8,128)S(1)}, f32[4,4,96,256]{3,2,1,0:T(8,128)S(1)}, u32[]{:S(2)}, u32[]{:S(2)}) collective-permute-start(f32[4,4,96,256]{3,2,1,0:T(8,128)S(1)} %slice_bitcast_fusion), channel_id=1, source_target_pairs={{0,4},{4,0},{1,5},{5,1},{2,6},{6,2},{3,7},{7,3},{8,12},{12,8},{9,1... | collective-permute-start | bytes 4718600 | tf_op jit(solution)/shard_map/factors/ppermute | solution.py:205
  110.4 2.8 %collective-permute-start.3 = (f32[128,256]{1,0:T(8,128)S(1)}, f32[128,256]{1,0:T(8,128)S(1)}, u32[]{:S(2)}, u32[]{:S(2)}) collective-permute-start(f32[128,256]{1,0:T(8,128)S(1)} %bitcast.37), channel_id=1, source_target_pairs={{0,4},{4,0},{1,5},{5,1},{2,6},{6,2},{3,7},{7,3},{8,12},{12,8},{9,1... | collective-permute-start | bytes 393224 | tf_op jit(solution)/shard_map/roots/ppermute | solution.py:205
  134.4 23.6 %copy-start.3 = (s32[1,9]{1,0:T(1,128)S(1)}, s32[1,9]{1,0:T(1,128)}, u32[]{:S(2)}) copy-start(s32[1,9]{1,0:T(1,128)} %param.5) | copy-start | bytes 112
  152.3 3.0 %collective-permute-start.4 = (bf16[4,256,256]{2,1,0:T(8,128)(2,1)S(1)}, bf16[4,256,256]{2,1,0:T(8,128)(2,1)S(1)}, u32[]{:S(2)}, u32[]{:S(2)}) collective-permute-start(bf16[4,256,256]{2,1,0:T(8,128)(2,1)S(1)} %all_to_all.23), channel_id=1, source_target_pairs={{0,4},{4,0},{1,5},{5,1},{2,6},{6,2},{3,7},{7,3},{8,12},{12,8},{9,1... | collective-permute-start | bytes 1572872 | tf_op jit(solution)/shard_map/roots/ppermute | solution.py:205
  155.4 2.9 %collective-permute-start.7 = (bf16[256,256]{1,0:T(8,128)(2,1)S(1)}, bf16[256,256]{1,0:T(8,128)(2,1)S(1)}, u32[]{:S(2)}, u32[]{:S(2)}) collective-permute-start(bf16[256,256]{1,0:T(8,128)(2,1)S(1)} %dynamic-slice_bitcast_fusion.1), channel_id=1, source_target_pairs={{0,3},{32,35},{65,64},{97,96},{130,129},{162,161},{195,194},{227,2... | collective-permute-start | bytes 393224 | tf_op jit(solution)/shard_map/left_root/ppermute | solution.py:257
  156.1 2.2 %collective-permute-start.5 = (bf16[256,256]{1,0:T(8,128)(2,1)S(1)}, bf16[256,256]{1,0:T(8,128)(2,1)S(1)}, u32[]{:S(2)}, u32[]{:S(2)}) collective-permute-start(bf16[256,256]{1,0:T(8,128)(2,1)S(1)} %dynamic-slice_bitcast_fusion.1), channel_id=1, source_target_pairs={{0,1},{32,33},{65,66},{97,98},{130,131},{162,163},{195,192},{227,2... | collective-permute-start | bytes 393224 | tf_op jit(solution)/shard_map/left_root/ppermute | solution.py:257
  156.8 9.1 %collective-permute-start.6 = (bf16[256,256]{1,0:T(8,128)(2,1)S(1)}, bf16[256,256]{1,0:T(8,128)(2,1)S(1)}, u32[]{:S(2)}, u32[]{:S(2)}) collective-permute-start(bf16[256,256]{1,0:T(8,128)(2,1)S(1)} %dynamic-slice_bitcast_fusion.1), channel_id=1, source_target_pairs={{0,2},{32,34},{65,67},{97,99},{130,128},{162,160},{195,193},{227,2... | collective-permute-start | bytes 393224 | tf_op jit(solution)/shard_map/left_root/ppermute | solution.py:257
  166.9 19.5 %collective-permute-start.8 = (f32[128,640]{1,0:T(8,128)S(1)}, f32[128,640]{1,0:T(8,128)S(1)}, u32[]{:S(2)}, u32[]{:S(2)}) collective-permute-start(f32[128,640]{1,0:T(8,128)S(1)} %dynamic-slice_bitcast_fusion), channel_id=1, source_target_pairs={{0,128},{128,0},{1,129},{129,1},{2,130},{130,2},{3,131},{131,3},{4... | collective-permute-start | bytes 983048 | tf_op jit(solution)/shard_map/finish/ppermute | solution.py:205
  187.4 8.5 %collective-permute-start.9 = (f32[128,640]{1,0:T(8,128)S(1)}, f32[128,640]{1,0:T(8,128)S(1)}, u32[]{:S(2)}, u32[]{:S(2)}) collective-permute-start(f32[128,640]{1,0:T(8,128)S(1)} %bitcast_add_fusion.mine_ref), channel_id=1, source_target_pairs={{0,8},{8,0},{16,24},{24,16},{1,9},{9,1},{17,25},{25,17},{2,10},{10... | collective-permute-start | bytes 983048 | tf_op jit(solution)/shard_map/finish/ppermute | solution.py:281
  194.3 4.3 %collective-permute-start.10 = (f32[128,640]{1,0:T(8,128)S(1)}, f32[128,640]{1,0:T(8,128)S(1)}, u32[]{:S(2)}, u32[]{:S(2)}) collective-permute-start(f32[128,640]{1,0:T(8,128)S(1)} %bitcast_add_fusion.mine_ref), channel_id=1, source_target_pairs={{0,4},{4,0},{1,5},{5,1},{2,6},{6,2},{3,7},{7,3},{8,12},{12,8},{9,1... | collective-permute-start | bytes 983048 | tf_op jit(solution)/shard_map/finish/ppermute | solution.py:205
  195.9 3.0 %collective-permute-start.11 = (f32[128,640]{1,0:T(8,128)S(1)}, f32[128,640]{1,0:T(8,128)S(1)}, u32[]{:S(2)}, u32[]{:S(2)}) collective-permute-start(f32[128,640]{1,0:T(8,128)S(1)} %collective-permute-done.9.beside_ref), channel_id=1, source_target_pairs={{0,4},{4,0},{1,5},{5,1},{2,6},{6,2},{3,7},{7,3},{8,12},{12,8},{9,1... | collective-permute-start | bytes 983048 | tf_op jit(solution)/shard_map/finish/ppermute | solution.py:205
Sparse Core Ops, SparseCore 0:
  30.6 122.7 reduce-scatter.1

commit v3 on v2

--- a/solution.py
+++ b/solution.py
@@ -69,36 +69,36 @@
     )(where, acts, grads)
 
 
-def product_kernel(where_ref, low_ref, high_ref, low_other, high_other, grads_ref, grads_other, out_ref):
-    for zh, (mine, other) in enumerate(((low_ref, low_other), (high_ref, high_other))):
-        for xl in range(2):
-            cols = slice(xl * HALF, (xl + 1) * HALF)
-            out_ref[0, 0, xl, zh] = tdot(mine[:, cols], grads_ref[...]) + tdot(other[:, cols], grads_other[...])
-
-
-def product(where, acts, acts_other, grads, grads_other):
+def product_kernel(where_ref, a_mine, a_other, b_mine, b_other, grads_ref, grads_other, a_out, b_out):
+    a_out[0] = tdot(a_mine[...], grads_ref[...]) + tdot(a_other[...], grads_other[...])
+    b_out[0] = tdot(b_mine[...], grads_ref[...]) + tdot(b_other[...], grads_other[...])
+
+
+def product(where, shift, acts, acts_other, grads, grads_other):
     rows, width = grads_other.shape
-    low = pl.BlockSpec((rows, BS), lambda y, h, w: (0, y * 2 + h))
-    high = pl.BlockSpec((rows, BS), lambda y, h, w: (0, 8 + y * 2 + h))
+    first = pl.BlockSpec((rows, HALF), lambda j, w: (0, 4 * j + lax.rem(w[3] + shift, 4)))
+    second = pl.BlockSpec((rows, HALF), lambda j, w: (0, 16 + 4 * lax.rem(w[4] + shift, 4) + j))
+    out = pl.BlockSpec((1, HALF, width), lambda j, w: (j, 0, 0))
+    shape = jax.ShapeDtypeStruct((4, HALF, width), F32)
     return pl.pallas_call(
         product_kernel,
         grid_spec=pltpu.PrefetchScalarGridSpec(
             num_scalar_prefetch=1,
-            grid=(4, 2),
+            grid=(4,),
             in_specs=[
-                low,
-                high,
-                low,
-                high,
-                pl.BlockSpec((rows, width), lambda y, h, w: (0, w[1])),
-                pl.BlockSpec((rows, width), lambda y, h, w: (0, 0)),
+                first,
+                first,
+                second,
+                second,
+                pl.BlockSpec((rows, width), lambda j, w: (0, w[1])),
+                pl.BlockSpec((rows, width), lambda j, w: (0, 0)),
             ],
-            out_specs=pl.BlockSpec((1, 1, 2, 2, HALF, width), lambda y, h, w: (y, h, 0, 0, 0, 0)),
+            out_specs=[out, out],
         ),
-        out_shape=jax.ShapeDtypeStruct((4, 2, 2, 2, HALF, width), F32),
-        compiler_params=pltpu.CompilerParams(vmem_limit_bytes=40 * 2**20),
-        cost_estimate=pl.CostEstimate(flops=4 * rows * 4096 * width, bytes_accessed=20 * 2**20, transcendentals=0),
-    )(where, acts, acts, acts_other, acts_other, grads, grads_other)
+        out_shape=[shape, shape],
+        compiler_params=pltpu.CompilerParams(vmem_limit_bytes=24 * 2**20),
+        cost_estimate=pl.CostEstimate(flops=4 * rows * 1024 * width, bytes_accessed=6 * 2**20, transcendentals=0),
+    )(where, acts, acts_other, acts, acts_other, grads, grads_other)
 
 
 def root_kernel(where_ref, block_ref, mine_ref, other_ref, out_ref, last):
@@ -205,11 +205,25 @@
     return lax.ppermute(value, axis, [(0, 1), (1, 0)])
 
 
+def away(value, axis, shift):
+    if shift == 0:
+        return value
+    return lax.ppermute(value, axis, [(i, (i + shift) % 4) for i in range(4)])
+
+
+def across(value, axis, at):
+    parts = [
+        away(lax.dynamic_index_in_dim(value, lax.rem(at + shift, 4), 0, keepdims=False), axis, shift)
+        for shift in (2, 1, 3, 0)
+    ]
+    return (parts[3] + parts[0]) + (parts[1] + parts[2])
+
+
 def per_device(acts, grads, owners):
     zh, y, x, core, column = (lax.axis_index(a) for a in ("zh", "y", "x", "c", "mp"))
     x_high, x_low = x // 2, x % 2
     rows, width = grads.shape
-    where = jnp.stack([column, core, x_low]).astype(jnp.int32)
+    where = jnp.stack([column, core, x_low, x, y]).astype(jnp.int32)
 
     with jax.named_scope("exchange"):
         acts_other = swap(acts, "c")
@@ -221,10 +235,11 @@
         mine = parts[0] + swap(parts[1], "c")
 
     with jax.named_scope("product"):
-        raw = product(where, acts, acts_other, grads, grads_other)
-        raw = raw.reshape(16 * 2 * HALF, width // 2)
-        raw = lax.psum_scatter(raw, ("y", "x"), scatter_dimension=0, tiled=True)
-        raw = raw.reshape(2, HALF, width // 2)
+        first, second = [], []
+        for shift in (2, 1, 3, 0):
+            one, two = product(where, shift, acts, acts_other, grads, grads_other)
+            first.append(away(one, "x", shift))
+            second.append(away(two, "y", shift))
 
     with jax.named_scope("sum_factors"):
         mine = lax.all_to_all(mine.reshape(16 * 96, BS), ("y", "x"), 0, 0, tiled=True)
@@ -274,10 +289,10 @@
         )
 
     with jax.named_scope("finish"):
-        raw, left = lax.optimization_barrier((raw, left))
-        away = lax.dynamic_index_in_dim(raw, 1 - zh, 0, keepdims=False)
-        stay = lax.dynamic_index_in_dim(raw, zh, 0, keepdims=False)
-        total = stay + swap(away, "zh")
+        low = across((first[3] + first[0]) + (first[1] + first[2]), "y", y)
+        high = across((second[3] + second[0]) + (second[1] + second[2]), "x", x)
+        stay = jnp.where(zh == 0, low, high)
+        total = stay + swap(jnp.where(zh == 0, high, low), "zh")
         beside = lax.ppermute(total, "x", [(0, 1), (1, 0), (2, 3), (3, 2)])
         pieces = (total, beside, swap(total, "c"), swap(beside, "c"))
         update = apply_roots(where, pieces, left, output_roots, last_root)

time: 210 us -> 213 us (1.014)
  the two profiles are of different devices: /device:TPU:65 before, /device:TPU:32 now
where the time goes in v3:
time: 213 us; the launch traced here: 211 us
  waiting for transfers between devices  77.6 us (36%)
  Pallas kernels  49.6 us (23%)
  starting transfers between devices  49.1 us (23%)
  local copies, waits for them, and re-layouts  16.3 us (8%)
  other arithmetic  12.5 us (6%)
  between operations  5.76 us (3%)
    ppermute x12, waiting for transfers between devices, away(): return lax.ppermute(value, axis, [(i, (i + shift) % 4) for i in range(4)])  31.9 us
    all_to_all x1, waiting for transfers between devices, per_device(): lax.all_to_all(mine.reshape(16 * 96, BS), ('y', 'x'), 0, 0, tiled=True)  25.5 us
    pallas_call x4, Pallas kernels, product(): pl.pallas_call(product_kernel, grid_spec=pltpu.PrefetchScalarGridSpec(num...  21.3 us
    pallas_call x1, Pallas kernels, two_roots(): pl.pallas_call(root_kernel, grid_spec=pltpu.PrefetchScalarGridSpec(num_sc...  21.2 us
    ppermute x12, starting transfers between devices, away(): return lax.ppermute(value, axis, [(i, (i + shift) % 4) for i in range(4)])  19.7 us
    unnamed x20, local copies, waits for them, and re-layouts  11.1 us
    all_to_all x1, starting transfers between devices, per_device(): lax.all_to_all(mine, ('zh', 'y'), 0, 0, tiled=True).reshape(2, 4, 96, BS)  8.92 us
    all_to_all x1, starting transfers between devices, per_device(): lax.all_to_all(mine.reshape(16 * 96, BS), ('y', 'x'), 0, 0, tiled=True)  7.22 us
  transfers between devices with their start and end apart: 27, of which 11 were waited for; matrix products, arithmetic and copies ran while one was open for 8% of the time, Pallas kernels for 22%

profile of v3, /device:TPU:32, one launch (start us, length us, event | category | flops | bytes accessed | tf_op | source)
XLA Modules:
  0.0 210.7 jit_solution(8893841283798576424)
XLA Ops:
  4.3 3.6 %factors.1 = f32[2,4,4,96,256]{4,3,2,1,0:T(8,128)S(1)} custom-call(s32[5]{0:T(128)S(1)} %stack.28.where_ref, bf16[512,4096]{1,0:T(8,128)(2,1)S(1)} %copy-done, bf16[512,1280]{1,0:T(8,128)(2,1)S(1)} %copy-done.4), custom_call_target="tpu_custom_call" | custom-call | flops 603979776 | bytes 6291456 | tf_op jit(solution)/shard_map/factors/pallas_call | solution.py:55
  8.6 3.0 %collective-permute-done.18 = f32[4,4,96,256]{3,2,1,0:T(8,128)S(1)} collective-permute-done((f32[4,4,96,256]{3,2,1,0:T(8,128)S(1)}, f32[4,4,96,256]{3,2,1,0:T(8,128)S(1)}, u32[]{:S(2)}, u32[]{:S(2)}) %collective-permute-start.18) | collective-permute-done | bytes 1572896 | tf_op jit(solution)/shard_map/factors/ppermute | solution.py:205
  13.0 7.2 %all-to-all-start = ((f32[16,96,256]{2,1,0:T(8,128)}), f32[16,96,256]{2,1,0:T(8,128)}, u32[]{:S(2)}, u32[]{:S(2)}) async-start(f32[16,96,256]{2,1,0:T(8,128)} %bitcast.15), calls=%async_computation | async-start | bytes 3145728 | tf_op jit(solution)/shard_map/sum_factors/all_to_all | solution.py:245
  20.5 25.5 %all-to-all-done = f32[16,96,256]{2,1,0:T(8,128)} async-done(((f32[16,96,256]{2,1,0:T(8,128)}), f32[16,96,256]{2,1,0:T(8,128)}, u32[]{:S(2)}, u32[]{:S(2)}) %all-to-all-start) | async-done | bytes 1572896 | tf_op jit(solution)/shard_map/sum_factors/all_to_all | solution.py:245
  48.5 8.9 %all-to-all-start.1 = ((f32[8,96,256]{2,1,0:T(8,128)}), f32[8,96,256]{2,1,0:T(8,128)S(1)}, u32[]{:S(2)}, u32[]{:S(2)}) async-start(f32[8,96,256]{2,1,0:T(8,128)} %broadcast_in_dim.14), calls=%async_computation.1 | async-start | bytes 1572864 | tf_op jit(solution)/shard_map/sum_factors/all_to_all | solution.py:248
  59.6 5.5 %product.6 = (f32[4,128,640]{2,1,0:T(8,128)}, f32[4,128,640]{2,1,0:T(8,128)}) custom-call(s32[5]{0:T(128)S(1)} %stack.28.where_ref, bf16[512,4096]{1,0:T(8,128)(2,1)S(1)} %copy-done.1, bf16[512,4096]{1,0:T(8,128)(2,1)} %collective-permute-done.a_other.b_other, bf16[512,4096]{1,0:T(8,128)(2,1)S(1)} %copy-done.1, ...), custom_call_target="tpu_custom_call" | custom-call | flops 1342177280 | bytes 6291456 | tf_op jit(solution)/shard_map/product/pallas_call | solution.py:83
  67.7 5.5 %product.7 = (f32[4,128,640]{2,1,0:T(8,128)}, f32[4,128,640]{2,1,0:T(8,128)}) custom-call(s32[5]{0:T(128)S(1)} %stack.28.where_ref, bf16[512,4096]{1,0:T(8,128)(2,1)S(1)} %copy-done.2, bf16[512,4096]{1,0:T(8,128)(2,1)} %collective-permute-done.a_other.b_other, bf16[512,4096]{1,0:T(8,128)(2,1)S(1)} %copy-done.2, ...), custom_call_target="tpu_custom_call" | custom-call | flops 1342177280 | bytes 6291456 | tf_op jit(solution)/shard_map/product/pallas_call | solution.py:83
  73.2 3.2 %collective-permute-start.4 = (f32[4,128,640]{2,1,0:T(8,128)}, f32[4,128,640]{2,1,0:T(8,128)}, u32[]{:S(2)}, u32[]{:S(2)}) collective-permute-start(f32[4,128,640]{2,1,0:T(8,128)} %get-tuple-element.14), channel_id=1, source_target_pairs={{0,24},{8,0},{16,8},{24,16},{1,25},{9,1},{17,9},{25,17},{2,26},{10... | collective-permute-start | bytes 3932168 | tf_op jit(solution)/shard_map/product/ppermute | solution.py:211
  76.4 4.6 %all-to-all-done.1 = f32[8,96,256]{2,1,0:T(8,128)S(1)} async-done(((f32[8,96,256]{2,1,0:T(8,128)}), f32[8,96,256]{2,1,0:T(8,128)S(1)}, u32[]{:S(2)}, u32[]{:S(2)}) %all-to-all-start.1) | async-done | bytes 786464 | tf_op jit(solution)/shard_map/sum_factors/all_to_all | solution.py:248
  83.4 5.5 %product.5 = (f32[4,128,640]{2,1,0:T(8,128)}, f32[4,128,640]{2,1,0:T(8,128)}) custom-call(s32[5]{0:T(128)S(1)} %stack.28.where_ref, bf16[512,4096]{1,0:T(8,128)(2,1)S(1)} %copy-done.3, bf16[512,4096]{1,0:T(8,128)(2,1)} %collective-permute-done.a_other.b_other, bf16[512,4096]{1,0:T(8,128)(2,1)S(1)} %copy-done.3, ...), custom_call_target="tpu_custom_call" | custom-call | flops 1342177280 | bytes 6291456 | tf_op jit(solution)/shard_map/product/pallas_call | solution.py:83
  90.6 4.7 %product.4 = (f32[4,128,640]{2,1,0:T(8,128)S(1)}, f32[4,128,640]{2,1,0:T(8,128)S(1)}) custom-call(s32[5]{0:T(128)S(1)} %stack.28.where_ref, bf16[512,4096]{1,0:T(8,128)(2,1)S(1)} %copy-done.3, bf16[512,4096]{1,0:T(8,128)(2,1)} %collective-permute-done.a_other.b_other, bf16[512,4096]{1,0:T(8,128)(2,1)S(1)} %copy-done.3, ...), custom_call_target="tpu_custom_call" | custom-call | flops 1342177280 | bytes 6291456 | tf_op jit(solution)/shard_map/product/pallas_call | solution.py:83
  96.4 2.9 %collective-permute-start.10 = (f32[4,128,640]{2,1,0:T(8,128)}, f32[4,128,640]{2,1,0:T(8,128)}, u32[]{:S(2)}, u32[]{:S(2)}) collective-permute-start(f32[4,128,640]{2,1,0:T(8,128)} %get-tuple-element.18), channel_id=1, source_target_pairs={{0,96},{32,0},{64,32},{96,64},{1,97},{33,1},{65,33},{97,65},{2,98}... | collective-permute-start | bytes 3932168 | tf_op jit(solution)/shard_map/product/ppermute | solution.py:211
  99.3 25.1 %collective-permute-done.3 = f32[4,128,640]{2,1,0:T(8,128)} collective-permute-done((f32[4,128,640]{2,1,0:T(8,128)}, f32[4,128,640]{2,1,0:T(8,128)}, u32[]{:S(2)}, u32[]{:S(2)}) %collective-permute-start.3) | collective-permute-done | bytes 1310752 | tf_op jit(solution)/shard_map/product/ppermute | solution.py:211
  124.4 3.2 %collective-permute-start.8 = (f32[4,128,640]{2,1,0:T(8,128)}, f32[4,128,640]{2,1,0:T(8,128)}, u32[]{:S(2)}, u32[]{:S(2)}) collective-permute-start(f32[4,128,640]{2,1,0:T(8,128)} %get-tuple-element.16), channel_id=1, source_target_pairs={{0,64},{32,96},{64,0},{96,32},{1,65},{33,97},{65,1},{97,33},{2,66}... | collective-permute-start | bytes 3932168 | tf_op jit(solution)/shard_map/product/ppermute | solution.py:211
  127.7 21.2 %roots.1 = bf16[2,256,256]{2,1,0:T(8,128)(2,1)S(1)} custom-call(s32[5]{0:T(128)S(1)} %stack.28.where_ref, f32[256,256]{1,0:T(8,128)S(1)} %bitcast.54, f32[128,256]{1,0:T(8,128)S(1)} %bitcast.56, f32[128,256]{1,0:T(8,128)S(1)} %collective-permute-done.19.other_ref), custom_call_target="tpu_custom_call" | custom-call | flops 14495514624 | bytes 1048576 | tf_op jit(solution)/shard_map/roots/pallas_call | solution.py:137
  149.7 3.5 %all-to-all-start.2 = ((bf16[4,256,256]{2,1,0:T(8,128)(2,1)}), bf16[4,256,256]{2,1,0:T(8,128)(2,1)S(1)}, u32[]{:S(2)}, u32[]{:S(2)}) async-start(bf16[4,256,256]{2,1,0:T(8,128)(2,1)} %broadcast_in_dim.15), calls=%async_computation.2 | async-start | bytes 1048576 | tf_op jit(solution)/shard_map/roots/all_to_all | solution.py:257
  153.3 2.5 %add_add_fusion.1 = f32[4,128,640]{2,1,0:T(8,128)S(1)} fusion(f32[4,128,640]{2,1,0:T(8,128)} %collective-permute-done.3, f32[4,128,640]{2,1,0:T(8,128)} %collective-permute-done.4, f32[4,128,640]{2,1,0:T(8,128)S(1)} %copy-done.7, f32[4,128,640]{2,1,0:T(8,128)} %collective-permute-done.2), kind=kLoop, calls=%fused_computation.4 | loop fusion | flops 983040 | bytes 6553600 | tf_op jit(solution)/shard_map/finish/add | solution.py:292
  157.3 2.7 %collective-permute-start.7 = (f32[128,640]{1,0:T(8,128)}, f32[128,640]{1,0:T(8,128)}, u32[]{:S(2)}, u32[]{:S(2)}) collective-permute-start(f32[128,640]{1,0:T(8,128)} %get-tuple-element.27), channel_id=1, source_target_pairs={{0,96},{32,0},{64,32},{96,64},{1,97},{33,1},{65,33},{97,65},{2,98}... | collective-permute-start | bytes 983048 | tf_op jit(solution)/shard_map/finish/ppermute | solution.py:211
  160.0 2.5 %add_add_fusion = f32[4,128,640]{2,1,0:T(8,128)S(1)} fusion(f32[4,128,640]{2,1,0:T(8,128)} %collective-permute-done.9, f32[4,128,640]{2,1,0:T(8,128)} %collective-permute-done.10, f32[4,128,640]{2,1,0:T(8,128)S(1)} %get-tuple-element.15, f32[4,128,640]{2,1,0:T(8,128)} %collective-permute-done.8), kind=kLoop, calls=%fused_computation.3 | loop fusion | flops 983040 | bytes 6553600 | tf_op jit(solution)/shard_map/finish/add | solution.py:293
  172.5 4.4 %collective-permute-done.11 = f32[128,640]{1,0:T(8,128)} collective-permute-done((f32[128,640]{1,0:T(8,128)S(1)}, f32[128,640]{1,0:T(8,128)}, u32[]{:S(2)}, u32[]{:S(2)}) %collective-permute-start.11) | collective-permute-done | bytes 327712 | tf_op jit(solution)/shard_map/finish/ppermute | solution.py:211
  179.3 5.4 %collective-permute-start.14 = (f32[128,640]{1,0:T(8,128)}, f32[128,640]{1,0:T(8,128)S(1)}, u32[]{:S(2)}, u32[]{:S(2)}) collective-permute-start(f32[128,640]{1,0:T(8,128)} %get-tuple-element.20), channel_id=1, source_target_pairs={{0,128},{128,0},{1,129},{129,1},{2,130},{130,2},{3,131},{131,3},{4... | collective-permute-start | bytes 983048 | tf_op jit(solution)/shard_map/finish/ppermute | solution.py:205
  196.0 3.5 %collective-permute-done.15.beside_ref = f32[128,640]{1,0:T(8,128)S(1)} collective-permute-done((f32[128,640]{1,0:T(8,128)S(1)}, f32[128,640]{1,0:T(8,128)S(1)}, u32[]{:S(2)}, u32[]{:S(2)}) %collective-permute-start.15) | collective-permute-done | bytes 327712 | tf_op jit(solution)/shard_map/finish/ppermute | solution.py:296
  200.2 7.0 %collective-permute-done.21 = bf16[256,256]{1,0:T(8,128)(2,1)S(1)} collective-permute-done((bf16[256,256]{1,0:T(8,128)(2,1)S(1)}, bf16[256,256]{1,0:T(8,128)(2,1)S(1)}, u32[]{:S(2)}, u32[]{:S(2)}) %collective-permute-start.21) | collective-permute-done | bytes 131104 | tf_op jit(solution)/shard_map/left_root/ppermute | solution.py:272
  207.2 3.5 %finish.1 = bf16[64,1280]{1,0:T(8,128)(2,1)} custom-call(s32[5]{0:T(128)S(1)} %stack.28.where_ref, f32[128,640]{1,0:T(8,128)S(1)} %select_add_fusion.mine_ref, f32[128,640]{1,0:T(8,128)S(1)} %collective-permute-done.15.beside_ref, f32[128,640]{1,0:T(8,128)S(1)} %collective-permute-done.16.mine_other, f32[128,640]{1,0:T(8,128)S(1)} %collective-permute-done.17.beside_other, ...), custom_call_target="tpu_custom_call" | custom-call | flops 1006632960 | bytes 3145728 | tf_op jit(solution)/shard_map/finish/pallas_call | solution.py:181
  (87 shorter events, 40.3 us)
Async XLA Ops:
  0.6 56.8 %collective-permute-start = (bf16[512,4096]{1,0:T(8,128)(2,1)}, bf16[512,4096]{1,0:T(8,128)(2,1)}, u32[]{:S(2)}, u32[]{:S(2)}) collective-permute-start(bf16[512,4096]{1,0:T(8,128)(2,1)} %acts_ref.1), channel_id=1, source_target_pairs={{0,4},{4,0},{1,5},{5,1},{2,6},{6,2},{3,7},{7,3},{8,12},{12,8},{9,1... | collective-permute-start | bytes 12582920 | tf_op jit(solution)/shard_map/exchange/ppermute | solution.py:205
  13.0 33.0 %all-to-all-start = ((f32[16,96,256]{2,1,0:T(8,128)}), f32[16,96,256]{2,1,0:T(8,128)}, u32[]{:S(2)}, u32[]{:S(2)}) async-start(f32[16,96,256]{2,1,0:T(8,128)} %bitcast.15), calls=%async_computation | async-start | bytes 3145728 | tf_op jit(solution)/shard_map/sum_factors/all_to_all | solution.py:245
  20.4 37.1 %collective-permute-start.1 = (bf16[512,640]{1,0:T(8,128)(2,1)S(1)}, bf16[512,640]{1,0:T(8,128)(2,1)S(1)}, u32[]{:S(2)}, u32[]{:S(2)}) collective-permute-start(bf16[512,640]{1,0:T(8,128)(2,1)S(1)} %constant_dynamic-slice_fusion), channel_id=1, source_target_pairs={{0,4},{4,0},{1,5},{5,1},{2,6},{6,2},{3,7},{7,3},{8,12},{12,8},{9,1... | collective-permute-start | bytes 1966088 | tf_op jit(solution)/shard_map/exchange/ppermute | solution.py:205
  48.5 32.5 %all-to-all-start.1 = ((f32[8,96,256]{2,1,0:T(8,128)}), f32[8,96,256]{2,1,0:T(8,128)S(1)}, u32[]{:S(2)}, u32[]{:S(2)}) async-start(f32[8,96,256]{2,1,0:T(8,128)} %broadcast_in_dim.14), calls=%async_computation.1 | async-start | bytes 1572864 | tf_op jit(solution)/shard_map/sum_factors/all_to_all | solution.py:248
  65.2 59.3 %collective-permute-start.3 = (f32[4,128,640]{2,1,0:T(8,128)}, f32[4,128,640]{2,1,0:T(8,128)}, u32[]{:S(2)}, u32[]{:S(2)}) collective-permute-start(f32[4,128,640]{2,1,0:T(8,128)} %get-tuple-element.13), channel_id=1, source_target_pairs={{0,8},{8,16},{16,24},{24,0},{1,9},{9,17},{17,25},{25,1},{2,10},{10... | collective-permute-start | bytes 3932168 | tf_op jit(solution)/shard_map/product/ppermute | solution.py:211
  73.2 80.0 %collective-permute-start.4 = (f32[4,128,640]{2,1,0:T(8,128)}, f32[4,128,640]{2,1,0:T(8,128)}, u32[]{:S(2)}, u32[]{:S(2)}) collective-permute-start(f32[4,128,640]{2,1,0:T(8,128)} %get-tuple-element.14), channel_id=1, source_target_pairs={{0,24},{8,0},{16,8},{24,16},{1,25},{9,1},{17,9},{25,17},{2,26},{10... | collective-permute-start | bytes 3932168 | tf_op jit(solution)/shard_map/product/ppermute | solution.py:211
  81.1 15.3 %collective-permute-start.19 = (f32[128,256]{1,0:T(8,128)S(1)}, f32[128,256]{1,0:T(8,128)S(1)}, u32[]{:S(2)}, u32[]{:S(2)}) collective-permute-start(f32[128,256]{1,0:T(8,128)S(1)} %bitcast.55), channel_id=1, source_target_pairs={{0,4},{4,0},{1,5},{5,1},{2,6},{6,2},{3,7},{7,3},{8,12},{12,8},{9,1... | collective-permute-start | bytes 393224 | tf_op jit(solution)/shard_map/roots/ppermute | solution.py:205
  88.9 64.3 %collective-permute-start.2 = (f32[4,128,640]{2,1,0:T(8,128)}, f32[4,128,640]{2,1,0:T(8,128)}, u32[]{:S(2)}, u32[]{:S(2)}) collective-permute-start(f32[4,128,640]{2,1,0:T(8,128)} %get-tuple-element.12), channel_id=1, source_target_pairs={{0,16},{8,24},{16,0},{24,8},{1,17},{9,25},{17,1},{25,9},{2,18},{10... | collective-permute-start | bytes 3932168 | tf_op jit(solution)/shard_map/product/ppermute | solution.py:211
  90.1 69.9 %collective-permute-start.9 = (f32[4,128,640]{2,1,0:T(8,128)}, f32[4,128,640]{2,1,0:T(8,128)}, u32[]{:S(2)}, u32[]{:S(2)}) collective-permute-start(f32[4,128,640]{2,1,0:T(8,128)} %get-tuple-element.17), channel_id=1, source_target_pairs={{0,32},{32,64},{64,96},{96,0},{1,33},{33,65},{65,97},{97,1},{2,34}... | collective-permute-start | bytes 3932168 | tf_op jit(solution)/shard_map/product/ppermute | solution.py:211
  96.4 63.6 %collective-permute-start.10 = (f32[4,128,640]{2,1,0:T(8,128)}, f32[4,128,640]{2,1,0:T(8,128)}, u32[]{:S(2)}, u32[]{:S(2)}) collective-permute-start(f32[4,128,640]{2,1,0:T(8,128)} %get-tuple-element.18), channel_id=1, source_target_pairs={{0,96},{32,0},{64,32},{96,64},{1,97},{33,1},{65,33},{97,65},{2,98}... | collective-permute-start | bytes 3932168 | tf_op jit(solution)/shard_map/product/ppermute | solution.py:211
  124.4 35.6 %collective-permute-start.8 = (f32[4,128,640]{2,1,0:T(8,128)}, f32[4,128,640]{2,1,0:T(8,128)}, u32[]{:S(2)}, u32[]{:S(2)}) collective-permute-start(f32[4,128,640]{2,1,0:T(8,128)} %get-tuple-element.16), channel_id=1, source_target_pairs={{0,64},{32,96},{64,0},{96,32},{1,65},{33,97},{65,1},{97,33},{2,66}... | collective-permute-start | bytes 3932168 | tf_op jit(solution)/shard_map/product/ppermute | solution.py:211
  149.7 19.8 %all-to-all-start.2 = ((bf16[4,256,256]{2,1,0:T(8,128)(2,1)}), bf16[4,256,256]{2,1,0:T(8,128)(2,1)S(1)}, u32[]{:S(2)}, u32[]{:S(2)}) async-start(bf16[4,256,256]{2,1,0:T(8,128)(2,1)} %broadcast_in_dim.15), calls=%async_computation.2 | async-start | bytes 1048576 | tf_op jit(solution)/shard_map/roots/all_to_all | solution.py:257
  156.7 9.8 %collective-permute-start.6 = (f32[128,640]{1,0:T(8,128)S(1)}, f32[128,640]{1,0:T(8,128)}, u32[]{:S(2)}, u32[]{:S(2)}) collective-permute-start(f32[128,640]{1,0:T(8,128)S(1)} %get-tuple-element.28), channel_id=1, source_target_pairs={{0,32},{32,64},{64,96},{96,0},{1,33},{33,65},{65,97},{97,1},{2,34}... | collective-permute-start | bytes 983048 | tf_op jit(solution)/shard_map/finish/ppermute | solution.py:211
  157.3 12.6 %collective-permute-start.7 = (f32[128,640]{1,0:T(8,128)}, f32[128,640]{1,0:T(8,128)}, u32[]{:S(2)}, u32[]{:S(2)}) collective-permute-start(f32[128,640]{1,0:T(8,128)} %get-tuple-element.27), channel_id=1, source_target_pairs={{0,96},{32,0},{64,32},{96,64},{1,97},{33,1},{65,33},{97,65},{2,98}... | collective-permute-start | bytes 983048 | tf_op jit(solution)/shard_map/finish/ppermute | solution.py:211
  160.0 10.5 %collective-permute-start.5 = (f32[128,640]{1,0:T(8,128)}, f32[128,640]{1,0:T(8,128)}, u32[]{:S(2)}, u32[]{:S(2)}) collective-permute-start(f32[128,640]{1,0:T(8,128)} %get-tuple-element.26), channel_id=1, source_target_pairs={{0,64},{32,96},{64,0},{96,32},{1,65},{33,97},{65,1},{97,33},{2,66}... | collective-permute-start | bytes 983048 | tf_op jit(solution)/shard_map/finish/ppermute | solution.py:211
  163.3 8.6 %collective-permute-start.12 = (f32[128,640]{1,0:T(8,128)}, f32[128,640]{1,0:T(8,128)}, u32[]{:S(2)}, u32[]{:S(2)}) collective-permute-start(f32[128,640]{1,0:T(8,128)} %get-tuple-element.25), channel_id=1, source_target_pairs={{0,8},{8,16},{16,24},{24,0},{1,9},{9,17},{17,25},{25,1},{2,10},{10... | collective-permute-start | bytes 983048 | tf_op jit(solution)/shard_map/finish/ppermute | solution.py:211
  165.3 7.2 %collective-permute-start.13 = (f32[128,640]{1,0:T(8,128)S(1)}, f32[128,640]{1,0:T(8,128)}, u32[]{:S(2)}, u32[]{:S(2)}) collective-permute-start(f32[128,640]{1,0:T(8,128)S(1)} %get-tuple-element.24), channel_id=1, source_target_pairs={{0,24},{8,0},{16,8},{24,16},{1,25},{9,1},{17,9},{25,17},{2,26},{10... | collective-permute-start | bytes 983048 | tf_op jit(solution)/shard_map/finish/ppermute | solution.py:211
  166.6 10.3 %collective-permute-start.11 = (f32[128,640]{1,0:T(8,128)S(1)}, f32[128,640]{1,0:T(8,128)}, u32[]{:S(2)}, u32[]{:S(2)}) collective-permute-start(f32[128,640]{1,0:T(8,128)S(1)} %get-tuple-element.23), channel_id=1, source_target_pairs={{0,16},{8,24},{16,0},{24,8},{1,17},{9,25},{17,1},{25,9},{2,18},{10... | collective-permute-start | bytes 983048 | tf_op jit(solution)/shard_map/finish/ppermute | solution.py:211
  169.9 20.2 %collective-permute-start.20 = (bf16[4,256,256]{2,1,0:T(8,128)(2,1)S(1)}, bf16[4,256,256]{2,1,0:T(8,128)(2,1)S(1)}, u32[]{:S(2)}, u32[]{:S(2)}) collective-permute-start(bf16[4,256,256]{2,1,0:T(8,128)(2,1)S(1)} %all-to-all-done.2), channel_id=1, source_target_pairs={{0,4},{4,0},{1,5},{5,1},{2,6},{6,2},{3,7},{7,3},{8,12},{12,8},{9,1... | collective-permute-start | bytes 1572872 | tf_op jit(solution)/shard_map/roots/ppermute | solution.py:205
  179.3 12.9 %collective-permute-start.14 = (f32[128,640]{1,0:T(8,128)}, f32[128,640]{1,0:T(8,128)S(1)}, u32[]{:S(2)}, u32[]{:S(2)}) collective-permute-start(f32[128,640]{1,0:T(8,128)} %get-tuple-element.20), channel_id=1, source_target_pairs={{0,128},{128,0},{1,129},{129,1},{2,130},{130,2},{3,131},{131,3},{4... | collective-permute-start | bytes 983048 | tf_op jit(solution)/shard_map/finish/ppermute | solution.py:205
  193.7 13.5 %collective-permute-start.21 = (bf16[256,256]{1,0:T(8,128)(2,1)S(1)}, bf16[256,256]{1,0:T(8,128)(2,1)S(1)}, u32[]{:S(2)}, u32[]{:S(2)}) collective-permute-start(bf16[256,256]{1,0:T(8,128)(2,1)S(1)} %dynamic-slice_bitcast_fusion.6), channel_id=1, source_target_pairs={{0,1},{32,33},{65,66},{97,98},{130,131},{162,163},{195,192},{227,2... | collective-permute-start | bytes 393224 | tf_op jit(solution)/shard_map/left_root/ppermute | solution.py:272
  195.0 12.2 %collective-permute-start.22 = (bf16[256,256]{1,0:T(8,128)(2,1)S(1)}, bf16[256,256]{1,0:T(8,128)(2,1)S(1)}, u32[]{:S(2)}, u32[]{:S(2)}) collective-permute-start(bf16[256,256]{1,0:T(8,128)(2,1)S(1)} %dynamic-slice_bitcast_fusion.6), channel_id=1, source_target_pairs={{0,2},{32,34},{65,67},{97,99},{130,128},{162,160},{195,193},{227,2... | collective-permute-start | bytes 393224 | tf_op jit(solution)/shard_map/left_root/ppermute | solution.py:272
  195.9 11.3 %collective-permute-start.16 = (f32[128,640]{1,0:T(8,128)S(1)}, f32[128,640]{1,0:T(8,128)S(1)}, u32[]{:S(2)}, u32[]{:S(2)}) collective-permute-start(f32[128,640]{1,0:T(8,128)S(1)} %select_add_fusion.mine_ref), channel_id=1, source_target_pairs={{0,4},{4,0},{1,5},{5,1},{2,6},{6,2},{3,7},{7,3},{8,12},{12,8},{9,1... | collective-permute-start | bytes 983048 | tf_op jit(solution)/shard_map/finish/ppermute | solution.py:205
  199.4 7.8 %collective-permute-start.17 = (f32[128,640]{1,0:T(8,128)S(1)}, f32[128,640]{1,0:T(8,128)S(1)}, u32[]{:S(2)}, u32[]{:S(2)}) collective-permute-start(f32[128,640]{1,0:T(8,128)S(1)} %collective-permute-done.15.beside_ref), channel_id=1, source_target_pairs={{0,4},{4,0},{1,5},{5,1},{2,6},{6,2},{3,7},{7,3},{8,12},{12,8},{9,1... | collective-permute-start | bytes 983048 | tf_op jit(solution)/shard_map/finish/ppermute | solution.py:205
  (13 other events, 64.1 us)

commit v4 on v2

v4 whole, which is shorter than its diff:
```python
import functools
import math

import jax
import jax.numpy as jnp
from jax import lax
from jax.experimental import pallas as pl
from jax.experimental.pallas import tpu as pltpu
from jax.sharding import Mesh, PartitionSpec as P

BS = 256
HALF = 128
ITERS = 12
MOST = 2
DAMPING = 0.1
TOKENS = 32768
DP = ("zh", "y", "x", "c")
HIGHEST = lax.Precision.HIGHEST
F32 = jnp.float32
BF16 = jnp.bfloat16


def tdot(lhs, rhs):
    return lax.dot_general(lhs, rhs, (((0,), (0,)), ((), ())), preferred_element_type=F32)


SMEM = pl.BlockSpec(memory_space=pltpu.SMEM)
ANY = pl.BlockSpec(memory_space=pl.ANY)
SHIFTS = (2, 1, 3, 0)


def at(start, size, step=HALF):
    return pl.ds(pl.multiple_of(start, step), size)


def whole(array):
    return pl.BlockSpec(array.shape, lambda *_: (0,) * len(array.shape))


def call(kernel, grid, scalars, in_specs, out_specs, out_shape, operands, scratch=(), limit=60, flops=0):
    return pl.pallas_call(
        kernel,
        grid_spec=pltpu.PrefetchScalarGridSpec(
            num_scalar_prefetch=1, grid=grid, in_specs=in_specs, out_specs=out_specs, scratch_shapes=scratch
        ),
        out_shape=out_shape,
        compiler_params=pltpu.CompilerParams(vmem_limit_bytes=limit * 2**20),
        cost_estimate=pl.CostEstimate(flops=flops, bytes_accessed=2**18, transcendentals=0),
    )(scalars, *operands)


def factor_kernel(where_ref, acts_ref, grads_ref, kept_ref, sent_ref):
    def write(out_ref, ref, half):
        for block in range(4):
            span = ref[:, block * BS : (block + 1) * BS]
            value = tdot(span, span)
            for row in range(4):
                out_ref[row, block, 0:64, :] = value[row * 64 : (row + 1) * 64]
        value = tdot(grads_ref[:, 4 * BS + half * HALF : 4 * BS + (half + 1) * HALF], grads_ref[:, 4 * BS :])
        for row in range(4):
            for block in range(4):
                out_ref[row, block, 64:96, :] = value[row * 32 : (row + 1) * 32]

    @pl.when(where_ref[1] == 0)
    def _():
        write(kept_ref, acts_ref, 0)
        write(sent_ref, grads_ref, 1)

    @pl.when(where_ref[1] == 1)
    def _():
        write(sent_ref, acts_ref, 0)
        write(kept_ref, grads_ref, 1)


def factor_parts(where, acts, grads):
    rows = acts.shape[0]
    shape = jax.ShapeDtypeStruct((4, 4, 96, BS), F32)
    return call(
        factor_kernel,
        (1,),
        where,
        [pl.BlockSpec((rows, 4 * BS), lambda i, w: (0, w[0])), whole(grads)],
        [whole(shape)] * 2,
        [shape] * 2,
        (acts, grads),
    )


def multiply_all(mine, other, grads_ref, grads_other):
    def multiply(left, right):
        return tdot(grads_ref[...], left) + tdot(grads_other[...], right)

    return (
        multiply(jnp.concatenate([r[...] for r in mine[:4]], axis=1), jnp.concatenate([r[...] for r in other[:4]], axis=1)),
        multiply(mine[4][...], other[4][...]),
    )


def far_kernel(where_ref, *refs):
    for part, value in enumerate(multiply_all(refs[0:5], refs[5:10], refs[10], refs[11])):
        for j in range(4):
            refs[13 + part * 2 + j // 2][j % 2] = value[:, j * HALF : (j + 1) * HALF]


def near_kernel(where_ref, *refs):
    outs, slots, sems = refs[13:17], refs[17], refs[18]
    step = pl.program_id(0)

    def copies(k):
        return [pltpu.make_async_copy(slots.at[k, part], outs[part * 2 + k], sems.at[k, part]) for part in range(2)]

    for k in range(2):

        @pl.when(step == k)
        def _(k=k):
            for part, value in enumerate(multiply_all(refs[0:5], refs[5:10], refs[10], refs[11])):
                for j in range(4):
                    slots[k, part, j] = value[:, j * HALF : (j + 1) * HALF]
            for copy in copies(k):
                copy.start()

    @pl.when(step == 1)
    def _():
        for k in range(2):
            for copy in copies(k):
                copy.wait()


def home_kernel(where_ref, *refs):
    for value, out in zip(multiply_all(refs[0:5], refs[5:10], refs[10], refs[11]), refs[13:15], strict=True):
        for j in range(4):
            out[j] = value[:, j * HALF : (j + 1) * HALF]


def product(kernel, where, shifts, acts, acts_other, grads, grads_other, earlier, out_specs, out_shape, **more):
    rows, width = grads.shape[0], grads.shape[1] // 2

    def there(place, i):
        shift = shifts[0]
        for k in range(1, len(shifts)):
            shift = jnp.where(i == k, shifts[k], shift)
        return lax.rem(place + shift, 4)

    lefts = [
        pl.BlockSpec((rows, HALF), functools.partial(lambda j, i, w: (0, 4 * j + there(w[3], i)), j)) for j in range(4)
    ] + [pl.BlockSpec((rows, 4 * HALF), lambda i, w: (0, 4 + there(w[4], i)))]
    columns = pl.BlockSpec((rows, width), lambda i, w: (0, w[1]))
    return call(
        kernel,
        (len(shifts),),
        where,
        lefts + lefts + [columns, columns, ANY],
        out_specs,
        out_shape,
        [acts] * 5 + [acts_other] * 5 + [grads, grads_other, earlier],
        **more,
    )


def far_products(where, *inputs):
    two = jax.ShapeDtypeStruct((2, inputs[2].shape[1] // 2, HALF), F32)
    return product(far_kernel, where, (2,), *inputs, [whole(two)] * 4, [two] * 4)


def near_products(where, *inputs):
    width = inputs[2].shape[1] // 2
    four = jax.ShapeDtypeStruct((4, width, HALF), F32)
    scratch = [pltpu.VMEM((2, 2, 4, width, HALF), F32), pltpu.SemaphoreType.DMA((2, 2))]
    return product(near_kernel, where, (1, 3), *inputs, [ANY] * 4, [four] * 4, scratch=scratch)


def home_products(where, *inputs):
    four = jax.ShapeDtypeStruct((4, inputs[2].shape[1] // 2, HALF), F32)
    return product(home_kernel, where, (0,), *inputs, [whole(four)] * 2, [four] * 2)


def merge_kernel(_, *refs):
    for k in range(4):
        refs[9 + k][...] = refs[k][...] + refs[4 + k][...]


def merge(where, near, came, earlier):
    shape = near[0].shape
    block = (1, *shape[1:])
    low = pl.BlockSpec(block, lambda i, w: (i, 0, 0))
    high = pl.BlockSpec(block, lambda i, w: (2 + i, 0, 0))
    return pl.pallas_call(
        merge_kernel,
        grid_spec=pltpu.PrefetchScalarGridSpec(
            num_scalar_prefetch=1,
            grid=(2,),
            in_specs=[low, high, low, high] + [low] * 4 + [ANY],
            out_specs=[low, high, low, high],
        ),
        out_shape=[jax.ShapeDtypeStruct(shape, F32)] * 4,
        input_output_aliases={1: 0, 2: 1, 3: 2, 4: 3},
        compiler_params=pltpu.CompilerParams(vmem_limit_bytes=60 * 2**20),
        cost_estimate=pl.CostEstimate(flops=0, bytes_accessed=2**18, transcendentals=0),
    )(where, *near, *came, earlier)


def route_kernel(_, *refs):
    for part in range(2):
        own, below, above = refs[part * 3 : part * 3 + 3]
        refs[7 + part][...] = own[...] + (below[...] + above[...])


def route(where, first, second, earlier):
    shape = jax.ShapeDtypeStruct(first[0].shape, F32)
    every = pl.BlockSpec((1, *shape.shape[1:]), lambda i, w: (i, 0, 0))
    return call(
        route_kernel, (4,), where, [every] * 6 + [ANY], [every] * 2, [shape] * 2, (*first, *second, earlier)
    )


def settle_kernel(where_ref, low_ref, h0, h1, h2, h3, _, stay_ref, leave_ref):
    low = (low_ref[0] + low_ref[1]) + (low_ref[2] + low_ref[3])
    high = (h3[...] + h0[...]) + (h1[...] + h2[...])

    @pl.when(where_ref[5] == 0)
    def _():
        stay_ref[...] = low
        leave_ref[...] = high

    @pl.when(where_ref[5] == 1)
    def _():
        stay_ref[...] = high
        leave_ref[...] = low


def settle(where, low, high, earlier):
    shape = jax.ShapeDtypeStruct(low.shape[1:], F32)
    specs = [whole(low)] + [whole(shape)] * 4 + [ANY]
    return call(settle_kernel, (1,), where, specs, [whole(shape)] * 2, [shape] * 2, (low, *high, earlier), limit=16)


def fold_kernel(_, in_ref, out_ref):
    rows = out_ref.shape[0]
    total = in_ref[0:rows]
    for source in range(1, 16):
        total = total + in_ref[source * rows : (source + 1) * rows]
    out_ref[...] = total


def fold(where, parts):
    shape = jax.ShapeDtypeStruct((parts.shape[0] // 16, BS), F32)
    return call(fold_kernel, (1,), where, [whole(parts)], whole(shape), shape, (parts,), limit=16)


def root_kernel(where_ref, p0, p1, p2, p3, _, out_ref, block_ref, last):
    core = where_ref[1]
    for shift, piece in enumerate((p0, p1, p2, p3)):
        place = lax.rem(where_ref[4] + 4 - shift, 4)
        block_ref[at(place * 64, 64, 64), :] = piece[0:64]
        last[at(core * HALF + place * 32, 32, 32), :] = piece[64:96]
        last[at((1 - core) * HALF + place * 32, 32, 32), :] = piece[96:128]
    row = lax.broadcasted_iota(jnp.int32, (BS, BS), 0)
    col = lax.broadcasted_iota(jnp.int32, (BS, BS), 1)
    identity = jnp.where(row == col, 1.0, 0.0).astype(F32)
    mul = functools.partial(jnp.dot, precision=HIGHEST, preferred_element_type=F32)

    def start(summed):
        factor = summed * (1.0 / TOKENS) + DAMPING * identity
        norm = jnp.sqrt(jnp.sum(factor * factor, keepdims=True))
        current = factor / norm
        step = 1.5 * identity - 0.5 * current
        return norm, mul(current, step), step

    norm_a, cur_a, est_a = start(block_ref[...])
    norm_b, cur_b, est_b = start(last[...])

    def advance(_, carry):
        cur_a, est_a, cur_b, est_b = carry
        step_a = 1.5 * identity - 0.5 * mul(est_a, cur_a)
        step_b = 1.5 * identity - 0.5 * mul(est_b, cur_b)
        return mul(cur_a, step_a), mul(step_a, est_a), mul(cur_b, step_b), mul(step_b, est_b)

    cur_a, est_a, cur_b, est_b = lax.fori_loop(0, ITERS - 2, advance, (cur_a, est_a, cur_b, est_b))
    step_a = 1.5 * identity - 0.5 * mul(est_a, cur_a)
    step_b = 1.5 * identity - 0.5 * mul(est_b, cur_b)
    out_ref[0] = (mul(step_a, est_a) / jnp.sqrt(norm_a)).astype(BF16)
    out_ref[1] = (mul(step_b, est_b) / jnp.sqrt(norm_b)).astype(BF16)


def two_roots(where, pieces, earlier):
    shape = jax.ShapeDtypeStruct((2, BS, BS), BF16)
    return call(
        root_kernel,
        (1,),
        where,
        [whole(p) for p in pieces] + [ANY],
        whole(shape),
        shape,
        (*pieces, earlier),
        scratch=[pltpu.VMEM((BS, BS), F32), pltpu.VMEM((BS, BS), F32)],
        limit=32,
    )


def apply_kernel(where_ref, mine_ref, beside_ref, mine_other, beside_other, left_ref, right_ref, last_ref, out_ref, left_done, done):
    core, x_low = where_ref[1], where_ref[2]
    width = mine_ref.shape[0]
    cols = at(x_low * HALF, HALF)

    def side(place, part):
        return jnp.dot(part, left_ref[at(place * HALF, HALF), cols].astype(F32), precision=HIGHEST, preferred_element_type=F32)

    for place, mine, beside in ((core, mine_ref, beside_ref), (1 - core, mine_other, beside_other)):
        left_done[at(place * width, width), :] = side(x_low, mine[...]) + side(1 - x_low, beside[...])
    for block in range(5):
        root = right_ref[block] if block < 4 else last_ref[...]
        span = slice(block * BS, (block + 1) * BS)
        done[:, span] = lax.dot_general(
            left_done[span, :], root.astype(F32), (((0,), (0,)), ((), ())), precision=HIGHEST, preferred_element_type=F32
        )
    out_ref[...] = (done[at(core * 64, 64, 64), :] * (1.0 / math.sqrt(TOKENS))).astype(BF16)


def apply_roots(where, pieces, left, right, last):
    width = 2 * pieces[0].shape[0]
    shape = jax.ShapeDtypeStruct((64, width), BF16)
    return call(
        apply_kernel,
        (1,),
        where,
        [whole(p) for p in (*pieces, left, right, last)],
        whole(shape),
        shape,
        (*pieces, left, right, last),
        scratch=[pltpu.VMEM((width, HALF), F32), pltpu.VMEM((HALF, width), F32)],
        limit=32,
    )


def swap(value, axis):
    return lax.ppermute(value, axis, [(0, 1), (1, 0)])


def away(value, axis, shift):
    if shift == 0:
        return value
    return lax.ppermute(value, axis, [(i, (i + shift) % 4) for i in range(4)])


def per_device(acts, grads, owners):
    zh, y, x, core, column = (lax.axis_index(a) for a in ("zh", "y", "x", "c", "mp"))
    x_high, x_low = x // 2, x % 2
    rows, width = grads.shape
    where = jnp.stack([column, core, x_low, x, y, zh]).astype(jnp.int32)

    with jax.named_scope("exchange"):
        acts_other = swap(acts, "c")
        grads_other = swap(grads, "c")

    with jax.named_scope("factors"):
        mine, sent = factor_parts(where, acts, grads)
        mine = mine + swap(sent, "c")
        mine = lax.all_to_all(mine.reshape(16 * 96, BS), ("y", "x"), 0, 0, tiled=True)

    with jax.named_scope("product"):
        inputs = (acts, acts_other, grads, grads_other)
        far = far_products(where, *inputs, where)
        near = list(near_products(where, *inputs, far[0]))
        came = [away(far[0], "x", 1), away(far[1], "x", 3), away(far[2], "y", 1), away(far[3], "y", 3)]
        home = list(home_products(where, *inputs, near[0]))
        mine, *came, home[0] = lax.optimization_barrier((mine, *came, home[0]))

    with jax.named_scope("sum_factors"):
        mine = fold(where, mine)
        near = merge(where, near, came, mine)
        mine = mine + swap(mine, "zh")
        mine = jnp.concatenate([mine, swap(mine[64:], "c")], axis=0)
        pieces = [away(mine, "y", shift) for shift in range(4)]

    with jax.named_scope("roots"):
        pieces[1], pieces[2], pieces[3], *near = lax.optimization_barrier((pieces[1], pieces[2], pieces[3], *near))
        passed = [away(near[0], "x", 1), away(near[1], "x", 3), away(near[2], "y", 1), away(near[3], "y", 3)]
        roots = two_roots(where, pieces, near[0])
        last_root = roots[1]
        four = jnp.broadcast_to(roots[0], (4, BS, BS)).reshape(4 * BS, BS)
        four = lax.all_to_all(four, "x", 0, 0, tiled=True)

    with jax.named_scope("route"):
        low, high = route(where, (home[0], *passed[:2]), (home[1], *passed[2:]), roots)
        four, low = lax.optimization_barrier((four, low))
        low = lax.all_to_all(low, "y", 0, 0, tiled=True)
        routed = [lax.dynamic_index_in_dim(high, lax.rem(x + shift, 4), 0, keepdims=False) for shift in SHIFTS]
        high = [away(v, "x", shift) for v, shift in zip(routed, SHIFTS, strict=True)]

    with jax.named_scope("share"):
        four = four.reshape(4, BS, BS)
        other_four = swap(four, "c")
        input_roots = jnp.where(core == 0, four, other_four)
        output_roots = jnp.where(core == 0, other_four, four)

    with jax.named_scope("left_root"):
        holder = zh * 2 + y // 2
        left = lax.dynamic_index_in_dim(input_roots, (y % 2) * 2 + x_high, 0, keepdims=False)
        got = jnp.zeros_like(left)
        for shift in range(1, 4):
            pairs = []
            for a in range(2):
                for b in range(4):
                    source = a * 2 + b // 2
                    pairs.append(((a * 4 + b) * 4 + source, (a * 4 + b) * 4 + (source + shift) % 4))
            got = got + lax.ppermute(left, ("zh", "y", "mp"), pairs)
        left = jnp.where(column == holder, left, got)

    with jax.named_scope("kept"):
        data_rank = ((zh * 4 + y) * 4 + x) * 2 + core
        owned = (owners[0] == data_rank).astype(jnp.int32)
        order = jnp.cumsum(owned) - 1
        slots = jnp.arange(MOST, dtype=jnp.int32)
        select = owned[None, :] * (order[None, :] == slots[:, None]).astype(jnp.int32)
        filled = jnp.sum(select, axis=1)
        place = jnp.argmax(select, axis=1)
        every = jnp.concatenate([input_roots, output_roots, last_root[None]], axis=0)
        kept = jnp.stack(
            [
                jnp.where(filled[s] > 0, lax.dynamic_index_in_dim(every, place[s], 0, keepdims=False), 0).astype(BF16)
                for s in range(MOST)
            ]
        )

    with jax.named_scope("finish"):
        stay, leave = settle(where, low, high, other_four)
        total = stay + swap(leave, "zh")
        total, left = lax.optimization_barrier((total, left))
        beside = lax.ppermute(total, "x", [(0, 1), (1, 0), (2, 3), (3, 2)])
        pieces = (total, beside, swap(total, "c"), swap(beside, "c"))
        update = apply_roots(where, pieces, left, output_roots, last_root)
    return update, kept


def solution(mesh):
    fine = Mesh(mesh.devices.reshape(2, 4, 4, 2, 4), ("zh", "y", "x", "c", "mp"))
    return jax.shard_map(
        per_device,
        mesh=fine,
        in_specs=(P(DP, None), P(DP, "mp"), P("mp", None)),
        out_specs=(P(DP, "mp"), P(DP, "mp", None)),
        check_vma=False,
    )
```

time: 210 us -> 190 us (0.905)
  the two profiles are of different devices: /device:TPU:65 before, /device:TPU:32 now
where the time goes in v4:
time: 190 us; the launch traced here: 189 us
  Pallas kernels  60.4 us (32%)
  starting transfers between devices  57.7 us (30%)
  waiting for transfers between devices  45.9 us (24%)
  local copies, waits for them, and re-layouts  11.7 us (6%)
  other arithmetic  6.96 us (4%)
  between operations  6.27 us (3%)
    pallas_call x9, Pallas kernels, call(): pl.pallas_call(kernel, grid_spec=pltpu.PrefetchScalarGridSpec(num_scalar_...  56 us
    ppermute x9, waiting for transfers between devices, swap(): return lax.ppermute(value, axis, [(0, 1), (1, 0)])  24.2 us
    ppermute x14, starting transfers between devices, away(): return lax.ppermute(value, axis, [(i, (i + shift) % 4) for i in range(4)])  24 us
    ppermute x14, waiting for transfers between devices, away(): return lax.ppermute(value, axis, [(i, (i + shift) % 4) for i in range(4)])  17.7 us
    ppermute x9, starting transfers between devices, swap(): return lax.ppermute(value, axis, [(0, 1), (1, 0)])  13.8 us
    all_to_all x1, starting transfers between devices, per_device(): lax.all_to_all(mine.reshape(16 * 96, BS), ('y', 'x'), 0, 0, tiled=True)  7.04 us
    unnamed x38, local copies, waits for them, and re-layouts  6.19 us
    pallas_call x1, Pallas kernels, merge(): pl.pallas_call(merge_kernel, grid_spec=pltpu.PrefetchScalarGridSpec(num_s...  4.41 us
  transfers between devices with their start and end apart: 30, of which 14 were waited for; matrix products, arithmetic and copies ran while one was open for 7% of the time, Pallas kernels for 30%

profile of v4, /device:TPU:32, one launch (start us, length us, event | category | flops | bytes accessed | tf_op | source)
XLA Modules:
  0.0 189.0 jit_solution(5992705141265827033)
XLA Ops:
  1.3 4.9 %factors.1 = (f32[4,4,96,256]{3,2,1,0:T(8,128)}, f32[4,4,96,256]{3,2,1,0:T(8,128)}) custom-call(s32[6]{0:T(128)} %stack.32.where_ref.refs_12_._, bf16[512,4096]{1,0:T(8,128)(2,1)} %refs_4_.5, bf16[512,1280]{1,0:T(8,128)(2,1)} %refs_10_.5), custom_call_target="tpu_custom_call" | custom-call | bytes 262144 | tf_op jit(solution)/shard_map/factors/pallas_call | solution.py:41
  6.8 5.0 %collective-permute-done = f32[4,4,96,256]{3,2,1,0:T(8,128)S(1)} collective-permute-done((f32[4,4,96,256]{3,2,1,0:T(8,128)}, f32[4,4,96,256]{3,2,1,0:T(8,128)S(1)}, u32[]{:S(2)}, u32[]{:S(2)}) %collective-permute-start) | collective-permute-done | bytes 1572896 | tf_op jit(solution)/shard_map/factors/ppermute | solution.py:336
  11.8 2.8 %add.79 = f32[4,4,96,256]{3,2,1,0:T(8,128)} add(f32[4,4,96,256]{3,2,1,0:T(8,128)} %get-tuple-element.40, f32[4,4,96,256]{3,2,1,0:T(8,128)S(1)} %collective-permute-done) | non-fusion elementwise | flops 393216 | bytes 4718592 | tf_op jit(solution)/shard_map/factors/add | solution.py:357
  14.6 7.0 %all-to-all-start = ((f32[16,96,256]{2,1,0:T(8,128)}), f32[16,96,256]{2,1,0:T(8,128)S(1)}, u32[]{:S(2)}, u32[]{:S(2)}) async-start(f32[16,96,256]{2,1,0:T(8,128)} %bitcast.37), calls=%async_computation | async-start | bytes 3145728 | tf_op jit(solution)/shard_map/factors/all_to_all | solution.py:358
  21.7 5.4 %product.3 = (f32[2,640,128]{2,1,0:T(8,128)}, f32[2,640,128]{2,1,0:T(8,128)}, f32[2,640,128]{2,1,0:T(8,128)}, f32[2,640,128]{2,1,0:T(8,128)}) custom-call(s32[6]{0:T(128)} %stack.32.where_ref.refs_12_._, bf16[512,4096]{1,0:T(8,128)(2,1)} %refs_4_.5, bf16[512,4096]{1,0:T(8,128)(2,1)} %refs_4_.5, bf16[512,4096]{1,0:T(8,128)(2,1)} %refs_4_.5, ...), custom_call_target="tpu_custom_call" | custom-call | bytes 262144 | tf_op jit(solution)/shard_map/product/pallas_call | solution.py:41
  33.5 7.6 %product.4 = (f32[4,640,128]{2,1,0:T(8,128)}, f32[4,640,128]{2,1,0:T(8,128)}, f32[4,640,128]{2,1,0:T(8,128)}, f32[4,640,128]{2,1,0:T(8,128)}) custom-call(s32[6]{0:T(128)} %stack.32.where_ref.refs_12_._, bf16[512,4096]{1,0:T(8,128)(2,1)} %refs_4_.5, bf16[512,4096]{1,0:T(8,128)(2,1)} %refs_4_.5, bf16[512,4096]{1,0:T(8,128)(2,1)} %refs_4_.5, ...), custom_call_target="tpu_custom_call" | custom-call | bytes 262144 | tf_op jit(solution)/shard_map/product/pallas_call | solution.py:41
  41.2 5.5 %product.5 = (f32[4,640,128]{2,1,0:T(8,128)}, f32[4,640,128]{2,1,0:T(8,128)}) custom-call(s32[6]{0:T(128)} %stack.32.where_ref.refs_12_._, bf16[512,4096]{1,0:T(8,128)(2,1)} %refs_4_.5, bf16[512,4096]{1,0:T(8,128)(2,1)} %refs_4_.5, bf16[512,4096]{1,0:T(8,128)(2,1)} %refs_4_.5, bf16[512,4096]{1,0:T(8,128)(2,1)} %refs_4_.5, bf16[512,4096]{1,0:T(8,128)(2,1)} %refs_4_.5, ...), custom_call_target="tpu_custom_call" | custom-call | bytes 262144 | tf_op jit(solution)/shard_map/product/pallas_call | solution.py:41
  48.4 9.1 %collective-permute-done.3.refs_4_ = f32[2,640,128]{2,1,0:T(8,128)S(1)} collective-permute-done((f32[2,640,128]{2,1,0:T(8,128)}, f32[2,640,128]{2,1,0:T(8,128)S(1)}, u32[]{:S(2)}, u32[]{:S(2)}) %collective-permute-start.3) | collective-permute-done | bytes 655392 | tf_op jit(solution)/shard_map/product/ppermute | solution.py:342
  58.6 6.4 %collective-permute-start.7 = (f32[96,256]{1,0:T(8,128)S(1)}, f32[96,256]{1,0:T(8,128)S(1)}, u32[]{:S(2)}, u32[]{:S(2)}) collective-permute-start(f32[96,256]{1,0:T(8,128)S(1)} %sum_factors.2.refs_8_), channel_id=1, source_target_pairs={{0,128},{128,0},{1,129},{129,1},{2,130},{130,2},{3,131},{131,3},{4... | collective-permute-start | bytes 294920 | tf_op jit(solution)/shard_map/sum_factors/ppermute | solution.py:336
  65.0 3.9 %collective-permute-done.7 = f32[96,256]{1,0:T(8,128)S(1)} collective-permute-done((f32[96,256]{1,0:T(8,128)S(1)}, f32[96,256]{1,0:T(8,128)S(1)}, u32[]{:S(2)}, u32[]{:S(2)}) %collective-permute-start.7) | collective-permute-done | bytes 98336 | tf_op jit(solution)/shard_map/sum_factors/ppermute | solution.py:336
  70.5 3.0 %collective-permute-start.10 = (f32[128,256]{1,0:T(8,128)S(1)}, f32[128,256]{1,0:T(8,128)S(1)}, u32[]{:S(2)}, u32[]{:S(2)}) collective-permute-start(f32[128,256]{1,0:T(8,128)S(1)} %pad_maximum_fusion.2.p0), channel_id=1, source_target_pairs={{0,64},{32,96},{64,0},{96,32},{1,65},{33,97},{65,1},{97,33},{2,66}... | collective-permute-start | bytes 393224 | tf_op jit(solution)/shard_map/sum_factors/ppermute | solution.py:342
  75.5 4.4 %sum_factors.3 = (f32[4,640,128]{2,1,0:T(8,128)}, f32[4,640,128]{2,1,0:T(8,128)}, f32[4,640,128]{2,1,0:T(8,128)}, f32[4,640,128]{2,1,0:T(8,128)}) custom-call(s32[6]{0:T(128)} %stack.32.where_ref.refs_12_._, f32[4,640,128]{2,1,0:T(8,128)} %get-tuple-element.46.refs_12_.refs_0_, ...), custom_call_target="tpu_custom_call", output_to_operand_aliasing={{0}: (1, {}), {1}: (2, {}), {2}: (3, {}), {3}: (4, {})} | custom-call | bytes 262144 | tf_op jit(solution)/shard_map/sum_factors/pallas_call | solution.py:187
  82.1 2.3 %collective-permute-start.13 = (f32[4,640,128]{2,1,0:T(8,128)}, f32[4,640,128]{2,1,0:T(8,128)S(1)}, u32[]{:S(2)}, u32[]{:S(2)}) collective-permute-start(f32[4,640,128]{2,1,0:T(8,128)} %get-tuple-element.65), channel_id=1, source_target_pairs={{0,24},{8,0},{16,8},{24,16},{1,25},{9,1},{17,9},{25,17},{2,26},{10... | collective-permute-start | bytes 3932168 | tf_op jit(solution)/shard_map/roots/ppermute | solution.py:342
  85.4 2.3 %collective-permute-start.15 = (f32[4,640,128]{2,1,0:T(8,128)}, f32[4,640,128]{2,1,0:T(8,128)}, u32[]{:S(2)}, u32[]{:S(2)}) collective-permute-start(f32[4,640,128]{2,1,0:T(8,128)} %get-tuple-element.68), channel_id=1, source_target_pairs={{0,96},{32,0},{64,32},{96,64},{1,97},{33,1},{65,33},{97,65},{2,98}... | collective-permute-start | bytes 3932168 | tf_op jit(solution)/shard_map/roots/ppermute | solution.py:342
  89.0 21.2 %roots.1.refs_6_ = bf16[2,256,256]{2,1,0:T(8,128)(2,1)S(1)} custom-call(s32[6]{0:T(128)S(1)} %copy-done.8, f32[128,256]{1,0:T(8,128)S(1)} %pad_maximum_fusion.2.p0, f32[128,256]{1,0:T(8,128)S(1)} %collective-permute-done.9.p1, f32[128,256]{1,0:T(8,128)S(1)} %collective-permute-done.10.p2, f32[128,256]{1,0:T(8,128)S(1)} %collective-permute-done.11.p3, ...), custom_call_target="tpu_custom_call" | custom-call | bytes 262144 | tf_op jit(solution)/shard_map/roots/pallas_call | solution.py:41
  111.7 4.2 %all-to-all-start.1 = ((bf16[4,256,256]{2,1,0:T(8,128)(2,1)}), bf16[4,256,256]{2,1,0:T(8,128)(2,1)}, u32[]{:S(2)}, u32[]{:S(2)}) async-start(bf16[4,256,256]{2,1,0:T(8,128)(2,1)} %broadcast_in_dim.11), calls=%async_computation.1 | async-start | bytes 1048576 | tf_op jit(solution)/shard_map/roots/all_to_all | solution.py:381
  117.5 5.8 %route.1 = (f32[4,640,128]{2,1,0:T(8,128)}, f32[4,640,128]{2,1,0:T(8,128)}) custom-call(s32[6]{0:T(128)} %stack.32.where_ref.refs_12_._, f32[4,640,128]{2,1,0:T(8,128)} %get-tuple-element.64.refs_0_, f32[4,640,128]{2,1,0:T(8,128)} %copy-done.13, f32[4,640,128]{2,1,0:T(8,128)} %copy-done.14, f32[4,640,128]{2,1,0:T(8,128)} %get-tuple-element.66.refs_3_, ...), custom_call_target="tpu_custom_call" | custom-call | bytes 262144 | tf_op jit(solution)/shard_map/route/pallas_call | solution.py:41
  124.1 3.7 %all-to-all-start.2 = ((f32[4,640,128]{2,1,0:T(8,128)}), f32[4,640,128]{2,1,0:T(8,128)S(1)}, u32[]{:S(2)}, u32[]{:S(2)}) async-start(f32[4,640,128]{2,1,0:T(8,128)} %get-tuple-element.70), calls=%async_computation.2 | async-start | bytes 2621440 | tf_op jit(solution)/shard_map/route/all_to_all | solution.py:386
  129.3 2.7 %collective-permute-start.16 = (f32[640,128]{1,0:T(8,128)S(1)}, f32[640,128]{1,0:T(8,128)S(1)}, u32[]{:S(2)}, u32[]{:S(2)}) collective-permute-start(f32[640,128]{1,0:T(8,128)S(1)} %get-tuple-element.81), channel_id=1, source_target_pairs={{0,16},{8,24},{16,0},{24,8},{1,17},{9,25},{17,1},{25,9},{2,18},{10... | collective-permute-start | bytes 983048 | tf_op jit(solution)/shard_map/route/ppermute | solution.py:342
  132.6 2.7 %collective-permute-start.18 = (f32[640,128]{1,0:T(8,128)S(1)}, f32[640,128]{1,0:T(8,128)S(1)}, u32[]{:S(2)}, u32[]{:S(2)}) collective-permute-start(f32[640,128]{1,0:T(8,128)S(1)} %get-tuple-element.79), channel_id=1, source_target_pairs={{0,24},{8,0},{16,8},{24,16},{1,25},{9,1},{17,9},{25,17},{2,26},{10... | collective-permute-start | bytes 983048 | tf_op jit(solution)/shard_map/route/ppermute | solution.py:342
  142.8 5.1 %collective-permute-done.17.h1 = f32[640,128]{1,0:T(8,128)S(1)} collective-permute-done((f32[640,128]{1,0:T(8,128)S(1)}, f32[640,128]{1,0:T(8,128)S(1)}, u32[]{:S(2)}, u32[]{:S(2)}) %collective-permute-start.17) | collective-permute-done | bytes 327712 | tf_op jit(solution)/shard_map/route/ppermute | solution.py:342
  152.8 6.4 %collective-permute-start.20 = (f32[640,128]{1,0:T(8,128)}, f32[640,128]{1,0:T(8,128)S(1)}, u32[]{:S(2)}, u32[]{:S(2)}) collective-permute-start(f32[640,128]{1,0:T(8,128)} %get-tuple-element.74), channel_id=1, source_target_pairs={{0,128},{128,0},{1,129},{129,1},{2,130},{130,2},{3,131},{131,3},{4... | collective-permute-start | bytes 983048 | tf_op jit(solution)/shard_map/finish/ppermute | solution.py:336
  161.0 13.4 %collective-permute-done.20 = f32[640,128]{1,0:T(8,128)S(1)} collective-permute-done((f32[640,128]{1,0:T(8,128)}, f32[640,128]{1,0:T(8,128)S(1)}, u32[]{:S(2)}, u32[]{:S(2)}) %collective-permute-start.20) | collective-permute-done | bytes 327712 | tf_op jit(solution)/shard_map/finish/ppermute | solution.py:336
  185.6 3.4 %finish.3 = bf16[64,1280]{1,0:T(8,128)(2,1)} custom-call(s32[6]{0:T(128)S(1)} %copy-done.9, f32[640,128]{1,0:T(8,128)S(1)} %add.88.mine_ref, f32[640,128]{1,0:T(8,128)S(1)} %collective-permute-done.24.beside_ref, f32[640,128]{1,0:T(8,128)S(1)} %collective-permute-done.25.mine_other, f32[640,128]{1,0:T(8,128)S(1)} %collective-permute-done.26.beside_other, ...), custom_call_target="tpu_custom_call" | custom-call | bytes 262144 | tf_op jit(solution)/shard_map/finish/pallas_call | solution.py:41
  (106 shorter events, 44.4 us)
Async XLA Ops:
  0.6 21.0 %collective-permute-start.1 = (bf16[512,4096]{1,0:T(8,128)(2,1)}, bf16[512,4096]{1,0:T(8,128)(2,1)}, u32[]{:S(2)}, u32[]{:S(2)}) collective-permute-start(bf16[512,4096]{1,0:T(8,128)(2,1)} %refs_4_.5), channel_id=1, source_target_pairs={{0,4},{4,0},{1,5},{5,1},{2,6},{6,2},{3,7},{7,3},{8,12},{12,8},{9,1... | collective-permute-start | bytes 12582920 | tf_op jit(solution)/shard_map/exchange/ppermute | solution.py:336
  6.7 14.9 %collective-permute-start.2 = (bf16[512,1280]{1,0:T(8,128)(2,1)S(1)}, bf16[512,1280]{1,0:T(8,128)(2,1)}, u32[]{:S(2)}, u32[]{:S(2)}) collective-permute-start(bf16[512,1280]{1,0:T(8,128)(2,1)S(1)} %copy-done.10), channel_id=1, source_target_pairs={{0,4},{4,0},{1,5},{5,1},{2,6},{6,2},{3,7},{7,3},{8,12},{12,8},{9,1... | collective-permute-start | bytes 3932168 | tf_op jit(solution)/shard_map/exchange/ppermute | solution.py:336
  14.6 33.8 %all-to-all-start = ((f32[16,96,256]{2,1,0:T(8,128)}), f32[16,96,256]{2,1,0:T(8,128)S(1)}, u32[]{:S(2)}, u32[]{:S(2)}) async-start(f32[16,96,256]{2,1,0:T(8,128)} %bitcast.37), calls=%async_computation | async-start | bytes 3145728 | tf_op jit(solution)/shard_map/factors/all_to_all | solution.py:358
  27.0 30.4 %collective-permute-start.3 = (f32[2,640,128]{2,1,0:T(8,128)}, f32[2,640,128]{2,1,0:T(8,128)S(1)}, u32[]{:S(2)}, u32[]{:S(2)}) collective-permute-start(f32[2,640,128]{2,1,0:T(8,128)} %get-tuple-element.42.refs_12_), channel_id=1, source_target_pairs={{0,8},{8,16},{16,24},{24,0},{1,9},{9,17},{17,25},{25,1},{2,10},{10... | collective-permute-start | bytes 1966088 | tf_op jit(solution)/shard_map/product/ppermute | solution.py:342
  29.0 29.0 %collective-permute-start.4 = (f32[2,640,128]{2,1,0:T(8,128)}, f32[2,640,128]{2,1,0:T(8,128)S(1)}, u32[]{:S(2)}, u32[]{:S(2)}) collective-permute-start(f32[2,640,128]{2,1,0:T(8,128)} %get-tuple-element.43), channel_id=1, source_target_pairs={{0,24},{8,0},{16,8},{24,16},{1,25},{9,1},{17,9},{25,17},{2,26},{10... | collective-permute-start | bytes 1966088 | tf_op jit(solution)/shard_map/product/ppermute | solution.py:342
  30.3 27.7 %collective-permute-start.5 = (f32[2,640,128]{2,1,0:T(8,128)}, f32[2,640,128]{2,1,0:T(8,128)}, u32[]{:S(2)}, u32[]{:S(2)}) collective-permute-start(f32[2,640,128]{2,1,0:T(8,128)} %get-tuple-element.44), channel_id=1, source_target_pairs={{0,32},{32,64},{64,96},{96,0},{1,33},{33,65},{65,97},{97,1},{2,34}... | collective-permute-start | bytes 1966088 | tf_op jit(solution)/shard_map/product/ppermute | solution.py:342
  32.2 25.8 %collective-permute-start.6 = (f32[2,640,128]{2,1,0:T(8,128)}, f32[2,640,128]{2,1,0:T(8,128)}, u32[]{:S(2)}, u32[]{:S(2)}) collective-permute-start(f32[2,640,128]{2,1,0:T(8,128)} %get-tuple-element.45), channel_id=1, source_target_pairs={{0,96},{32,0},{64,32},{96,64},{1,97},{33,1},{65,33},{97,65},{2,98}... | collective-permute-start | bytes 1966088 | tf_op jit(solution)/shard_map/product/ppermute | solution.py:342
  58.6 10.3 %collective-permute-start.7 = (f32[96,256]{1,0:T(8,128)S(1)}, f32[96,256]{1,0:T(8,128)S(1)}, u32[]{:S(2)}, u32[]{:S(2)}) collective-permute-start(f32[96,256]{1,0:T(8,128)S(1)} %sum_factors.2.refs_8_), channel_id=1, source_target_pairs={{0,128},{128,0},{1,129},{129,1},{2,130},{130,2},{3,131},{131,3},{4... | collective-permute-start | bytes 294920 | tf_op jit(solution)/shard_map/sum_factors/ppermute | solution.py:336
  70.5 9.5 %collective-permute-start.10 = (f32[128,256]{1,0:T(8,128)S(1)}, f32[128,256]{1,0:T(8,128)S(1)}, u32[]{:S(2)}, u32[]{:S(2)}) collective-permute-start(f32[128,256]{1,0:T(8,128)S(1)} %pad_maximum_fusion.2.p0), channel_id=1, source_target_pairs={{0,64},{32,96},{64,0},{96,32},{1,65},{33,97},{65,1},{97,33},{2,66}... | collective-permute-start | bytes 393224 | tf_op jit(solution)/shard_map/sum_factors/ppermute | solution.py:342
  81.2 34.8 %collective-permute-start.12 = (f32[4,640,128]{2,1,0:T(8,128)}, f32[4,640,128]{2,1,0:T(8,128)S(1)}, u32[]{:S(2)}, u32[]{:S(2)}) collective-permute-start(f32[4,640,128]{2,1,0:T(8,128)} %get-tuple-element.63._), channel_id=1, source_target_pairs={{0,8},{8,16},{16,24},{24,0},{1,9},{9,17},{17,25},{25,1},{2,10},{10... | collective-permute-start | bytes 3932168 | tf_op jit(solution)/shard_map/roots/ppermute | solution.py:342
  82.1 33.9 %collective-permute-start.13 = (f32[4,640,128]{2,1,0:T(8,128)}, f32[4,640,128]{2,1,0:T(8,128)S(1)}, u32[]{:S(2)}, u32[]{:S(2)}) collective-permute-start(f32[4,640,128]{2,1,0:T(8,128)} %get-tuple-element.65), channel_id=1, source_target_pairs={{0,24},{8,0},{16,8},{24,16},{1,25},{9,1},{17,9},{25,17},{2,26},{10... | collective-permute-start | bytes 3932168 | tf_op jit(solution)/shard_map/roots/ppermute | solution.py:342
  84.4 31.6 %collective-permute-start.14 = (f32[4,640,128]{2,1,0:T(8,128)}, f32[4,640,128]{2,1,0:T(8,128)}, u32[]{:S(2)}, u32[]{:S(2)}) collective-permute-start(f32[4,640,128]{2,1,0:T(8,128)} %get-tuple-element.67), channel_id=1, source_target_pairs={{0,32},{32,64},{64,96},{96,0},{1,33},{33,65},{65,97},{97,1},{2,34}... | collective-permute-start | bytes 3932168 | tf_op jit(solution)/shard_map/roots/ppermute | solution.py:342
  85.4 30.7 %collective-permute-start.15 = (f32[4,640,128]{2,1,0:T(8,128)}, f32[4,640,128]{2,1,0:T(8,128)}, u32[]{:S(2)}, u32[]{:S(2)}) collective-permute-start(f32[4,640,128]{2,1,0:T(8,128)} %get-tuple-element.68), channel_id=1, source_target_pairs={{0,96},{32,0},{64,32},{96,64},{1,97},{33,1},{65,33},{97,65},{2,98}... | collective-permute-start | bytes 3932168 | tf_op jit(solution)/shard_map/roots/ppermute | solution.py:342
  111.7 12.3 %all-to-all-start.1 = ((bf16[4,256,256]{2,1,0:T(8,128)(2,1)}), bf16[4,256,256]{2,1,0:T(8,128)(2,1)}, u32[]{:S(2)}, u32[]{:S(2)}) async-start(bf16[4,256,256]{2,1,0:T(8,128)(2,1)} %broadcast_in_dim.11), calls=%async_computation.1 | async-start | bytes 1048576 | tf_op jit(solution)/shard_map/roots/all_to_all | solution.py:381
  124.1 11.3 %collective-permute-start.19 = (bf16[4,256,256]{2,1,0:T(8,128)(2,1)}, bf16[4,256,256]{2,1,0:T(8,128)(2,1)S(1)}, u32[]{:S(2)}, u32[]{:S(2)}) collective-permute-start(bf16[4,256,256]{2,1,0:T(8,128)(2,1)} %bitcast.14), channel_id=1, source_target_pairs={{0,4},{4,0},{1,5},{5,1},{2,6},{6,2},{3,7},{7,3},{8,12},{12,8},{9,1... | collective-permute-start | bytes 1572872 | tf_op jit(solution)/shard_map/share/ppermute | solution.py:336
  124.1 25.3 %all-to-all-start.2 = ((f32[4,640,128]{2,1,0:T(8,128)}), f32[4,640,128]{2,1,0:T(8,128)S(1)}, u32[]{:S(2)}, u32[]{:S(2)}) async-start(f32[4,640,128]{2,1,0:T(8,128)} %get-tuple-element.70), calls=%async_computation.2 | async-start | bytes 2621440 | tf_op jit(solution)/shard_map/route/all_to_all | solution.py:386
  129.3 12.2 %collective-permute-start.16 = (f32[640,128]{1,0:T(8,128)S(1)}, f32[640,128]{1,0:T(8,128)S(1)}, u32[]{:S(2)}, u32[]{:S(2)}) collective-permute-start(f32[640,128]{1,0:T(8,128)S(1)} %get-tuple-element.81), channel_id=1, source_target_pairs={{0,16},{8,24},{16,0},{24,8},{1,17},{9,25},{17,1},{25,9},{2,18},{10... | collective-permute-start | bytes 983048 | tf_op jit(solution)/shard_map/route/ppermute | solution.py:342
  132.1 15.9 %collective-permute-start.17 = (f32[640,128]{1,0:T(8,128)S(1)}, f32[640,128]{1,0:T(8,128)S(1)}, u32[]{:S(2)}, u32[]{:S(2)}) collective-permute-start(f32[640,128]{1,0:T(8,128)S(1)} %get-tuple-element.80), channel_id=1, source_target_pairs={{0,8},{8,16},{16,24},{24,0},{1,9},{9,17},{17,25},{25,1},{2,10},{10... | collective-permute-start | bytes 983048 | tf_op jit(solution)/shard_map/route/ppermute | solution.py:342
  132.6 16.0 %collective-permute-start.18 = (f32[640,128]{1,0:T(8,128)S(1)}, f32[640,128]{1,0:T(8,128)S(1)}, u32[]{:S(2)}, u32[]{:S(2)}) collective-permute-start(f32[640,128]{1,0:T(8,128)S(1)} %get-tuple-element.79), channel_id=1, source_target_pairs={{0,24},{8,0},{16,8},{24,16},{1,25},{9,1},{17,9},{25,17},{2,26},{10... | collective-permute-start | bytes 983048 | tf_op jit(solution)/shard_map/route/ppermute | solution.py:342
  137.2 22.7 %collective-permute-start.21 = (bf16[256,256]{1,0:T(8,128)(2,1)}, bf16[256,256]{1,0:T(8,128)(2,1)}, u32[]{:S(2)}, u32[]{:S(2)}) collective-permute-start(bf16[256,256]{1,0:T(8,128)(2,1)} %dynamic-slice_bitcast_fusion.4), channel_id=1, source_target_pairs={{0,1},{32,33},{65,66},{97,98},{130,131},{162,163},{195,192},{227,2... | collective-permute-start | bytes 393224 | tf_op jit(solution)/shard_map/left_root/ppermute | solution.py:406
  138.4 21.4 %collective-permute-start.22 = (bf16[256,256]{1,0:T(8,128)(2,1)}, bf16[256,256]{1,0:T(8,128)(2,1)}, u32[]{:S(2)}, u32[]{:S(2)}) collective-permute-start(bf16[256,256]{1,0:T(8,128)(2,1)} %dynamic-slice_bitcast_fusion.4), channel_id=1, source_target_pairs={{0,2},{32,34},{65,67},{97,99},{130,128},{162,160},{195,193},{227,2... | collective-permute-start | bytes 393224 | tf_op jit(solution)/shard_map/left_root/ppermute | solution.py:406
  141.5 18.3 %collective-permute-start.23 = (bf16[256,256]{1,0:T(8,128)(2,1)}, bf16[256,256]{1,0:T(8,128)(2,1)}, u32[]{:S(2)}, u32[]{:S(2)}) collective-permute-start(bf16[256,256]{1,0:T(8,128)(2,1)} %dynamic-slice_bitcast_fusion.4), channel_id=1, source_target_pairs={{0,3},{32,35},{65,64},{97,96},{130,129},{162,161},{195,194},{227,2... | collective-permute-start | bytes 393224 | tf_op jit(solution)/shard_map/left_root/ppermute | solution.py:406
  152.8 21.5 %collective-permute-start.20 = (f32[640,128]{1,0:T(8,128)}, f32[640,128]{1,0:T(8,128)S(1)}, u32[]{:S(2)}, u32[]{:S(2)}) collective-permute-start(f32[640,128]{1,0:T(8,128)} %get-tuple-element.74), channel_id=1, source_target_pairs={{0,128},{128,0},{1,129},{129,1},{2,130},{130,2},{3,131},{131,3},{4... | collective-permute-start | bytes 983048 | tf_op jit(solution)/shard_map/finish/ppermute | solution.py:336
  174.4 9.6 %collective-permute-start.24 = (f32[640,128]{1,0:T(8,128)S(1)}, f32[640,128]{1,0:T(8,128)S(1)}, u32[]{:S(2)}, u32[]{:S(2)}) collective-permute-start(f32[640,128]{1,0:T(8,128)S(1)} %add.88.mine_ref), channel_id=1, source_target_pairs={{0,8},{8,0},{16,24},{24,16},{1,9},{9,1},{17,25},{25,17},{2,10},{10... | collective-permute-start | bytes 983048 | tf_op jit(solution)/shard_map/finish/ppermute | solution.py:429
  (25 other events, 222.2 us)

commit v5 on v4

--- a/solution.py
+++ b/solution.py
@@ -55,11 +55,18 @@
             span = ref[:, block * BS : (block + 1) * BS]
             value = tdot(span, span)
             for row in range(4):
-                out_ref[row, block, 0:64, :] = value[row * 64 : (row + 1) * 64]
-        value = tdot(grads_ref[:, 4 * BS + half * HALF : 4 * BS + (half + 1) * HALF], grads_ref[:, 4 * BS :])
+                first, last = slice(row * 32, row * 32 + 32), slice(HALF + row * 32, HALF + row * 32 + 32)
+                out_ref[row, block, 0:32, :] = value[first, :HALF]
+                out_ref[row, block, 32:64, :] = value[first, HALF:]
+                out_ref[row, block, 64:96, :] = value[last, HALF:]
+        span = grads_ref[:, 4 * BS :]
+        value = tdot(span, span)
         for row in range(4):
+            tile = value[half * HALF + row * 32 : half * HALF + row * 32 + 32, half * HALF : (half + 1) * HALF]
+            corner = value[half * 64 + row * 16 : half * 64 + row * 16 + 16, HALF:]
             for block in range(4):
-                out_ref[row, block, 64:96, :] = value[row * 32 : (row + 1) * 32]
+                out_ref[row, block, 96:128, :] = tile
+                out_ref[row, block, 128:144, :] = corner
 
     @pl.when(where_ref[1] == 0)
     def _():
@@ -74,7 +81,7 @@
 
 def factor_parts(where, acts, grads):
     rows = acts.shape[0]
-    shape = jax.ShapeDtypeStruct((4, 4, 96, BS), F32)
+    shape = jax.ShapeDtypeStruct((4, 4, 144, HALF), F32)
     return call(
         factor_kernel,
         (1,),
@@ -199,39 +206,55 @@
     )(where, *near, *came, earlier)
 
 
-def route_kernel(_, *refs):
+def route_kernel(where_ref, *refs):
+    step = pl.program_id(0)
+    outs = refs[7:]
     for part in range(2):
         own, below, above = refs[part * 3 : part * 3 + 3]
-        refs[7 + part][...] = own[...] + (below[...] + above[...])
+        distance = lax.rem(step + 4 - where_ref[4 - part], 4)
+        value = own[0] + (below[0] + above[0])
+        for k, shift in enumerate(SHIFTS):
+            for keep in range(2):
+
+                @pl.when(jnp.logical_and(distance == shift, (where_ref[5] == part) == (keep == 1)))
+                def _(out=outs[keep * 4 + k], value=value):
+                    out[...] = value
 
 
 def route(where, first, second, earlier):
-    shape = jax.ShapeDtypeStruct(first[0].shape, F32)
-    every = pl.BlockSpec((1, *shape.shape[1:]), lambda i, w: (i, 0, 0))
-    return call(
-        route_kernel, (4,), where, [every] * 6 + [ANY], [every] * 2, [shape] * 2, (*first, *second, earlier)
-    )
-
-
-def settle_kernel(where_ref, low_ref, h0, h1, h2, h3, _, stay_ref, leave_ref):
-    low = (low_ref[0] + low_ref[1]) + (low_ref[2] + low_ref[3])
-    high = (h3[...] + h0[...]) + (h1[...] + h2[...])
-
-    @pl.when(where_ref[5] == 0)
-    def _():
-        stay_ref[...] = low
-        leave_ref[...] = high
-
-    @pl.when(where_ref[5] == 1)
-    def _():
-        stay_ref[...] = high
-        leave_ref[...] = low
-
-
-def settle(where, low, high, earlier):
-    shape = jax.ShapeDtypeStruct(low.shape[1:], F32)
-    specs = [whole(low)] + [whole(shape)] * 4 + [ANY]
-    return call(settle_kernel, (1,), where, specs, [whole(shape)] * 2, [shape] * 2, (low, *high, earlier), limit=16)
+    shape = jax.ShapeDtypeStruct(first[0].shape[1:], F32)
+    every = pl.BlockSpec((1, *shape.shape), lambda i, w: (i, 0, 0))
+    outs = call(
+        route_kernel,
+        (4,),
+        where,
+        [every] * 6 + [ANY],
+        [whole(shape)] * 8,
+        [shape] * 8,
+        (*first, *second, earlier),
+    )
+    return list(outs[:4]), list(outs[4:])
+
+
+def sum_kernel(_, *refs):
+    refs[5][...] = (refs[3][...] + refs[0][...]) + (refs[1][...] + refs[2][...])
+
+
+def sum_four(where, parts, earlier):
+    shape = jax.ShapeDtypeStruct(parts[0].shape, F32)
+    return call(sum_kernel, (1,), where, [whole(shape)] * 4 + [ANY], whole(shape), shape, (*parts, earlier))
+
+
+def along(value, shift, keep):
+    if shift == 0:
+        return value
+    pairs = []
+    for z in range(2):
+        for i in range(4):
+            for j in range(4):
+                y, x = ((i + shift) % 4, j) if (z == 0) == keep else (i, (j + shift) % 4)
+                pairs.append(((z * 4 + i) * 4 + j, (z * 4 + y) * 4 + x))
+    return lax.ppermute(value, ("zh", "y", "x"), pairs)
 
 
 def fold_kernel(_, in_ref, out_ref):
@@ -243,7 +266,7 @@
 
 
 def fold(where, parts):
-    shape = jax.ShapeDtypeStruct((parts.shape[0] // 16, BS), F32)
+    shape = jax.ShapeDtypeStruct((parts.shape[0] // 16, parts.shape[1]), F32)
     return call(fold_kernel, (1,), where, [whole(parts)], whole(shape), shape, (parts,), limit=16)
 
 
@@ -251,9 +274,23 @@
     core = where_ref[1]
     for shift, piece in enumerate((p0, p1, p2, p3)):
         place = lax.rem(where_ref[4] + 4 - shift, 4)
-        block_ref[at(place * 64, 64, 64), :] = piece[0:64]
-        last[at(core * HALF + place * 32, 32, 32), :] = piece[64:96]
-        last[at((1 - core) * HALF + place * 32, 32, 32), :] = piece[96:128]
+        first, second = at(place * 32, 32, 32), at(HALF + place * 32, 32, 32)
+        block_ref[first, :HALF] = piece[0:32]
+        block_ref[first, HALF:] = piece[32:64]
+        block_ref[second, HALF:] = piece[64:96]
+        for half, wanted in ((0, core == 0), (1, core == 1)):
+
+            @pl.when(wanted)
+            def _(half=half, piece=piece, place=place, first=first, second=second):
+                start = 96 if half == 0 else 144
+                last[first, :HALF] = piece[start : start + 32]
+                last[at(place * 16, 16, 16), HALF:] = piece[start + 32 : start + 48]
+                start = 240 - start
+                last[second, HALF:] = piece[start : start + 32]
+                last[at(64 + place * 16, 16, 16), HALF:] = piece[start + 32 : start + 48]
+
+    block_ref[HALF:, :HALF] = block_ref[:HALF, HALF:].T
+    last[HALF:, :HALF] = last[:HALF, HALF:].T
     row = lax.broadcasted_iota(jnp.int32, (BS, BS), 0)
     col = lax.broadcasted_iota(jnp.int32, (BS, BS), 1)
     identity = jnp.where(row == col, 1.0, 0.0).astype(F32)
@@ -297,7 +334,9 @@
     )
 
 
-def apply_kernel(where_ref, mine_ref, beside_ref, mine_other, beside_other, left_ref, right_ref, last_ref, out_ref, left_done, done):
+def apply_kernel(
+    where_ref, mine_ref, beside_ref, mine_other, beside_other, left_ref, input_ref, right_ref, last_ref, out_ref, kept_ref, left_done, done
+):
     core, x_low = where_ref[1], where_ref[2]
     width = mine_ref.shape[0]
     cols = at(x_low * HALF, HALF)
@@ -314,19 +353,32 @@
             left_done[span, :], root.astype(F32), (((0,), (0,)), ((), ())), precision=HIGHEST, preferred_element_type=F32
         )
     out_ref[...] = (done[at(core * 64, 64, 64), :] * (1.0 / math.sqrt(TOKENS))).astype(BF16)
-
-
-def apply_roots(where, pieces, left, right, last):
+    kept_ref[...] = jnp.zeros_like(kept_ref)
+    count = jnp.int32(0)
+    for block in range(9):
+        root = input_ref.at[block] if block < 4 else right_ref.at[block - 4] if block < 8 else last_ref
+        owned = where_ref[7 + block] == where_ref[6]
+        for slot in range(MOST):
+
+            @pl.when(jnp.logical_and(owned, count == slot))
+            def _(root=root, slot=slot):
+                kept_ref[slot] = root[...]
+
+        count = count + owned.astype(jnp.int32)
+
+
+def apply_roots(where, pieces, left, inputs, right, last):
     width = 2 * pieces[0].shape[0]
     shape = jax.ShapeDtypeStruct((64, width), BF16)
+    kept = jax.ShapeDtypeStruct((MOST, BS, BS), BF16)
     return call(
         apply_kernel,
         (1,),
         where,
-        [whole(p) for p in (*pieces, left, right, last)],
-        whole(shape),
-        shape,
-        (*pieces, left, right, last),
+        [whole(p) for p in (*pieces, left, inputs, right, last)],
+        [whole(shape), whole(kept)],
+        [shape, kept],
+        (*pieces, left, inputs, right, last),
         scratch=[pltpu.VMEM((width, HALF), F32), pltpu.VMEM((HALF, width), F32)],
         limit=32,
     )
@@ -346,34 +398,38 @@
     zh, y, x, core, column = (lax.axis_index(a) for a in ("zh", "y", "x", "c", "mp"))
     x_high, x_low = x // 2, x % 2
     rows, width = grads.shape
-    where = jnp.stack([column, core, x_low, x, y, zh]).astype(jnp.int32)
-
-    with jax.named_scope("exchange"):
-        acts_other = swap(acts, "c")
-        grads_other = swap(grads, "c")
+    data_rank = ((zh * 4 + y) * 4 + x) * 2 + core
+    places = jnp.stack([column, core, x_low, x, y, zh, data_rank]).astype(jnp.int32)
+    where = places[:6]
 
     with jax.named_scope("factors"):
         mine, sent = factor_parts(where, acts, grads)
-        mine = mine + swap(sent, "c")
-        mine = lax.all_to_all(mine.reshape(16 * 96, BS), ("y", "x"), 0, 0, tiled=True)
+        sent = swap(sent, "c")
+        sent, acts_late, grads_late = lax.optimization_barrier((sent, acts, grads))
+        mine = mine + sent
+        mine = lax.all_to_all(mine.reshape(16 * 144, HALF), ("y", "x"), 0, 0, tiled=True)
+
+    with jax.named_scope("exchange"):
+        acts_other = swap(acts_late, "c")
+        grads_other = swap(grads_late, "c")
 
     with jax.named_scope("product"):
         inputs = (acts, acts_other, grads, grads_other)
         far = far_products(where, *inputs, where)
         near = list(near_products(where, *inputs, far[0]))
         came = [away(far[0], "x", 1), away(far[1], "x", 3), away(far[2], "y", 1), away(far[3], "y", 3)]
-        home = list(home_products(where, *inputs, near[0]))
-        mine, *came, home[0] = lax.optimization_barrier((mine, *came, home[0]))
+        mine, near[0] = lax.optimization_barrier((mine, near[0]))
 
     with jax.named_scope("sum_factors"):
         mine = fold(where, mine)
-        near = merge(where, near, came, mine)
-        mine = mine + swap(mine, "zh")
-        mine = jnp.concatenate([mine, swap(mine[64:], "c")], axis=0)
+        home = home_products(where, *inputs, mine)
+        near = list(merge(where, near, came, home[0]))
+        mine, near[0] = lax.optimization_barrier((mine + swap(mine, "zh"), near[0]))
+        mine = jnp.concatenate([mine, swap(mine[96:], "c")], axis=0)
         pieces = [away(mine, "y", shift) for shift in range(4)]
 
     with jax.named_scope("roots"):
-        pieces[1], pieces[2], pieces[3], *near = lax.optimization_barrier((pieces[1], pieces[2], pieces[3], *near))
+        pieces[1], pieces[2], pieces[3], near[2], near[3] = lax.optimization_barrier((*pieces[1:], near[2], near[3]))
         passed = [away(near[0], "x", 1), away(near[1], "x", 3), away(near[2], "y", 1), away(near[3], "y", 3)]
         roots = two_roots(where, pieces, near[0])
         last_root = roots[1]
@@ -381,11 +437,12 @@
         four = lax.all_to_all(four, "x", 0, 0, tiled=True)
 
     with jax.named_scope("route"):
-        low, high = route(where, (home[0], *passed[:2]), (home[1], *passed[2:]), roots)
-        four, low = lax.optimization_barrier((four, low))
-        low = lax.all_to_all(low, "y", 0, 0, tiled=True)
-        routed = [lax.dynamic_index_in_dim(high, lax.rem(x + shift, 4), 0, keepdims=False) for shift in SHIFTS]
-        high = [away(v, "x", shift) for v, shift in zip(routed, SHIFTS, strict=True)]
+        other, own = route(where, (home[0], *passed[:2]), (home[1], *passed[2:]), roots)
+        far_plane = [along(v, shift, False) for v, shift in zip(other, SHIFTS, strict=True)]
+        this_plane = [along(v, shift, True) for v, shift in zip(own, SHIFTS, strict=True)]
+        four, own[3] = lax.optimization_barrier((four, own[3]))
+        leave = sum_four(where, far_plane, four)
+        four, leave = lax.optimization_barrier((four, leave))
 
     with jax.named_scope("share"):
         four = four.reshape(4, BS, BS)
@@ -393,9 +450,13 @@
         input_roots = jnp.where(core == 0, four, other_four)
         output_roots = jnp.where(core == 0, other_four, four)
 
+    with jax.named_scope("finish"):
+        came_over = swap(leave, "zh")
+
     with jax.named_scope("left_root"):
         holder = zh * 2 + y // 2
         left = lax.dynamic_index_in_dim(input_roots, (y % 2) * 2 + x_high, 0, keepdims=False)
+        left, this_plane[0] = lax.optimization_barrier((left, this_plane[0]))
         got = jnp.zeros_like(left)
         for shift in range(1, 4):
             pairs = []
@@ -406,29 +467,11 @@
             got = got + lax.ppermute(left, ("zh", "y", "mp"), pairs)
         left = jnp.where(column == holder, left, got)
 
-    with jax.named_scope("kept"):
-        data_rank = ((zh * 4 + y) * 4 + x) * 2 + core
-        owned = (owners[0] == data_rank).astype(jnp.int32)
-        order = jnp.cumsum(owned) - 1
-        slots = jnp.arange(MOST, dtype=jnp.int32)
-        select = owned[None, :] * (order[None, :] == slots[:, None]).astype(jnp.int32)
-        filled = jnp.sum(select, axis=1)
-        place = jnp.argmax(select, axis=1)
-        every = jnp.concatenate([input_roots, output_roots, last_root[None]], axis=0)
-        kept = jnp.stack(
-            [
-                jnp.where(filled[s] > 0, lax.dynamic_index_in_dim(every, place[s], 0, keepdims=False), 0).astype(BF16)
-                for s in range(MOST)
-            ]
-        )
-
     with jax.named_scope("finish"):
-        stay, leave = settle(where, low, high, other_four)
-        total = stay + swap(leave, "zh")
-        total, left = lax.optimization_barrier((total, left))
+        total = sum_four(where, [*this_plane[:3], own[3]], leave) + came_over
         beside = lax.ppermute(total, "x", [(0, 1), (1, 0), (2, 3), (3, 2)])
         pieces = (total, beside, swap(total, "c"), swap(beside, "c"))
-        update = apply_roots(where, pieces, left, output_roots, last_root)
+        update, kept = apply_roots(jnp.concatenate([places, owners[0]]), pieces, left, input_roots, output_roots, last_root)
     return update, kept
 
 

time: 190 us -> 172 us (0.905)
  waiting for transfers between devices: 45.9 us -> 39.3 us
  between operations: 6.27 us -> 0.94 us
  local copies, waits for them, and re-layouts: 11.7 us -> 6.88 us
  Pallas kernels: 60.4 us -> 65 us
  starting transfers between devices: 57.7 us -> 53.9 us
    ppermute x0 -> x6, waiting for transfers between devices: none -> 19 us  [along(): return lax.ppermute(value, ('zh', 'y', 'x'), pairs)]
    ppermute x9, waiting for transfers between devices: 24.2 us -> 6 us  [swap(): return lax.ppermute(value, axis, [(0, 1), (1, 0)])]
    ppermute x14 -> x11, waiting for transfers between devices: 17.7 us -> 4.37 us  [away(): return lax.ppermute(value, axis, [(i, (i + shift) % 4) for i in range(4)])]
    ppermute x0 -> x6, starting transfers between devices: none -> 11 us  [along(): return lax.ppermute(value, ('zh', 'y', 'x'), pairs)]
    ppermute x14 -> x11, starting transfers between devices: 24 us -> 15.4 us  [away(): return lax.ppermute(value, axis, [(i, (i + shift) % 4) for i in range(4)])]
    pallas_call x9 -> x10, Pallas kernels: 56 us -> 60.5 us  [call(): pl.pallas_call(kernel, grid_spec=pltpu.PrefetchScalarGridSpec(num_scalar_...]
    ppermute x3, waiting for transfers between devices: 0.01 us -> 4.12 us  [per_device(): got = got + lax.ppermute(left, ('zh', 'y', 'mp'), pairs)]
    all_to_all x2 -> x1, starting transfers between devices: 10.7 us -> 7.04 us  [per_device(): lax.all_to_all(mine.reshape(16 * 144, HALF), ('y', 'x'), 0, 0, tiled=True)]
  transfers between devices with their start and end apart: 30 -> 32, of which waited for: 14 -> 14; matrix products, arithmetic and copies ran while one was open for 7% -> 3% of each run, Pallas kernels for 30% -> 29%
where the time goes in v5:
time: 172 us; the launch traced here: 171 us
  Pallas kernels  65 us (38%)
  starting transfers between devices  53.9 us (31%)
  waiting for transfers between devices  39.3 us (23%)
  local copies, waits for them, and re-layouts  6.88 us (4%)
  other arithmetic  5.52 us (3%)
    pallas_call x10, Pallas kernels, call(): pl.pallas_call(kernel, grid_spec=pltpu.PrefetchScalarGridSpec(num_scalar_...  60.5 us
    ppermute x6, waiting for transfers between devices, along(): return lax.ppermute(value, ('zh', 'y', 'x'), pairs)  19 us
    ppermute x11, starting transfers between devices, away(): return lax.ppermute(value, axis, [(i, (i + shift) % 4) for i in range(4)])  15.4 us
    ppermute x9, starting transfers between devices, swap(): return lax.ppermute(value, axis, [(0, 1), (1, 0)])  12.6 us
    ppermute x6, starting transfers between devices, along(): return lax.ppermute(value, ('zh', 'y', 'x'), pairs)  11 us
    all_to_all x1, starting transfers between devices, per_device(): lax.all_to_all(mine.reshape(16 * 144, HALF), ('y', 'x'), 0, 0, tiled=True)  7.04 us
    ppermute x9, waiting for transfers between devices, swap(): return lax.ppermute(value, axis, [(0, 1), (1, 0)])  6 us
    unnamed x39, local copies, waits for them, and re-layouts  5.22 us
  transfers between devices with their start and end apart: 32, of which 14 were waited for; matrix products, arithmetic and copies ran while one was open for 3% of the time, Pallas kernels for 29%

profile of v5, /device:TPU:32, one launch (start us, length us, event | category | flops | bytes accessed | tf_op | source)
XLA Modules:
  0.0 171.5 jit_solution(4580811947060964367)
XLA Ops:
  1.3 4.7 %factors.1 = (f32[4,4,144,128]{3,2,1,0:T(8,128)}, f32[4,4,144,128]{3,2,1,0:T(8,128)}) custom-call(s32[6]{0:T(128)} %stack.31.where_ref.refs_12_._, bf16[512,4096]{1,0:T(8,128)(2,1)} %refs_4_.5, bf16[512,1280]{1,0:T(8,128)(2,1)} %refs_10_.5), custom_call_target="tpu_custom_call" | custom-call | bytes 262144 | tf_op jit(solution)/shard_map/factors/pallas_call | solution.py:41
  6.1 3.1 %collective-permute-done = f32[4,4,144,128]{3,2,1,0:T(8,128)S(1)} collective-permute-done((f32[4,4,144,128]{3,2,1,0:T(8,128)}, f32[4,4,144,128]{3,2,1,0:T(8,128)S(1)}, u32[]{:S(2)}, u32[]{:S(2)}) %collective-permute-start) | collective-permute-done | bytes 1179680 | tf_op jit(solution)/shard_map/factors/ppermute | solution.py:388
  12.1 7.0 %all-to-all-start = ((f32[16,144,128]{2,1,0:T(8,128)}), f32[16,144,128]{2,1,0:T(8,128)S(1)}, u32[]{:S(2)}, u32[]{:S(2)}) async-start(f32[16,144,128]{2,1,0:T(8,128)} %bitcast.20), calls=%async_computation | async-start | bytes 2359296 | tf_op jit(solution)/shard_map/factors/all_to_all | solution.py:410
  19.2 5.4 %product.2 = (f32[2,640,128]{2,1,0:T(8,128)}, f32[2,640,128]{2,1,0:T(8,128)}, f32[2,640,128]{2,1,0:T(8,128)}, f32[2,640,128]{2,1,0:T(8,128)}) custom-call(s32[6]{0:T(128)} %stack.31.where_ref.refs_12_._, bf16[512,4096]{1,0:T(8,128)(2,1)} %refs_4_.5, bf16[512,4096]{1,0:T(8,128)(2,1)} %refs_4_.5, bf16[512,4096]{1,0:T(8,128)(2,1)} %refs_4_.5, ...), custom_call_target="tpu_custom_call" | custom-call | bytes 262144 | tf_op jit(solution)/shard_map/product/pallas_call | solution.py:41
  24.5 3.1 %collective-permute-start.5 = (f32[2,640,128]{2,1,0:T(8,128)}, f32[2,640,128]{2,1,0:T(8,128)S(1)}, u32[]{:S(2)}, u32[]{:S(2)}) collective-permute-start(f32[2,640,128]{2,1,0:T(8,128)} %get-tuple-element.56), channel_id=1, source_target_pairs={{0,24},{8,0},{16,8},{24,16},{1,25},{9,1},{17,9},{25,17},{2,26},{10... | collective-permute-start | bytes 1966088 | tf_op jit(solution)/shard_map/product/ppermute | solution.py:394
  30.9 7.7 %product.3 = (f32[4,640,128]{2,1,0:T(8,128)}, f32[4,640,128]{2,1,0:T(8,128)}, f32[4,640,128]{2,1,0:T(8,128)}, f32[4,640,128]{2,1,0:T(8,128)}) custom-call(s32[6]{0:T(128)} %stack.31.where_ref.refs_12_._, bf16[512,4096]{1,0:T(8,128)(2,1)} %refs_4_.5, bf16[512,4096]{1,0:T(8,128)(2,1)} %refs_4_.5, bf16[512,4096]{1,0:T(8,128)(2,1)} %refs_4_.5, ...), custom_call_target="tpu_custom_call" | custom-call | bytes 262144 | tf_op jit(solution)/shard_map/product/pallas_call | solution.py:41
  40.0 6.4 %collective-permute-start.3 = (f32[144,128]{1,0:T(8,128)S(1)}, f32[144,128]{1,0:T(8,128)S(1)}, u32[]{:S(2)}, u32[]{:S(2)}) collective-permute-start(f32[144,128]{1,0:T(8,128)S(1)} %sum_factors.3.refs_12_), channel_id=1, source_target_pairs={{0,128},{128,0},{1,129},{129,1},{2,130},{130,2},{3,131},{131,3},{4... | collective-permute-start | bytes 221192 | tf_op jit(solution)/shard_map/sum_factors/ppermute | solution.py:388
  46.3 5.3 %sum_factors.4 = (f32[4,640,128]{2,1,0:T(8,128)}, f32[4,640,128]{2,1,0:T(8,128)}) custom-call(s32[6]{0:T(128)} %stack.31.where_ref.refs_12_._, bf16[512,4096]{1,0:T(8,128)(2,1)} %refs_4_.5, bf16[512,4096]{1,0:T(8,128)(2,1)} %refs_4_.5, bf16[512,4096]{1,0:T(8,128)(2,1)} %refs_4_.5, bf16[512,4096]{1,0:T(8,128)(2,1)} %refs_4_.5, bf16[512,4096]{1,0:T(8,128)(2,1)} %refs_4_.5, ...), custom_call_target="tpu_custom_call" | custom-call | bytes 262144 | tf_op jit(solution)/shard_map/sum_factors/pallas_call | solution.py:41
  53.9 4.5 %sum_factors.5 = (f32[4,640,128]{2,1,0:T(8,128)}, f32[4,640,128]{2,1,0:T(8,128)}, f32[4,640,128]{2,1,0:T(8,128)}, f32[4,640,128]{2,1,0:T(8,128)}) custom-call(s32[6]{0:T(128)} %stack.31.where_ref.refs_12_._, f32[4,640,128]{2,1,0:T(8,128)} %get-tuple-element.52.refs_0_, ...), custom_call_target="tpu_custom_call", output_to_operand_aliasing={{0}: (1, {}), {1}: (2, {}), {2}: (3, {}), {3}: (4, {})} | custom-call | bytes 262144 | tf_op jit(solution)/shard_map/sum_factors/pallas_call | solution.py:194
  68.9 3.2 %collective-permute-start.15 = (f32[4,640,128]{2,1,0:T(8,128)}, f32[4,640,128]{2,1,0:T(8,128)}, u32[]{:S(2)}, u32[]{:S(2)}) collective-permute-start(f32[4,640,128]{2,1,0:T(8,128)} %get-tuple-element.71), channel_id=1, source_target_pairs={{0,96},{32,0},{64,32},{96,64},{1,97},{33,1},{65,33},{97,65},{2,98}... | collective-permute-start | bytes 3932168 | tf_op jit(solution)/shard_map/roots/ppermute | solution.py:394
  73.5 21.3 %roots.1.refs_6_ = bf16[2,256,256]{2,1,0:T(8,128)(2,1)S(1)} custom-call(s32[6]{0:T(128)S(1)} %copy-done.4, f32[192,128]{1,0:T(8,128)S(1)} %constant_dynamic-update-slice_fusion.p0, f32[192,128]{1,0:T(8,128)S(1)} %collective-permute-done.9.p1, f32[192,128]{1,0:T(8,128)S(1)} %collective-permute-done.10.p2, f32[192,128]{1,0:T(8,128)S(1)} %collective-permute-done.11.p3, ...), custom_call_target="tpu_custom_call" | custom-call | bytes 262144 | tf_op jit(solution)/shard_map/roots/pallas_call | solution.py:41
  95.6 4.4 %all-to-all-start.1 = ((bf16[4,256,256]{2,1,0:T(8,128)(2,1)}), bf16[4,256,256]{2,1,0:T(8,128)(2,1)S(1)}, u32[]{:S(2)}, u32[]{:S(2)}) async-start(bf16[4,256,256]{2,1,0:T(8,128)(2,1)} %broadcast_in_dim.3), calls=%async_computation.1 | async-start | bytes 1048576 | tf_op jit(solution)/shard_map/roots/all_to_all | solution.py:437
  101.6 6.4 %route.2 = (f32[640,128]{1,0:T(8,128)}, f32[640,128]{1,0:T(8,128)}, f32[640,128]{1,0:T(8,128)}, f32[640,128]{1,0:T(8,128)}, f32[640,128]{1,0:T(8,128)}, /*index=...) custom-call(s32[6]{0:T(128)} %stack.31.where_ref.refs_12_._, ...), custom_call_target="tpu_custom_call" | custom-call | bytes 262144 | tf_op jit(solution)/shard_map/route/pallas_call | solution.py:41
  108.0 3.5 %collective-permute-start.16 = (f32[640,128]{1,0:T(8,128)}, f32[640,128]{1,0:T(8,128)S(1)}, u32[]{:S(2)}, u32[]{:S(2)}) collective-permute-start(f32[640,128]{1,0:T(8,128)} %get-tuple-element.74), channel_id=1, source_target_pairs={{0,16},{8,24},{16,0},{24,8},{32,48},{40,56},{48,32},{56,40},{64,80... | collective-permute-start | bytes 983048 | tf_op jit(solution)/shard_map/route/ppermute | solution.py:257
  112.1 2.7 %collective-permute-start.18 = (f32[640,128]{1,0:T(8,128)}, f32[640,128]{1,0:T(8,128)S(1)}, u32[]{:S(2)}, u32[]{:S(2)}) collective-permute-start(f32[640,128]{1,0:T(8,128)} %get-tuple-element.76), channel_id=1, source_target_pairs={{0,24},{8,0},{16,8},{24,16},{32,56},{40,32},{48,40},{56,48},{64,88... | collective-permute-start | bytes 983048 | tf_op jit(solution)/shard_map/route/ppermute | solution.py:257
  114.8 5.6 %collective-permute-done.16.refs_0_ = f32[640,128]{1,0:T(8,128)S(1)} collective-permute-done((f32[640,128]{1,0:T(8,128)}, f32[640,128]{1,0:T(8,128)S(1)}, u32[]{:S(2)}, u32[]{:S(2)}) %collective-permute-start.16) | collective-permute-done | bytes 327712 | tf_op jit(solution)/shard_map/route/ppermute | solution.py:257
  120.4 4.9 %collective-permute-done.17.refs_1_ = f32[640,128]{1,0:T(8,128)S(1)} collective-permute-done((f32[640,128]{1,0:T(8,128)}, f32[640,128]{1,0:T(8,128)S(1)}, u32[]{:S(2)}, u32[]{:S(2)}) %collective-permute-start.17) | collective-permute-done | bytes 327712 | tf_op jit(solution)/shard_map/route/ppermute | solution.py:257
  126.3 2.7 %route.3.refs_4_ = f32[640,128]{1,0:T(8,128)} custom-call(s32[6]{0:T(128)} %stack.31.where_ref.refs_12_._, f32[640,128]{1,0:T(8,128)} %copy-done.12, f32[640,128]{1,0:T(8,128)} %copy-done.13, f32[640,128]{1,0:T(8,128)} %copy-done.14, f32[640,128]{1,0:T(8,128)} %get-tuple-element.77.refs_3_, bf16[1024,256]{1,0:T(8,128)(2,1)} %bitcast.19), custom_call_target="tpu_custom_call" | custom-call | bytes 262144 | tf_op jit(solution)/shard_map/route/pallas_call | solution.py:41
  133.3 5.3 %collective-permute-start.23 = (f32[640,128]{1,0:T(8,128)}, f32[640,128]{1,0:T(8,128)S(1)}, u32[]{:S(2)}, u32[]{:S(2)}) collective-permute-start(f32[640,128]{1,0:T(8,128)} %route.3.refs_4_), channel_id=1, source_target_pairs={{0,128},{128,0},{1,129},{129,1},{2,130},{130,2},{3,131},{131,3},{4... | collective-permute-start | bytes 983048 | tf_op jit(solution)/shard_map/finish/ppermute | solution.py:388
  141.3 6.6 %collective-permute-done.21.refs_1_ = f32[640,128]{1,0:T(8,128)S(1)} collective-permute-done((f32[640,128]{1,0:T(8,128)}, f32[640,128]{1,0:T(8,128)S(1)}, u32[]{:S(2)}, u32[]{:S(2)}) %collective-permute-start.21) | collective-permute-done | bytes 327712 | tf_op jit(solution)/shard_map/route/ppermute | solution.py:257
  149.4 2.7 %finish.2 = f32[640,128]{1,0:T(8,128)} custom-call(s32[6]{0:T(128)} %stack.31.where_ref.refs_12_._, f32[640,128]{1,0:T(8,128)} %copy-done.15, f32[640,128]{1,0:T(8,128)} %copy-done.16, f32[640,128]{1,0:T(8,128)} %copy-done.17, f32[640,128]{1,0:T(8,128)} %get-tuple-element.83.refs_3_, f32[640,128]{1,0:T(8,128)} %route.3.refs_4_), custom_call_target="tpu_custom_call" | custom-call | bytes 262144 | tf_op jit(solution)/shard_map/finish/pallas_call | solution.py:41
  158.5 5.1 %collective-permute-done.24.beside_ref = f32[640,128]{1,0:T(8,128)S(1)} collective-permute-done((f32[640,128]{1,0:T(8,128)S(1)}, f32[640,128]{1,0:T(8,128)S(1)}, u32[]{:S(2)}, u32[]{:S(2)}) %collective-permute-start.24) | collective-permute-done | bytes 327712 | tf_op jit(solution)/shard_map/finish/ppermute | solution.py:472
  163.7 4.1 %collective-permute-done.27 = bf16[256,256]{1,0:T(8,128)(2,1)S(1)} collective-permute-done((bf16[256,256]{1,0:T(8,128)(2,1)S(1)}, bf16[256,256]{1,0:T(8,128)(2,1)S(1)}, u32[]{:S(2)}, u32[]{:S(2)}) %collective-permute-start.27) | collective-permute-done | bytes 131104 | tf_op jit(solution)/shard_map/left_root/ppermute | solution.py:467
  167.9 3.6 %finish.3 = (bf16[64,1280]{1,0:T(8,128)(2,1)}, bf16[2,256,256]{2,1,0:T(8,128)(2,1)}) custom-call(s32[16]{0:T(128)S(1)} %concatenate.8.where_ref, f32[640,128]{1,0:T(8,128)S(1)} %add.52.mine_ref, f32[640,128]{1,0:T(8,128)S(1)} %collective-permute-done.24.beside_ref, f32[640,128]{1,0:T(8,128)S(1)} %collective-permute-done.25.mine_other, ...), custom_call_target="tpu_custom_call" | custom-call | bytes 262144 | tf_op jit(solution)/shard_map/finish/pallas_call | solution.py:41
  (102 shorter events, 41.0 us)
Async XLA Ops:
  9.1 10.1 %collective-permute-start.1 = (bf16[512,4096]{1,0:T(8,128)(2,1)}, bf16[512,4096]{1,0:T(8,128)(2,1)}, u32[]{:S(2)}, u32[]{:S(2)}) collective-permute-start(bf16[512,4096]{1,0:T(8,128)(2,1)} %refs_4_.5), channel_id=1, source_target_pairs={{0,4},{4,0},{1,5},{5,1},{2,6},{6,2},{3,7},{7,3},{8,12},{12,8},{9,1... | collective-permute-start | bytes 12582920 | tf_op jit(solution)/shard_map/exchange/ppermute | solution.py:388
  9.3 9.9 %collective-permute-start.2 = (bf16[512,1280]{1,0:T(8,128)(2,1)S(1)}, bf16[512,1280]{1,0:T(8,128)(2,1)}, u32[]{:S(2)}, u32[]{:S(2)}) collective-permute-start(bf16[512,1280]{1,0:T(8,128)(2,1)S(1)} %copy-done.5), channel_id=1, source_target_pairs={{0,4},{4,0},{1,5},{5,1},{2,6},{6,2},{3,7},{7,3},{8,12},{12,8},{9,1... | collective-permute-start | bytes 3932168 | tf_op jit(solution)/shard_map/exchange/ppermute | solution.py:388
  12.1 27.2 %all-to-all-start = ((f32[16,144,128]{2,1,0:T(8,128)}), f32[16,144,128]{2,1,0:T(8,128)S(1)}, u32[]{:S(2)}, u32[]{:S(2)}) async-start(f32[16,144,128]{2,1,0:T(8,128)} %bitcast.20), calls=%async_computation | async-start | bytes 2359296 | tf_op jit(solution)/shard_map/factors/all_to_all | solution.py:410
  24.5 28.0 %collective-permute-start.5 = (f32[2,640,128]{2,1,0:T(8,128)}, f32[2,640,128]{2,1,0:T(8,128)S(1)}, u32[]{:S(2)}, u32[]{:S(2)}) collective-permute-start(f32[2,640,128]{2,1,0:T(8,128)} %get-tuple-element.56), channel_id=1, source_target_pairs={{0,24},{8,0},{16,8},{24,16},{1,25},{9,1},{17,9},{25,17},{2,26},{10... | collective-permute-start | bytes 1966088 | tf_op jit(solution)/shard_map/product/ppermute | solution.py:394
  27.7 24.9 %collective-permute-start.6 = (f32[2,640,128]{2,1,0:T(8,128)}, f32[2,640,128]{2,1,0:T(8,128)S(1)}, u32[]{:S(2)}, u32[]{:S(2)}) collective-permute-start(f32[2,640,128]{2,1,0:T(8,128)} %get-tuple-element.57), channel_id=1, source_target_pairs={{0,32},{32,64},{64,96},{96,0},{1,33},{33,65},{65,97},{97,1},{2,34}... | collective-permute-start | bytes 1966088 | tf_op jit(solution)/shard_map/product/ppermute | solution.py:394
  29.1 23.5 %collective-permute-start.7 = (f32[2,640,128]{2,1,0:T(8,128)}, f32[2,640,128]{2,1,0:T(8,128)S(1)}, u32[]{:S(2)}, u32[]{:S(2)}) collective-permute-start(f32[2,640,128]{2,1,0:T(8,128)} %get-tuple-element.58), channel_id=1, source_target_pairs={{0,96},{32,0},{64,32},{96,64},{1,97},{33,1},{65,33},{97,65},{2,98}... | collective-permute-start | bytes 1966088 | tf_op jit(solution)/shard_map/product/ppermute | solution.py:394
  30.9 21.7 %collective-permute-start.4 = (f32[2,640,128]{2,1,0:T(8,128)}, f32[2,640,128]{2,1,0:T(8,128)}, u32[]{:S(2)}, u32[]{:S(2)}) collective-permute-start(f32[2,640,128]{2,1,0:T(8,128)} %get-tuple-element.49.refs_12_), channel_id=1, source_target_pairs={{0,8},{8,16},{16,24},{24,0},{1,9},{9,17},{17,25},{25,1},{2,10},{10... | collective-permute-start | bytes 1966088 | tf_op jit(solution)/shard_map/product/ppermute | solution.py:394
  40.0 11.7 %collective-permute-start.3 = (f32[144,128]{1,0:T(8,128)S(1)}, f32[144,128]{1,0:T(8,128)S(1)}, u32[]{:S(2)}, u32[]{:S(2)}) collective-permute-start(f32[144,128]{1,0:T(8,128)S(1)} %sum_factors.3.refs_12_), channel_id=1, source_target_pairs={{0,128},{128,0},{1,129},{129,1},{2,130},{130,2},{3,131},{131,3},{4... | collective-permute-start | bytes 221192 | tf_op jit(solution)/shard_map/sum_factors/ppermute | solution.py:388
  62.4 37.6 %collective-permute-start.12 = (f32[4,640,128]{2,1,0:T(8,128)}, f32[4,640,128]{2,1,0:T(8,128)S(1)}, u32[]{:S(2)}, u32[]{:S(2)}) collective-permute-start(f32[4,640,128]{2,1,0:T(8,128)} %get-tuple-element.67._), channel_id=1, source_target_pairs={{0,8},{8,16},{16,24},{24,0},{1,9},{9,17},{17,25},{25,1},{2,10},{10... | collective-permute-start | bytes 3932168 | tf_op jit(solution)/shard_map/roots/ppermute | solution.py:394
  63.1 36.9 %collective-permute-start.13 = (f32[4,640,128]{2,1,0:T(8,128)}, f32[4,640,128]{2,1,0:T(8,128)S(1)}, u32[]{:S(2)}, u32[]{:S(2)}) collective-permute-start(f32[4,640,128]{2,1,0:T(8,128)} %get-tuple-element.68), channel_id=1, source_target_pairs={{0,24},{8,0},{16,8},{24,16},{1,25},{9,1},{17,9},{25,17},{2,26},{10... | collective-permute-start | bytes 3932168 | tf_op jit(solution)/shard_map/roots/ppermute | solution.py:394
  68.9 32.2 %collective-permute-start.14 = (f32[4,640,128]{2,1,0:T(8,128)}, f32[4,640,128]{2,1,0:T(8,128)}, u32[]{:S(2)}, u32[]{:S(2)}) collective-permute-start(f32[4,640,128]{2,1,0:T(8,128)} %get-tuple-element.70), channel_id=1, source_target_pairs={{0,32},{32,64},{64,96},{96,0},{1,33},{33,65},{65,97},{97,1},{2,34}... | collective-permute-start | bytes 3932168 | tf_op jit(solution)/shard_map/roots/ppermute | solution.py:394
  68.9 32.2 %collective-permute-start.15 = (f32[4,640,128]{2,1,0:T(8,128)}, f32[4,640,128]{2,1,0:T(8,128)}, u32[]{:S(2)}, u32[]{:S(2)}) collective-permute-start(f32[4,640,128]{2,1,0:T(8,128)} %get-tuple-element.71), channel_id=1, source_target_pairs={{0,96},{32,0},{64,32},{96,64},{1,97},{33,1},{65,33},{97,65},{2,98}... | collective-permute-start | bytes 3932168 | tf_op jit(solution)/shard_map/roots/ppermute | solution.py:394
  95.6 19.1 %all-to-all-start.1 = ((bf16[4,256,256]{2,1,0:T(8,128)(2,1)}), bf16[4,256,256]{2,1,0:T(8,128)(2,1)S(1)}, u32[]{:S(2)}, u32[]{:S(2)}) async-start(bf16[4,256,256]{2,1,0:T(8,128)(2,1)} %broadcast_in_dim.3), calls=%async_computation.1 | async-start | bytes 1048576 | tf_op jit(solution)/shard_map/roots/all_to_all | solution.py:437
  108.0 12.4 %collective-permute-start.16 = (f32[640,128]{1,0:T(8,128)}, f32[640,128]{1,0:T(8,128)S(1)}, u32[]{:S(2)}, u32[]{:S(2)}) collective-permute-start(f32[640,128]{1,0:T(8,128)} %get-tuple-element.74), channel_id=1, source_target_pairs={{0,16},{8,24},{16,0},{24,8},{32,48},{40,56},{48,32},{56,40},{64,80... | collective-permute-start | bytes 983048 | tf_op jit(solution)/shard_map/route/ppermute | solution.py:257
  111.5 13.8 %collective-permute-start.17 = (f32[640,128]{1,0:T(8,128)}, f32[640,128]{1,0:T(8,128)S(1)}, u32[]{:S(2)}, u32[]{:S(2)}) collective-permute-start(f32[640,128]{1,0:T(8,128)} %get-tuple-element.75), channel_id=1, source_target_pairs={{0,8},{8,16},{16,24},{24,0},{32,40},{40,48},{48,56},{56,32},{64,72... | collective-permute-start | bytes 983048 | tf_op jit(solution)/shard_map/route/ppermute | solution.py:257
  112.1 13.5 %collective-permute-start.18 = (f32[640,128]{1,0:T(8,128)}, f32[640,128]{1,0:T(8,128)S(1)}, u32[]{:S(2)}, u32[]{:S(2)}) collective-permute-start(f32[640,128]{1,0:T(8,128)} %get-tuple-element.76), channel_id=1, source_target_pairs={{0,24},{8,0},{16,8},{24,16},{32,56},{40,32},{48,40},{56,48},{64,88... | collective-permute-start | bytes 983048 | tf_op jit(solution)/shard_map/route/ppermute | solution.py:257
  129.1 9.6 %collective-permute-start.19 = (bf16[4,256,256]{2,1,0:T(8,128)(2,1)}, bf16[4,256,256]{2,1,0:T(8,128)(2,1)S(1)}, u32[]{:S(2)}, u32[]{:S(2)}) collective-permute-start(bf16[4,256,256]{2,1,0:T(8,128)(2,1)} %copy-done.6), channel_id=1, source_target_pairs={{0,4},{4,0},{1,5},{5,1},{2,6},{6,2},{3,7},{7,3},{8,12},{12,8},{9,1... | collective-permute-start | bytes 1572872 | tf_op jit(solution)/shard_map/share/ppermute | solution.py:388
  129.1 12.3 %collective-permute-start.20 = (f32[640,128]{1,0:T(8,128)}, f32[640,128]{1,0:T(8,128)S(1)}, u32[]{:S(2)}, u32[]{:S(2)}) collective-permute-start(f32[640,128]{1,0:T(8,128)} %get-tuple-element.79), channel_id=1, source_target_pairs={{0,64},{8,72},{16,80},{24,88},{32,96},{40,104},{48,112},{56,120},{... | collective-permute-start | bytes 983048 | tf_op jit(solution)/shard_map/route/ppermute | solution.py:257
  130.1 17.8 %collective-permute-start.21 = (f32[640,128]{1,0:T(8,128)}, f32[640,128]{1,0:T(8,128)S(1)}, u32[]{:S(2)}, u32[]{:S(2)}) collective-permute-start(f32[640,128]{1,0:T(8,128)} %get-tuple-element.81), channel_id=1, source_target_pairs={{0,32},{8,40},{16,48},{24,56},{32,64},{40,72},{48,80},{56,88},{64,... | collective-permute-start | bytes 983048 | tf_op jit(solution)/shard_map/route/ppermute | solution.py:257
  132.1 15.8 %collective-permute-start.22 = (f32[640,128]{1,0:T(8,128)}, f32[640,128]{1,0:T(8,128)S(1)}, u32[]{:S(2)}, u32[]{:S(2)}) collective-permute-start(f32[640,128]{1,0:T(8,128)} %get-tuple-element.82), channel_id=1, source_target_pairs={{0,96},{8,104},{16,112},{24,120},{32,0},{40,8},{48,16},{56,24},{64... | collective-permute-start | bytes 983048 | tf_op jit(solution)/shard_map/route/ppermute | solution.py:257
  133.3 20.5 %collective-permute-start.23 = (f32[640,128]{1,0:T(8,128)}, f32[640,128]{1,0:T(8,128)S(1)}, u32[]{:S(2)}, u32[]{:S(2)}) collective-permute-start(f32[640,128]{1,0:T(8,128)} %route.3.refs_4_), channel_id=1, source_target_pairs={{0,128},{128,0},{1,129},{129,1},{2,130},{130,2},{3,131},{131,3},{4... | collective-permute-start | bytes 983048 | tf_op jit(solution)/shard_map/finish/ppermute | solution.py:388
  154.9 8.7 %collective-permute-start.24 = (f32[640,128]{1,0:T(8,128)S(1)}, f32[640,128]{1,0:T(8,128)S(1)}, u32[]{:S(2)}, u32[]{:S(2)}) collective-permute-start(f32[640,128]{1,0:T(8,128)S(1)} %add.52.mine_ref), channel_id=1, source_target_pairs={{0,8},{8,0},{16,24},{24,16},{1,9},{9,1},{17,25},{25,17},{2,10},{10... | collective-permute-start | bytes 983048 | tf_op jit(solution)/shard_map/finish/ppermute | solution.py:472
  157.1 10.7 %collective-permute-start.27 = (bf16[256,256]{1,0:T(8,128)(2,1)S(1)}, bf16[256,256]{1,0:T(8,128)(2,1)S(1)}, u32[]{:S(2)}, u32[]{:S(2)}) collective-permute-start(bf16[256,256]{1,0:T(8,128)(2,1)S(1)} %dynamic-slice_bitcast_fusion), channel_id=1, source_target_pairs={{0,1},{32,33},{65,66},{97,98},{130,131},{162,163},{195,192},{227,2... | collective-permute-start | bytes 393224 | tf_op jit(solution)/shard_map/left_root/ppermute | solution.py:467
  158.4 9.5 %collective-permute-start.25 = (f32[640,128]{1,0:T(8,128)S(1)}, f32[640,128]{1,0:T(8,128)S(1)}, u32[]{:S(2)}, u32[]{:S(2)}) collective-permute-start(f32[640,128]{1,0:T(8,128)S(1)} %add.52.mine_ref), channel_id=1, source_target_pairs={{0,4},{4,0},{1,5},{5,1},{2,6},{6,2},{3,7},{7,3},{8,12},{12,8},{9,1... | collective-permute-start | bytes 983048 | tf_op jit(solution)/shard_map/finish/ppermute | solution.py:388
  (27 other events, 148.0 us)

commit v6 on v5

--- a/solution.py
+++ b/solution.py
@@ -236,15 +236,6 @@
     return list(outs[:4]), list(outs[4:])
 
 
-def sum_kernel(_, *refs):
-    refs[5][...] = (refs[3][...] + refs[0][...]) + (refs[1][...] + refs[2][...])
-
-
-def sum_four(where, parts, earlier):
-    shape = jax.ShapeDtypeStruct(parts[0].shape, F32)
-    return call(sum_kernel, (1,), where, [whole(shape)] * 4 + [ANY], whole(shape), shape, (*parts, earlier))
-
-
 def along(value, shift, keep):
     if shift == 0:
         return value
@@ -270,57 +261,54 @@
     return call(fold_kernel, (1,), where, [whole(parts)], whole(shape), shape, (parts,), limit=16)
 
 
-def root_kernel(where_ref, p0, p1, p2, p3, _, out_ref, block_ref, last):
-    core = where_ref[1]
+def root_kernel(where_ref, p0, p1, p2, p3, mine_ref, other_ref, _, out_ref, summed_ref, root_ref):
+    core, x, y = where_ref[1], where_ref[3], where_ref[4]
     for shift, piece in enumerate((p0, p1, p2, p3)):
-        place = lax.rem(where_ref[4] + 4 - shift, 4)
+        place = lax.rem(y + 4 - shift, 4)
         first, second = at(place * 32, 32, 32), at(HALF + place * 32, 32, 32)
-        block_ref[first, :HALF] = piece[0:32]
-        block_ref[first, HALF:] = piece[32:64]
-        block_ref[second, HALF:] = piece[64:96]
-        for half, wanted in ((0, core == 0), (1, core == 1)):
-
-            @pl.when(wanted)
-            def _(half=half, piece=piece, place=place, first=first, second=second):
-                start = 96 if half == 0 else 144
-                last[first, :HALF] = piece[start : start + 32]
-                last[at(place * 16, 16, 16), HALF:] = piece[start + 32 : start + 48]
-                start = 240 - start
-                last[second, HALF:] = piece[start : start + 32]
-                last[at(64 + place * 16, 16, 16), HALF:] = piece[start + 32 : start + 48]
-
-    block_ref[HALF:, :HALF] = block_ref[:HALF, HALF:].T
-    last[HALF:, :HALF] = last[:HALF, HALF:].T
+
+        @pl.when(y < 3)
+        def _(piece=piece, first=first, second=second):
+            summed_ref[first, :HALF] = piece[0:32]
+            summed_ref[first, HALF:] = piece[32:64]
+            summed_ref[second, HALF:] = piece[64:96]
+
+        for half in range(2):
+
+            @pl.when(jnp.logical_and(y == 3, core == half))
+            def _(half=half, shift=shift, place=place, first=first, second=second):
+                upper, lower = (mine_ref, other_ref) if half == 0 else (other_ref, mine_ref)
+                tile, corner = slice(shift * 48, shift * 48 + 32), slice(shift * 48 + 32, shift * 48 + 48)
+                summed_ref[first, :HALF] = upper[tile]
+                summed_ref[at(place * 16, 16, 16), HALF:] = upper[corner]
+                summed_ref[second, HALF:] = lower[tile]
+                summed_ref[at(64 + place * 16, 16, 16), HALF:] = lower[corner]
+
+    summed_ref[HALF:, :HALF] = summed_ref[:HALF, HALF:].T
     row = lax.broadcasted_iota(jnp.int32, (BS, BS), 0)
     col = lax.broadcasted_iota(jnp.int32, (BS, BS), 1)
     identity = jnp.where(row == col, 1.0, 0.0).astype(F32)
     mul = functools.partial(jnp.dot, precision=HIGHEST, preferred_element_type=F32)
-
-    def start(summed):
-        factor = summed * (1.0 / TOKENS) + DAMPING * identity
-        norm = jnp.sqrt(jnp.sum(factor * factor, keepdims=True))
-        current = factor / norm
-        step = 1.5 * identity - 0.5 * current
-        return norm, mul(current, step), step
-
-    norm_a, cur_a, est_a = start(block_ref[...])
-    norm_b, cur_b, est_b = start(last[...])
+    factor = summed_ref[...] * (1.0 / TOKENS) + DAMPING * identity
+    norm = jnp.sqrt(jnp.sum(factor * factor, keepdims=True))
+    current = factor / norm
+    step = 1.5 * identity - 0.5 * current
 
     def advance(_, carry):
-        cur_a, est_a, cur_b, est_b = carry
-        step_a = 1.5 * identity - 0.5 * mul(est_a, cur_a)
-        step_b = 1.5 * identity - 0.5 * mul(est_b, cur_b)
-        return mul(cur_a, step_a), mul(step_a, est_a), mul(cur_b, step_b), mul(step_b, est_b)
-
-    cur_a, est_a, cur_b, est_b = lax.fori_loop(0, ITERS - 2, advance, (cur_a, est_a, cur_b, est_b))
-    step_a = 1.5 * identity - 0.5 * mul(est_a, cur_a)
-    step_b = 1.5 * identity - 0.5 * mul(est_b, cur_b)
-    out_ref[0] = (mul(step_a, est_a) / jnp.sqrt(norm_a)).astype(BF16)
-    out_ref[1] = (mul(step_b, est_b) / jnp.sqrt(norm_b)).astype(BF16)
-
-
-def two_roots(where, pieces, earlier):
-    shape = jax.ShapeDtypeStruct((2, BS, BS), BF16)
+        current, estimate = carry
+        step = 1.5 * identity - 0.5 * mul(estimate, current)
+        return mul(current, step), mul(step, estimate)
+
+    current, estimate = lax.fori_loop(0, ITERS - 2, advance, (mul(current, step), step))
+    step = 1.5 * identity - 0.5 * mul(estimate, current)
+    root_ref[...] = (mul(step, estimate) / jnp.sqrt(norm)).astype(BF16)
+    slab = root_ref[at(jnp.minimum(jnp.where(y < 3, 96 * y, 64 * x), 160), 96, 32), :]
+    for place in range(16):
+        out_ref[place] = slab
+
+
+def root_slabs(where, pieces, earlier):
+    shape = jax.ShapeDtypeStruct((16, 96, BS), BF16)
     return call(
         root_kernel,
         (1,),
@@ -329,9 +317,18 @@
         whole(shape),
         shape,
         (*pieces, earlier),
-        scratch=[pltpu.VMEM((BS, BS), F32), pltpu.VMEM((BS, BS), F32)],
+        scratch=[pltpu.VMEM((BS, BS), F32), pltpu.VMEM((BS, BS), BF16)],
         limit=32,
     )
+
+
+def thrice(value, root, contract):
+    high = value.astype(BF16)
+    rest = value - high.astype(F32)
+    middle = rest.astype(BF16)
+    low = (rest - middle.astype(F32)).astype(BF16)
+    multiply = functools.partial(lax.dot_general, dimension_numbers=(contract, ((), ())), preferred_element_type=F32)
+    return multiply(high, root) + (multiply(middle, root) + multiply(low, root))
 
 
 def apply_kernel(
@@ -342,16 +339,14 @@
     cols = at(x_low * HALF, HALF)
 
     def side(place, part):
-        return jnp.dot(part, left_ref[at(place * HALF, HALF), cols].astype(F32), precision=HIGHEST, preferred_element_type=F32)
+        return thrice(part, left_ref[0, at(place * HALF, HALF), cols], ((1,), (0,)))
 
     for place, mine, beside in ((core, mine_ref, beside_ref), (1 - core, mine_other, beside_other)):
         left_done[at(place * width, width), :] = side(x_low, mine[...]) + side(1 - x_low, beside[...])
     for block in range(5):
         root = right_ref[block] if block < 4 else last_ref[...]
         span = slice(block * BS, (block + 1) * BS)
-        done[:, span] = lax.dot_general(
-            left_done[span, :], root.astype(F32), (((0,), (0,)), ((), ())), precision=HIGHEST, preferred_element_type=F32
-        )
+        done[:, span] = thrice(left_done[span, :], root, ((0,), (0,)))
     out_ref[...] = (done[at(core * 64, 64, 64), :] * (1.0 / math.sqrt(TOKENS))).astype(BF16)
     kept_ref[...] = jnp.zeros_like(kept_ref)
     count = jnp.int32(0)
@@ -375,7 +370,9 @@
         apply_kernel,
         (1,),
         where,
-        [whole(p) for p in (*pieces, left, inputs, right, last)],
+        [whole(p) for p in pieces]
+        + [pl.BlockSpec((1, BS, BS), lambda i, w: (w[5] * 2 + w[4] // 2, 0, 0))]
+        + [whole(p) for p in (inputs, right, last)],
         [whole(shape), whole(kept)],
         [shape, kept],
         (*pieces, left, inputs, right, last),
@@ -422,30 +419,32 @@
 
     with jax.named_scope("sum_factors"):
         mine = fold(where, mine)
-        home = home_products(where, *inputs, mine)
-        near = list(merge(where, near, came, home[0]))
+        near = list(merge(where, near, came, mine))
+        home = list(home_products(where, *inputs, near[0]))
         mine, near[0] = lax.optimization_barrier((mine + swap(mine, "zh"), near[0]))
-        mine = jnp.concatenate([mine, swap(mine[96:], "c")], axis=0)
         pieces = [away(mine, "y", shift) for shift in range(4)]
 
     with jax.named_scope("roots"):
         pieces[1], pieces[2], pieces[3], near[2], near[3] = lax.optimization_barrier((*pieces[1:], near[2], near[3]))
         passed = [away(near[0], "x", 1), away(near[1], "x", 3), away(near[2], "y", 1), away(near[3], "y", 3)]
-        roots = two_roots(where, pieces, near[0])
-        last_root = roots[1]
-        four = jnp.broadcast_to(roots[0], (4, BS, BS)).reshape(4 * BS, BS)
-        four = lax.all_to_all(four, "x", 0, 0, tiled=True)
+        lasts = jnp.concatenate([v[96:] for v in pieces], axis=0)
+        slabs = root_slabs(where, (*pieces, lasts, swap(lasts, "c")), near[0])
+        slabs, home[0] = lax.optimization_barrier((slabs, home[0]))
+        four = lax.all_to_all(slabs.reshape(16 * 96, BS), ("y", "x"), 0, 0, tiled=True)
 
     with jax.named_scope("route"):
-        other, own = route(where, (home[0], *passed[:2]), (home[1], *passed[2:]), roots)
+        other, own = route(where, (home[0], *passed[:2]), (home[1], *passed[2:]), slabs)
         far_plane = [along(v, shift, False) for v, shift in zip(other, SHIFTS, strict=True)]
         this_plane = [along(v, shift, True) for v, shift in zip(own, SHIFTS, strict=True)]
         four, own[3] = lax.optimization_barrier((four, own[3]))
-        leave = sum_four(where, far_plane, four)
+        far_plane[2], this_plane[1], this_plane[2] = lax.optimization_barrier((far_plane[2], this_plane[1], this_plane[2]))
+        leave = (far_plane[3] + far_plane[0]) + (far_plane[1] + far_plane[2])
         four, leave = lax.optimization_barrier((four, leave))
 
     with jax.named_scope("share"):
-        four = four.reshape(4, BS, BS)
+        slabs = four.reshape(4, 4, 96, BS)
+        four = jnp.concatenate([slabs[0], slabs[1], slabs[2, :, 32:]], axis=1)
+        last_root = jnp.concatenate([slabs[3, 0, :64], slabs[3, 1, :64], slabs[3, 2, :64], slabs[3, 3, 32:]], axis=0)
         other_four = swap(four, "c")
         input_roots = jnp.where(core == 0, four, other_four)
         output_roots = jnp.where(core == 0, other_four, four)
@@ -454,21 +453,13 @@
         came_over = swap(leave, "zh")
 
     with jax.named_scope("left_root"):
-        holder = zh * 2 + y // 2
         left = lax.dynamic_index_in_dim(input_roots, (y % 2) * 2 + x_high, 0, keepdims=False)
         left, this_plane[0] = lax.optimization_barrier((left, this_plane[0]))
-        got = jnp.zeros_like(left)
-        for shift in range(1, 4):
-            pairs = []
-            for a in range(2):
-                for b in range(4):
-                    source = a * 2 + b // 2
-                    pairs.append(((a * 4 + b) * 4 + source, (a * 4 + b) * 4 + (source + shift) % 4))
-            got = got + lax.ppermute(left, ("zh", "y", "mp"), pairs)
-        left = jnp.where(column == holder, left, got)
+        left = jnp.broadcast_to(left, (4, BS, BS)).reshape(4 * BS, BS)
+        left = lax.all_to_all(left, "mp", 0, 0, tiled=True).reshape(4, BS, BS)
 
     with jax.named_scope("finish"):
-        total = sum_four(where, [*this_plane[:3], own[3]], leave) + came_over
+        total = ((own[3] + this_plane[0]) + (this_plane[1] + this_plane[2])) + came_over
         beside = lax.ppermute(total, "x", [(0, 1), (1, 0), (2, 3), (3, 2)])
         pieces = (total, beside, swap(total, "c"), swap(beside, "c"))
         update, kept = apply_roots(jnp.concatenate([places, owners[0]]), pieces, left, input_roots, output_roots, last_root)

time: 172 us -> 169 us (0.983)
  Pallas kernels: 65 us -> 50.8 us
  waiting for transfers between devices: 39.3 us -> 49.8 us
  local copies, waits for them, and re-layouts: 6.88 us -> 3.56 us
  starting transfers between devices: 53.9 us -> 57.2 us
    pallas_call x10 -> x8, Pallas kernels: 60.5 us -> 46.4 us  [call(): pl.pallas_call(kernel, grid_spec=pltpu.PrefetchScalarGridSpec(num_scalar_...]
    ppermute x11, waiting for transfers between devices: 4.37 us -> 15.3 us  [away(): return lax.ppermute(value, axis, [(i, (i + shift) % 4) for i in range(4)])]
    ppermute x9, waiting for transfers between devices: 6 us -> 13.4 us  [swap(): return lax.ppermute(value, axis, [(0, 1), (1, 0)])]
    all_to_all x1 -> x2, starting transfers between devices: 4.4 us -> 10.2 us  [the longest x1 6.13 us: per_device(): left = lax.all_to_all(left, 'mp', 0, 0, tiled=True).reshape(4, BS, BS)]
    ppermute x6, waiting for transfers between devices: 19 us -> 14.8 us  [along(): return lax.ppermute(value, ('zh', 'y', 'x'), pairs)]
    ppermute x3 -> x0, waiting for transfers between devices: 4.12 us -> none  [per_device(): got = got + lax.ppermute(left, ('zh', 'y', 'mp'), pairs)]
    unnamed x39 -> x24, local copies, waits for them, and re-layouts: 5.22 us -> 1.14 us
    ppermute x3 -> x0, starting transfers between devices: 2.62 us -> none  [per_device(): got = got + lax.ppermute(left, ('zh', 'y', 'mp'), pairs)]
  transfers between devices with their start and end apart: 32 -> 30, of which waited for: 14 -> 16; matrix products, arithmetic and copies ran while one was open for 3% -> 3% of each run, Pallas kernels for 29% -> 23%
where the time goes in v6:
time: 169 us; the launch traced here: 167 us
  starting transfers between devices  57.2 us (34%)
  Pallas kernels  50.8 us (30%)
  waiting for transfers between devices  49.8 us (29%)
  other arithmetic  4.91 us (3%)
  local copies, waits for them, and re-layouts  3.56 us (2%)
    pallas_call x8, Pallas kernels, call(): pl.pallas_call(kernel, grid_spec=pltpu.PrefetchScalarGridSpec(num_scalar_...  46.4 us
    ppermute x11, starting transfers between devices, away(): return lax.ppermute(value, axis, [(i, (i + shift) % 4) for i in range(4)])  15.9 us
    ppermute x11, waiting for transfers between devices, away(): return lax.ppermute(value, axis, [(i, (i + shift) % 4) for i in range(4)])  15.3 us
    ppermute x6, waiting for transfers between devices, along(): return lax.ppermute(value, ('zh', 'y', 'x'), pairs)  14.8 us
    ppermute x9, starting transfers between devices, swap(): return lax.ppermute(value, axis, [(0, 1), (1, 0)])  13.6 us
    ppermute x9, waiting for transfers between devices, swap(): return lax.ppermute(value, axis, [(0, 1), (1, 0)])  13.4 us
    ppermute x6, starting transfers between devices, along(): return lax.ppermute(value, ('zh', 'y', 'x'), pairs)  9.05 us
    all_to_all x1, starting transfers between devices, per_device(): lax.all_to_all(mine.reshape(16 * 144, HALF), ('y', 'x'), 0, 0, tiled=True)  7.04 us
  transfers between devices with their start and end apart: 30, of which 16 were waited for; matrix products, arithmetic and copies ran while one was open for 3% of the time, Pallas kernels for 23%

profile of v6, /device:TPU:32, one launch (start us, length us, event | category | flops | bytes accessed | tf_op | source)
XLA Modules:
  0.0 167.2 jit_solution(1328727740980512967)
XLA Ops:
  1.3 4.8 %factors.1 = (f32[4,4,144,128]{3,2,1,0:T(8,128)}, f32[4,4,144,128]{3,2,1,0:T(8,128)}) custom-call(s32[6]{0:T(128)} %stack.31.where_ref.refs_12_._, bf16[512,4096]{1,0:T(8,128)(2,1)} %refs_4_.5, bf16[512,1280]{1,0:T(8,128)(2,1)} %refs_10_.5), custom_call_target="tpu_custom_call" | custom-call | bytes 262144 | tf_op jit(solution)/shard_map/factors/pallas_call | solution.py:41
  6.1 3.1 %collective-permute-done = f32[4,4,144,128]{3,2,1,0:T(8,128)S(1)} collective-permute-done((f32[4,4,144,128]{3,2,1,0:T(8,128)}, f32[4,4,144,128]{3,2,1,0:T(8,128)S(1)}, u32[]{:S(2)}, u32[]{:S(2)}) %collective-permute-start) | collective-permute-done | bytes 1179680 | tf_op jit(solution)/shard_map/factors/ppermute | solution.py:385
  12.1 7.0 %all-to-all-start = ((f32[16,144,128]{2,1,0:T(8,128)}), f32[16,144,128]{2,1,0:T(8,128)S(1)}, u32[]{:S(2)}, u32[]{:S(2)}) async-start(f32[16,144,128]{2,1,0:T(8,128)} %bitcast.27), calls=%async_computation | async-start | bytes 2359296 | tf_op jit(solution)/shard_map/factors/all_to_all | solution.py:407
  19.2 5.4 %product.2 = (f32[2,640,128]{2,1,0:T(8,128)}, f32[2,640,128]{2,1,0:T(8,128)}, f32[2,640,128]{2,1,0:T(8,128)}, f32[2,640,128]{2,1,0:T(8,128)}) custom-call(s32[6]{0:T(128)} %stack.31.where_ref.refs_12_._, bf16[512,4096]{1,0:T(8,128)(2,1)} %refs_4_.5, bf16[512,4096]{1,0:T(8,128)(2,1)} %refs_4_.5, bf16[512,4096]{1,0:T(8,128)(2,1)} %refs_4_.5, ...), custom_call_target="tpu_custom_call" | custom-call | bytes 262144 | tf_op jit(solution)/shard_map/product/pallas_call | solution.py:41
  24.6 3.1 %collective-permute-start.5 = (f32[2,640,128]{2,1,0:T(8,128)}, f32[2,640,128]{2,1,0:T(8,128)S(1)}, u32[]{:S(2)}, u32[]{:S(2)}) collective-permute-start(f32[2,640,128]{2,1,0:T(8,128)} %get-tuple-element.61), channel_id=1, source_target_pairs={{0,24},{8,0},{16,8},{24,16},{1,25},{9,1},{17,9},{25,17},{2,26},{10... | collective-permute-start | bytes 1966088 | tf_op jit(solution)/shard_map/product/ppermute | solution.py:391
  31.0 7.7 %product.3 = (f32[4,640,128]{2,1,0:T(8,128)}, f32[4,640,128]{2,1,0:T(8,128)}, f32[4,640,128]{2,1,0:T(8,128)}, f32[4,640,128]{2,1,0:T(8,128)}) custom-call(s32[6]{0:T(128)} %stack.31.where_ref.refs_12_._, bf16[512,4096]{1,0:T(8,128)(2,1)} %refs_4_.5, bf16[512,4096]{1,0:T(8,128)(2,1)} %refs_4_.5, bf16[512,4096]{1,0:T(8,128)(2,1)} %refs_4_.5, ...), custom_call_target="tpu_custom_call" | custom-call | bytes 262144 | tf_op jit(solution)/shard_map/product/pallas_call | solution.py:41
  40.0 6.4 %collective-permute-start.3 = (f32[144,128]{1,0:T(8,128)S(1)}, f32[144,128]{1,0:T(8,128)S(1)}, u32[]{:S(2)}, u32[]{:S(2)}) collective-permute-start(f32[144,128]{1,0:T(8,128)S(1)} %sum_factors.3.refs_8_), channel_id=1, source_target_pairs={{0,128},{128,0},{1,129},{129,1},{2,130},{130,2},{3,131},{131,3},{4... | collective-permute-start | bytes 221192 | tf_op jit(solution)/shard_map/sum_factors/ppermute | solution.py:385
  51.2 4.4 %sum_factors.4 = (f32[4,640,128]{2,1,0:T(8,128)}, f32[4,640,128]{2,1,0:T(8,128)}, f32[4,640,128]{2,1,0:T(8,128)}, f32[4,640,128]{2,1,0:T(8,128)}) custom-call(s32[6]{0:T(128)} %stack.31.where_ref.refs_12_._, f32[4,640,128]{2,1,0:T(8,128)} %get-tuple-element.57.refs_0_, ...), custom_call_target="tpu_custom_call", output_to_operand_aliasing={{0}: (1, {}), {1}: (2, {}), {2}: (3, {}), {3}: (4, {})} | custom-call | bytes 262144 | tf_op jit(solution)/shard_map/sum_factors/pallas_call | solution.py:194
  64.2 3.2 %collective-permute-start.15 = (f32[4,640,128]{2,1,0:T(8,128)}, f32[4,640,128]{2,1,0:T(8,128)}, u32[]{:S(2)}, u32[]{:S(2)}) collective-permute-start(f32[4,640,128]{2,1,0:T(8,128)} %get-tuple-element.78), channel_id=1, source_target_pairs={{0,96},{32,0},{64,32},{96,64},{1,97},{33,1},{65,33},{97,65},{2,98}... | collective-permute-start | bytes 3932168 | tf_op jit(solution)/shard_map/roots/ppermute | solution.py:391
  67.6 5.6 %sum_factors.5 = (f32[4,640,128]{2,1,0:T(8,128)}, f32[4,640,128]{2,1,0:T(8,128)}) custom-call(s32[6]{0:T(128)} %stack.31.where_ref.refs_12_._, bf16[512,4096]{1,0:T(8,128)(2,1)} %refs_4_.5, bf16[512,4096]{1,0:T(8,128)(2,1)} %refs_4_.5, bf16[512,4096]{1,0:T(8,128)(2,1)} %refs_4_.5, bf16[512,4096]{1,0:T(8,128)(2,1)} %refs_4_.5, bf16[512,4096]{1,0:T(8,128)(2,1)} %refs_4_.5, ...), custom_call_target="tpu_custom_call" | custom-call | bytes 262144 | tf_op jit(solution)/shard_map/sum_factors/pallas_call | solution.py:41
  73.2 13.2 %roots.1.refs_6_ = bf16[16,96,256]{2,1,0:T(8,128)(2,1)} custom-call(s32[6]{0:T(128)S(1)} %copy-done.3, f32[144,128]{1,0:T(8,128)S(1)} %add.56.p0, f32[144,128]{1,0:T(8,128)S(1)} %collective-permute-done.8.p1, f32[144,128]{1,0:T(8,128)S(1)} %collective-permute-done.9.p2, f32[144,128]{1,0:T(8,128)S(1)} %collective-permute-done.10.p3, ...), custom_call_target="tpu_custom_call" | custom-call | bytes 262144 | tf_op jit(solution)/shard_map/roots/pallas_call | solution.py:41
  86.4 4.0 %all-to-all-start.1 = ((bf16[16,96,256]{2,1,0:T(8,128)(2,1)}), bf16[16,96,256]{2,1,0:T(8,128)(2,1)S(1)}, u32[]{:S(2)}, u32[]{:S(2)}) async-start(bf16[16,96,256]{2,1,0:T(8,128)(2,1)} %roots.1.refs_6_), calls=%async_computation.1 | async-start | bytes 1572864 | tf_op jit(solution)/shard_map/roots/all_to_all | solution.py:433
  90.5 5.8 %collective-permute-done.14.refs_4_ = f32[4,640,128]{2,1,0:T(8,128)} collective-permute-done((f32[4,640,128]{2,1,0:T(8,128)}, f32[4,640,128]{2,1,0:T(8,128)}, u32[]{:S(2)}, u32[]{:S(2)}) %collective-permute-start.14) | collective-permute-done | bytes 1310752 | tf_op jit(solution)/shard_map/roots/ppermute | solution.py:391
  96.3 6.1 %collective-permute-done.15.refs_5_ = f32[4,640,128]{2,1,0:T(8,128)} collective-permute-done((f32[4,640,128]{2,1,0:T(8,128)}, f32[4,640,128]{2,1,0:T(8,128)}, u32[]{:S(2)}, u32[]{:S(2)}) %collective-permute-start.15) | collective-permute-done | bytes 1310752 | tf_op jit(solution)/shard_map/roots/ppermute | solution.py:391
  102.4 6.4 %route.1 = (f32[640,128]{1,0:T(8,128)}, f32[640,128]{1,0:T(8,128)}, f32[640,128]{1,0:T(8,128)}, f32[640,128]{1,0:T(8,128)}, f32[640,128]{1,0:T(8,128)}, /*index=...) custom-call(s32[6]{0:T(128)} %stack.31.where_ref.refs_12_._, f32[4,640,128]{2,1,0:T(8,128)} %get-tuple-element.74.refs_0_, ...), custom_call_target="tpu_custom_call" | custom-call | bytes 262144 | tf_op jit(solution)/shard_map/route/pallas_call | solution.py:41
  111.8 3.5 %collective-permute-start.20 = (f32[640,128]{1,0:T(8,128)}, f32[640,128]{1,0:T(8,128)S(1)}, u32[]{:S(2)}, u32[]{:S(2)}) collective-permute-start(f32[640,128]{1,0:T(8,128)} %get-tuple-element.87), channel_id=1, source_target_pairs={{0,96},{8,104},{16,112},{24,120},{32,0},{40,8},{48,16},{56,24},{64... | collective-permute-start | bytes 983048 | tf_op jit(solution)/shard_map/route/ppermute | solution.py:248
  116.7 3.8 %collective-permute-done.19 = f32[640,128]{1,0:T(8,128)S(1)} collective-permute-done((f32[640,128]{1,0:T(8,128)}, f32[640,128]{1,0:T(8,128)S(1)}, u32[]{:S(2)}, u32[]{:S(2)}) %collective-permute-start.19) | collective-permute-done | bytes 327712 | tf_op jit(solution)/shard_map/route/ppermute | solution.py:248
  120.5 3.6 %collective-permute-done.16 = f32[640,128]{1,0:T(8,128)S(1)} collective-permute-done((f32[640,128]{1,0:T(8,128)}, f32[640,128]{1,0:T(8,128)S(1)}, u32[]{:S(2)}, u32[]{:S(2)}) %collective-permute-start.16) | collective-permute-done | bytes 327712 | tf_op jit(solution)/shard_map/route/ppermute | solution.py:248
  124.2 3.1 %collective-permute-done.17 = f32[640,128]{1,0:T(8,128)S(1)} collective-permute-done((f32[640,128]{1,0:T(8,128)}, f32[640,128]{1,0:T(8,128)S(1)}, u32[]{:S(2)}, u32[]{:S(2)}) %collective-permute-start.17) | collective-permute-done | bytes 327712 | tf_op jit(solution)/shard_map/route/ppermute | solution.py:248
  130.4 6.3 %collective-permute-start.23 = (f32[640,128]{1,0:T(8,128)S(1)}, f32[640,128]{1,0:T(8,128)}, u32[]{:S(2)}, u32[]{:S(2)}) collective-permute-start(f32[640,128]{1,0:T(8,128)S(1)} %add_add_fusion.1), channel_id=1, source_target_pairs={{0,128},{128,0},{1,129},{129,1},{2,130},{130,2},{3,131},{131,3},{4... | collective-permute-start | bytes 983048 | tf_op jit(solution)/shard_map/finish/ppermute | solution.py:385
  136.9 3.8 %collective-permute-done.22 = f32[640,128]{1,0:T(8,128)} collective-permute-done((f32[640,128]{1,0:T(8,128)}, f32[640,128]{1,0:T(8,128)}, u32[]{:S(2)}, u32[]{:S(2)}) %collective-permute-start.22) | collective-permute-done | bytes 327712 | tf_op jit(solution)/shard_map/route/ppermute | solution.py:248
  141.5 6.1 %all-to-all-start.2 = ((bf16[4,256,256]{2,1,0:T(8,128)(2,1)}), bf16[4,256,256]{2,1,0:T(8,128)(2,1)S(1)}, u32[]{:S(2)}, u32[]{:S(2)}) async-start(bf16[4,256,256]{2,1,0:T(8,128)(2,1)} %broadcast_in_dim.3), calls=%async_computation.2 | async-start | bytes 1048576 | tf_op jit(solution)/shard_map/left_root/all_to_all | solution.py:459
  147.6 6.9 %collective-permute-done.23 = f32[640,128]{1,0:T(8,128)} collective-permute-done((f32[640,128]{1,0:T(8,128)S(1)}, f32[640,128]{1,0:T(8,128)}, u32[]{:S(2)}, u32[]{:S(2)}) %collective-permute-start.23) | collective-permute-done | bytes 327712 | tf_op jit(solution)/shard_map/finish/ppermute | solution.py:385
  157.2 5.7 %collective-permute-done.24.beside_ref = f32[640,128]{1,0:T(8,128)S(1)} collective-permute-done((f32[640,128]{1,0:T(8,128)S(1)}, f32[640,128]{1,0:T(8,128)S(1)}, u32[]{:S(2)}, u32[]{:S(2)}) %collective-permute-start.24) | collective-permute-done | bytes 327712 | tf_op jit(solution)/shard_map/finish/ppermute | solution.py:463
  (88 shorter events, 37.0 us)
Async XLA Ops:
  9.1 10.0 %collective-permute-start.1 = (bf16[512,4096]{1,0:T(8,128)(2,1)}, bf16[512,4096]{1,0:T(8,128)(2,1)}, u32[]{:S(2)}, u32[]{:S(2)}) collective-permute-start(bf16[512,4096]{1,0:T(8,128)(2,1)} %refs_4_.5), channel_id=1, source_target_pairs={{0,4},{4,0},{1,5},{5,1},{2,6},{6,2},{3,7},{7,3},{8,12},{12,8},{9,1... | collective-permute-start | bytes 12582920 | tf_op jit(solution)/shard_map/exchange/ppermute | solution.py:385
  9.3 9.9 %collective-permute-start.2 = (bf16[512,1280]{1,0:T(8,128)(2,1)S(1)}, bf16[512,1280]{1,0:T(8,128)(2,1)}, u32[]{:S(2)}, u32[]{:S(2)}) collective-permute-start(bf16[512,1280]{1,0:T(8,128)(2,1)S(1)} %copy-done.4), channel_id=1, source_target_pairs={{0,4},{4,0},{1,5},{5,1},{2,6},{6,2},{3,7},{7,3},{8,12},{12,8},{9,1... | collective-permute-start | bytes 3932168 | tf_op jit(solution)/shard_map/exchange/ppermute | solution.py:385
  12.1 27.2 %all-to-all-start = ((f32[16,144,128]{2,1,0:T(8,128)}), f32[16,144,128]{2,1,0:T(8,128)S(1)}, u32[]{:S(2)}, u32[]{:S(2)}) async-start(f32[16,144,128]{2,1,0:T(8,128)} %bitcast.27), calls=%async_computation | async-start | bytes 2359296 | tf_op jit(solution)/shard_map/factors/all_to_all | solution.py:407
  24.6 24.4 %collective-permute-start.5 = (f32[2,640,128]{2,1,0:T(8,128)}, f32[2,640,128]{2,1,0:T(8,128)S(1)}, u32[]{:S(2)}, u32[]{:S(2)}) collective-permute-start(f32[2,640,128]{2,1,0:T(8,128)} %get-tuple-element.61), channel_id=1, source_target_pairs={{0,24},{8,0},{16,8},{24,16},{1,25},{9,1},{17,9},{25,17},{2,26},{10... | collective-permute-start | bytes 1966088 | tf_op jit(solution)/shard_map/product/ppermute | solution.py:391
  27.7 22.3 %collective-permute-start.6 = (f32[2,640,128]{2,1,0:T(8,128)}, f32[2,640,128]{2,1,0:T(8,128)S(1)}, u32[]{:S(2)}, u32[]{:S(2)}) collective-permute-start(f32[2,640,128]{2,1,0:T(8,128)} %get-tuple-element.62), channel_id=1, source_target_pairs={{0,32},{32,64},{64,96},{96,0},{1,33},{33,65},{65,97},{97,1},{2,34}... | collective-permute-start | bytes 1966088 | tf_op jit(solution)/shard_map/product/ppermute | solution.py:391
  29.2 20.9 %collective-permute-start.7 = (f32[2,640,128]{2,1,0:T(8,128)}, f32[2,640,128]{2,1,0:T(8,128)S(1)}, u32[]{:S(2)}, u32[]{:S(2)}) collective-permute-start(f32[2,640,128]{2,1,0:T(8,128)} %get-tuple-element.63), channel_id=1, source_target_pairs={{0,96},{32,0},{64,32},{96,64},{1,97},{33,1},{65,33},{97,65},{2,98}... | collective-permute-start | bytes 1966088 | tf_op jit(solution)/shard_map/product/ppermute | solution.py:391
  31.0 19.1 %collective-permute-start.4 = (f32[2,640,128]{2,1,0:T(8,128)}, f32[2,640,128]{2,1,0:T(8,128)}, u32[]{:S(2)}, u32[]{:S(2)}) collective-permute-start(f32[2,640,128]{2,1,0:T(8,128)} %get-tuple-element.54.refs_12_), channel_id=1, source_target_pairs={{0,8},{8,16},{16,24},{24,0},{1,9},{9,17},{17,25},{25,1},{2,10},{10... | collective-permute-start | bytes 1966088 | tf_op jit(solution)/shard_map/product/ppermute | solution.py:391
  40.0 9.0 %collective-permute-start.3 = (f32[144,128]{1,0:T(8,128)S(1)}, f32[144,128]{1,0:T(8,128)S(1)}, u32[]{:S(2)}, u32[]{:S(2)}) collective-permute-start(f32[144,128]{1,0:T(8,128)S(1)} %sum_factors.3.refs_8_), channel_id=1, source_target_pairs={{0,128},{128,0},{1,129},{129,1},{2,130},{130,2},{3,131},{131,3},{4... | collective-permute-start | bytes 221192 | tf_op jit(solution)/shard_map/sum_factors/ppermute | solution.py:385
  58.7 31.8 %collective-permute-start.12 = (f32[4,640,128]{2,1,0:T(8,128)}, f32[4,640,128]{2,1,0:T(8,128)S(1)}, u32[]{:S(2)}, u32[]{:S(2)}) collective-permute-start(f32[4,640,128]{2,1,0:T(8,128)} %get-tuple-element.71._.refs_12_), channel_id=1, source_target_pairs={{0,8},{8,16},{16,24},{24,0},{1,9},{9,17},{17,25},{25,1},{2,10},{10... | collective-permute-start | bytes 3932168 | tf_op jit(solution)/shard_map/roots/ppermute | solution.py:391
  60.1 30.4 %collective-permute-start.13 = (f32[4,640,128]{2,1,0:T(8,128)}, f32[4,640,128]{2,1,0:T(8,128)}, u32[]{:S(2)}, u32[]{:S(2)}) collective-permute-start(f32[4,640,128]{2,1,0:T(8,128)} %get-tuple-element.75), channel_id=1, source_target_pairs={{0,24},{8,0},{16,8},{24,16},{1,25},{9,1},{17,9},{25,17},{2,26},{10... | collective-permute-start | bytes 3932168 | tf_op jit(solution)/shard_map/roots/ppermute | solution.py:391
  64.2 32.1 %collective-permute-start.14 = (f32[4,640,128]{2,1,0:T(8,128)}, f32[4,640,128]{2,1,0:T(8,128)}, u32[]{:S(2)}, u32[]{:S(2)}) collective-permute-start(f32[4,640,128]{2,1,0:T(8,128)} %get-tuple-element.77), channel_id=1, source_target_pairs={{0,32},{32,64},{64,96},{96,0},{1,33},{33,65},{65,97},{97,1},{2,34}... | collective-permute-start | bytes 3932168 | tf_op jit(solution)/shard_map/roots/ppermute | solution.py:391
  64.2 38.2 %collective-permute-start.15 = (f32[4,640,128]{2,1,0:T(8,128)}, f32[4,640,128]{2,1,0:T(8,128)}, u32[]{:S(2)}, u32[]{:S(2)}) collective-permute-start(f32[4,640,128]{2,1,0:T(8,128)} %get-tuple-element.78), channel_id=1, source_target_pairs={{0,96},{32,0},{64,32},{96,64},{1,97},{33,1},{65,33},{97,65},{2,98}... | collective-permute-start | bytes 3932168 | tf_op jit(solution)/shard_map/roots/ppermute | solution.py:391
  86.4 29.9 %all-to-all-start.1 = ((bf16[16,96,256]{2,1,0:T(8,128)(2,1)}), bf16[16,96,256]{2,1,0:T(8,128)(2,1)S(1)}, u32[]{:S(2)}, u32[]{:S(2)}) async-start(bf16[16,96,256]{2,1,0:T(8,128)(2,1)} %roots.1.refs_6_), calls=%async_computation.1 | async-start | bytes 1572864 | tf_op jit(solution)/shard_map/roots/all_to_all | solution.py:433
  108.8 7.9 %collective-permute-start.18 = (f32[640,128]{1,0:T(8,128)}, f32[640,128]{1,0:T(8,128)S(1)}, u32[]{:S(2)}, u32[]{:S(2)}) collective-permute-start(f32[640,128]{1,0:T(8,128)} %get-tuple-element.85), channel_id=1, source_target_pairs={{0,24},{8,0},{16,8},{24,16},{32,56},{40,32},{48,40},{56,48},{64,88... | collective-permute-start | bytes 983048 | tf_op jit(solution)/shard_map/route/ppermute | solution.py:248
  111.8 8.7 %collective-permute-start.19 = (f32[640,128]{1,0:T(8,128)}, f32[640,128]{1,0:T(8,128)S(1)}, u32[]{:S(2)}, u32[]{:S(2)}) collective-permute-start(f32[640,128]{1,0:T(8,128)} %get-tuple-element.86), channel_id=1, source_target_pairs={{0,32},{8,40},{16,48},{24,56},{32,64},{40,72},{48,80},{56,88},{64,... | collective-permute-start | bytes 983048 | tf_op jit(solution)/shard_map/route/ppermute | solution.py:248
  111.8 8.7 %collective-permute-start.20 = (f32[640,128]{1,0:T(8,128)}, f32[640,128]{1,0:T(8,128)S(1)}, u32[]{:S(2)}, u32[]{:S(2)}) collective-permute-start(f32[640,128]{1,0:T(8,128)} %get-tuple-element.87), channel_id=1, source_target_pairs={{0,96},{8,104},{16,112},{24,120},{32,0},{40,8},{48,16},{56,24},{64... | collective-permute-start | bytes 983048 | tf_op jit(solution)/shard_map/route/ppermute | solution.py:248
  115.3 8.9 %collective-permute-start.16 = (f32[640,128]{1,0:T(8,128)}, f32[640,128]{1,0:T(8,128)S(1)}, u32[]{:S(2)}, u32[]{:S(2)}) collective-permute-start(f32[640,128]{1,0:T(8,128)} %get-tuple-element.83), channel_id=1, source_target_pairs={{0,16},{8,24},{16,0},{24,8},{32,48},{40,56},{48,32},{56,40},{64,80... | collective-permute-start | bytes 983048 | tf_op jit(solution)/shard_map/route/ppermute | solution.py:248
  115.3 12.0 %collective-permute-start.17 = (f32[640,128]{1,0:T(8,128)}, f32[640,128]{1,0:T(8,128)S(1)}, u32[]{:S(2)}, u32[]{:S(2)}) collective-permute-start(f32[640,128]{1,0:T(8,128)} %get-tuple-element.84), channel_id=1, source_target_pairs={{0,8},{8,16},{16,24},{24,0},{32,40},{40,48},{48,56},{56,32},{64,72... | collective-permute-start | bytes 983048 | tf_op jit(solution)/shard_map/route/ppermute | solution.py:248
  128.4 8.2 %collective-permute-start.21 = (bf16[4,256,256]{2,1,0:T(8,128)(2,1)S(1)}, bf16[4,256,256]{2,1,0:T(8,128)(2,1)S(1)}, u32[]{:S(2)}, u32[]{:S(2)}) collective-permute-start(bf16[4,256,256]{2,1,0:T(8,128)(2,1)S(1)} %pad_maximum_fusion), channel_id=1, source_target_pairs={{0,4},{4,0},{1,5},{5,1},{2,6},{6,2},{3,7},{7,3},{8,12},{12,8},{9,1... | collective-permute-start | bytes 1572872 | tf_op jit(solution)/shard_map/share/ppermute | solution.py:385
  128.8 11.9 %collective-permute-start.22 = (f32[640,128]{1,0:T(8,128)}, f32[640,128]{1,0:T(8,128)}, u32[]{:S(2)}, u32[]{:S(2)}) collective-permute-start(f32[640,128]{1,0:T(8,128)} %get-tuple-element.90), channel_id=1, source_target_pairs={{0,64},{8,72},{16,80},{24,88},{32,96},{40,104},{48,112},{56,120},{... | collective-permute-start | bytes 983048 | tf_op jit(solution)/shard_map/route/ppermute | solution.py:248
  130.4 24.2 %collective-permute-start.23 = (f32[640,128]{1,0:T(8,128)S(1)}, f32[640,128]{1,0:T(8,128)}, u32[]{:S(2)}, u32[]{:S(2)}) collective-permute-start(f32[640,128]{1,0:T(8,128)S(1)} %add_add_fusion.1), channel_id=1, source_target_pairs={{0,128},{128,0},{1,129},{129,1},{2,130},{130,2},{3,131},{131,3},{4... | collective-permute-start | bytes 983048 | tf_op jit(solution)/shard_map/finish/ppermute | solution.py:385
  141.5 23.0 %all-to-all-start.2 = ((bf16[4,256,256]{2,1,0:T(8,128)(2,1)}), bf16[4,256,256]{2,1,0:T(8,128)(2,1)S(1)}, u32[]{:S(2)}, u32[]{:S(2)}) async-start(bf16[4,256,256]{2,1,0:T(8,128)(2,1)} %broadcast_in_dim.3), calls=%async_computation.2 | async-start | bytes 1048576 | tf_op jit(solution)/shard_map/left_root/all_to_all | solution.py:459
  155.7 7.2 %collective-permute-start.24 = (f32[640,128]{1,0:T(8,128)S(1)}, f32[640,128]{1,0:T(8,128)S(1)}, u32[]{:S(2)}, u32[]{:S(2)}) collective-permute-start(f32[640,128]{1,0:T(8,128)S(1)} %add_add_fusion.mine_ref), channel_id=1, source_target_pairs={{0,8},{8,0},{16,24},{24,16},{1,9},{9,1},{17,25},{25,17},{2,10},{10... | collective-permute-start | bytes 983048 | tf_op jit(solution)/shard_map/finish/ppermute | solution.py:463
  157.2 6.6 %collective-permute-start.25 = (f32[640,128]{1,0:T(8,128)S(1)}, f32[640,128]{1,0:T(8,128)S(1)}, u32[]{:S(2)}, u32[]{:S(2)}) collective-permute-start(f32[640,128]{1,0:T(8,128)S(1)} %add_add_fusion.mine_ref), channel_id=1, source_target_pairs={{0,4},{4,0},{1,5},{5,1},{2,6},{6,2},{3,7},{7,3},{8,12},{12,8},{9,1... | collective-permute-start | bytes 983048 | tf_op jit(solution)/shard_map/finish/ppermute | solution.py:385
  (18 other events, 127.1 us)
